TPU v7x, 32 devices: a whole 2x2x4 slice. The times are simulated.
32 devices in a mesh: dp: 4 (over y, x), fsdp: 8 (over z, core).
Axes of the slice: x: 2, y: 2, z: 4, core: 2. Of those that a mesh axis runs over, the one named last changes fastest.
Arguments:
- byte_ids: int32 [2, 32, 1152], P(None, ('dp', 'fsdp')), may hold values from 0 to 255
- layouts: int32 [2, 32], P(None, ('dp', 'fsdp')), may hold values from 0 to 1
- weights: float32 [9728, 512], P(('dp', 'fsdp'))
- vectors: float32 [6, 512], P(None, ('dp', 'fsdp'))
- m_weights: float32 [9728, 512], P(('dp', 'fsdp')), may hold values from -0.002 to 0.002
- v_weights: float32 [9728, 512], P(('dp', 'fsdp')), may hold values from 2e-08 to 4e-07
- m_vectors: float32 [6, 512], P(None, ('dp', 'fsdp')), may hold values from -0.002 to 0.002
- v_vectors: float32 [6, 512], P(None, ('dp', 'fsdp')), may hold values from 2e-08 to 4e-07
Outputs:
- loss: float32 [], replicated
- grad_norm: float32 [], replicated
- m_weights_new: float32 [9728, 512], P(('dp', 'fsdp'))
- v_weights_new: float32 [9728, 512], P(('dp', 'fsdp'))
- weights_update: float32 [9728, 512], P(('dp', 'fsdp'))
- m_vectors_new: float32 [6, 512], P(None, ('dp', 'fsdp'))
- v_vectors_new: float32 [6, 512], P(None, ('dp', 'fsdp'))
- vectors_update: float32 [6, 512], P(None, ('dp', 'fsdp'))
All inputs are finite; a program needn't handle non-finite values.
Results may differ from a plain program's by a relative error of at most 0.0052.
The roundings to bfloat16 on the way count: a program that leaves them out, or rounds other values in their place, can miss the bound.
Values may be sent and summed in bfloat16 or wider, within the bound.
No kernel may reach another device: no remote copies, remote signals or barrier semaphores. Data moves between devices by JAX's collectives and lax.ppermute only.
A program may use at most 192 MiB of HBM per device.

v0:
```python
from functools import partial

import jax
import jax.numpy as jnp
from jax import lax
from jax.experimental import pallas as pl
from jax.experimental.pallas import tpu as pltpu
from jax.sharding import PartitionSpec as P

D = 512
HEADS = 8
HEAD = 64
FF = 2048
VOCAB = 256
POOL = 3

EPS_NORM = 1e-05
EPS_ADAM = 1e-08
CLIP = 0.2
RATE = 0.03
DECAY = 0.1
BETA = 0.5
STEP = 3
NEGATIVE = -1000000000.0

F32 = jnp.float32
BF16 = jnp.bfloat16

ROW_E = 0
ROW_P = VOCAB
ROW_QKV = ROW_P + POOL * D
ROW_O = ROW_QKV + 3 * D
ROW_F1 = ROW_O + D
ROW_F2 = ROW_F1 + FF
ROW_U = ROW_F2 + FF
ROW_H = ROW_U + POOL * D
ROW_END = ROW_H + VOCAB
ROW_HALF = ROW_END // 2
assert ROW_HALF - ROW_F1 == FF // 2

AXES = ("dp", "fsdp")
SHARD = ROW_END // 32
GATHER_CUT = 208
SCATTER_CUT = 400


def nn(left, right):
    return lax.dot_general(left, right, (((1,), (0,)), ((), ())), preferred_element_type=F32)


def nt(left, right):
    return lax.dot_general(left, right, (((1,), (1,)), ((), ())), preferred_element_type=F32)


def tn(left, right):
    return lax.dot_general(left, right, (((0,), (0,)), ((), ())), preferred_element_type=F32)


def norm_parts(values):
    center = values - jnp.mean(values, -1, keepdims=True)
    spread = jnp.mean(center * center, -1, keepdims=True)
    scale = lax.rsqrt(spread + EPS_NORM)
    return center * scale, scale


def norm_back(unit, scale, gain, grad):
    inner = grad * gain
    mean_inner = jnp.mean(inner, -1, keepdims=True)
    mean_cross = jnp.mean(inner * unit, -1, keepdims=True)
    return scale * (inner - mean_inner - unit * mean_cross)


def fold_rows(values):
    return jnp.sum(values.reshape(values.shape[0] // 8, 8, values.shape[1]), 0)


def one_hot_rows(ids):
    lanes = lax.broadcasted_iota(jnp.int32, (ids.shape[0], VOCAB), 1)
    return jnp.where(lanes == ids, 1.0, 0.0).astype(BF16)


def one_hot_cols(ids):
    lines = lax.broadcasted_iota(jnp.int32, (VOCAB, ids.shape[1]), 0)
    return jnp.where(lines == ids, 1.0, 0.0).astype(BF16)


def rows_of(index, size):
    return pl.ds(pl.multiple_of(index * size, size), size)


def gathered_parts(coords_ref):
    dp, z, core = coords_ref[0], coords_ref[1], coords_ref[2]
    for side in range(2):
        for k in range(4):
            for part in range(4):
                for kind in range(2):
                    d, e = (k, part) if kind == 0 else (part, k)
                    yield side * 8 + kind * 4 + k, part, kind, (dp ^ d) * 8 + (z ^ e) * 2 + (core ^ side)


class FetchGathered:
    def __init__(self, pieces, coords_ref, w_ref, sems, high):
        self.jobs = []
        for number, (piece, part, kind, shard) in enumerate(gathered_parts(coords_ref)):
            begin, size, step = ((0, GATHER_CUT, GATHER_CUT + 16), (GATHER_CUT, SHARD - GATHER_CUT, SHARD - GATHER_CUT))[kind]
            copy = pltpu.make_async_copy(
                pieces[piece].at[pl.ds(part * step, size)],
                w_ref.at[pl.ds(pl.multiple_of(shard * SHARD + begin, 16), size)],
                sems.at[number],
            )
            self.jobs.append((shard * SHARD < high, copy))

    def start(self, first):
        for early, copy in self.jobs:
            pl.when(early if first else jnp.logical_not(early))(copy.start)

    def wait(self, first):
        for early, copy in self.jobs:
            pl.when(early if first else jnp.logical_not(early))(copy.wait)


def fetch_rows(w_hbm, low, high, w_ref, sem):
    copy = pltpu.make_async_copy(w_hbm.at[pl.ds(low, high - low)], w_ref, sem)
    copy.start()
    return copy


def attend_kernel(short_len, slots, pieces, coords_ref, lay_ref, ids_ref, *refs):
    w_hbm, refs = refs[:pieces], refs[pieces:]
    if pieces == 1:
        vec_in_ref, refs = refs[0], refs[1:]
    if pieces > 1:
        w_out, refs = refs[0], refs[1:]
    (shifted_ref, short_ref, normed_ref, qkv_ref, lse_ref, mixed_ref, resid_ref, lines_ref, cols_ref, vec_ref,
     w_ref, dist_ref, mask_ref, part_ref, sems, part_sems) = refs
    rows = short_len * slots
    if pieces > 1:
        fetch = FetchGathered(w_hbm, coords_ref, w_ref, sems, ROW_F1)
        fetch.start(True)
    else:
        fetch = fetch_rows(w_hbm[0], 0, ROW_F1, w_ref, sems.at[0])
    copies = []
    if pieces > 1:
        for piece, part, kind, _ in gathered_parts(coords_ref):
            if kind == 0:
                place = pl.ds(part * (GATHER_CUT + 16) + GATHER_CUT, 16)
                number = len(copies)
                copies.append(
                    pltpu.make_async_copy(w_hbm[piece].at[place], part_ref.at[number], part_sems.at[number])
                )
        for copy in copies:
            copy.start()

    ids = ids_ref[...]
    group = lax.broadcasted_iota(jnp.int32, (1, rows), 1)
    starts = group == 0
    for slot in range(slots):
        starts = starts | (group == slot * short_len)
        starts = starts | ((group == slot * short_len + short_len // 2) & (lay_ref[slot] == 1))
    ends = group == rows - 1
    for slot in range(slots):
        ends = ends | (group == (slot + 1) * short_len - 1)
        ends = ends | ((group == slot * short_len + short_len // 2 - 1) & (lay_ref[slot] == 1))
    before, after = pltpu.roll(ids, 1, 1), pltpu.roll(ids, rows - 1, 1)
    own = [ids[j : j + 1] for j in range(POOL)]
    back = [jnp.where(starts, -1, before[1:2]), jnp.where(starts, -1, before[2:3]), ids[0:1]]
    ahead = [ids[1:2], ids[2:3], jnp.where(ends, -1, after[0:1])]
    for j in range(POOL):
        for kind, line in enumerate((own[j], back[j], ahead[j])):
            lines_ref[j, kind : kind + 1, :] = line
        lines_ref[j, 3:, :] = jnp.zeros((5, rows), jnp.int32)
        padded = jnp.concatenate([lines_ref[j].astype(F32), jnp.zeros((120, rows), F32)], 0)
        cols_ref[j] = padded.T.astype(jnp.int32)

    for copy in copies:
        copy.wait()
    if pieces > 1:
        both = part_ref[0].astype(F32)
        for k in range(1, len(copies)):
            both = both + part_ref[k].astype(F32)
        vec_ref[...] = both[:8]
        fetch.wait(True)
        fetch.start(False)
    else:
        vec_ref[...] = vec_in_ref[...]
        fetch.wait()
    gain, offset = vec_ref[0:1, :], vec_ref[1:2, :]

    def shift_step(j, carry):
        lanes = rows_of(j, D)
        hot = one_hot_rows(cols_ref[j, :, 1:2])
        shifted_ref[:, lanes] = nn(hot, w_ref[ROW_E:ROW_P, :]).astype(BF16)
        return carry

    lax.fori_loop(0, POOL, shift_step, 0)

    def short_step(block, carry):
        at = rows_of(block, rows // 2)
        short = nn(shifted_ref[at, :], w_ref[ROW_P:ROW_QKV, :])
        short_ref[at, :] = short
        unit, _ = norm_parts(short)
        normed_ref[at, :] = (unit * gain + offset).astype(BF16)
        qkv_ref[at, :] = nt(normed_ref[at, :], w_ref[ROW_QKV:ROW_O, :]).astype(BF16)
        return carry

    lax.fori_loop(0, 2, short_step, 0)
    if pieces > 1:
        fetch.wait(False)
        leave = pltpu.make_async_copy(w_ref, w_out, part_sems.at[len(copies)])
        leave.start()

    left_lanes = lax.broadcasted_iota(jnp.int32, (short_len, 2 * HEAD), 1) < HEAD

    def slot_step(index, carry):
        slot, lower = index // 2, index % 2
        at = rows_of(slot, short_len)

        @pl.when(lower == 0)
        def _():
            attention_bias(lay_ref[slot], short_len, dist_ref, mask_ref)

        for pair in range(HEADS // 4):
            lanes, lanes_k, lanes_v = (pair_lanes(part, lower, pair) for part in range(3))
            queries = qkv_ref[at, lanes] * jnp.asarray(0.125, BF16)
            keys, values = qkv_ref[at, lanes_k], qkv_ref[at, lanes_v]
            mixed = jnp.zeros((short_len, 2 * HEAD), F32)
            for side in range(2):
                head = lower * (HEADS // 2) + pair * 2 + side
                slope = head_slope(lower, pair * 2 + side)
                scores = nt(one_side(left_lanes, side, keys), queries)
                scores = scores + jnp.minimum(dist_ref[...] * slope, mask_ref[...])
                top = jnp.max(scores, 0, keepdims=True)
                expo = jnp.exp(scores - top)
                total = jnp.sum(expo, 0, keepdims=True)
                lse_ref[slot, head] = top + jnp.log(total)
                probs = (expo * (1.0 / total)).astype(BF16)
                mixed = mixed + tn(probs, one_side(left_lanes, side, values))
            mixed_ref[at, lanes] = mixed.astype(BF16)
        return carry

    lax.fori_loop(0, 2 * slots, slot_step, 0)
    resid_ref[...] = short_ref[...] + nn(mixed_ref[...], w_ref[ROW_O:ROW_F1, :])
    if pieces > 1:
        leave.wait()


def head_slope(lower, head):
    return jnp.where(lower == 0, *(2.0 ** (-8.0 * (head + more + 1.0) / HEADS) for more in (0, HEADS // 2)))


def pair_lanes(part, lower, pair):
    return pl.ds(pl.multiple_of(part * D + lower * (D // 2) + pair * 2 * HEAD, 2 * HEAD), 2 * HEAD)


def one_side(left_lanes, side, array):
    zero = jnp.zeros_like(array)
    return jnp.where(left_lanes, array, zero) if side == 0 else jnp.where(left_lanes, zero, array)


def attention_bias(layout, short_len, dist_ref, mask_ref):
    key = lax.broadcasted_iota(jnp.int32, (short_len, short_len), 0)
    query = lax.broadcasted_iota(jnp.int32, (short_len, short_len), 1)
    half = jnp.where(layout == 1, short_len // 2, short_len)
    allowed = (key <= query) & ((key >= half) == (query >= half))
    dist_ref[...] = (key - query).astype(F32)
    mask_ref[...] = jnp.where(allowed, 0.0, NEGATIVE)


def gelu_parts(hidden):
    size = jnp.abs(hidden)
    near = 1.0 / (1.0 + (0.3275911 * 0.7071067811865476) * size)
    bell = jnp.exp(hidden * hidden * -0.5)
    tail = near * (0.127414796 + near * (-0.142248368 + near * (0.7107068705 + near * (-0.7265760135 + near * 0.5307027145))))
    tail = tail * bell
    cdf = jnp.where(hidden >= 0.0, 1.0 - tail, tail)
    return hidden * cdf, cdf + hidden * bell * 0.3989422804014327


def split_store(keep_ref, send_ref, core, rows, values):
    half = D // 2
    low, high = values[:, :half].astype(BF16), values[:, half:].astype(BF16)
    keep_ref[rows, :] = jnp.where(core == 0, low, high)
    send_ref[rows, :] = jnp.where(core == 0, high, low)


def deep_kernel(count, coords_ref, vec_ref, cols_ref, lines_ref, resid_ref, w_hbm, *refs):
    (keep_mid, send_mid, keep_ref, send_ref, table_ref, dresid_ref, small_ref,
     w_ref, e_ref, normed_ref, act_ref, slope_ref, deep_ref, final_ref, dlog_ref, dup_ref,
     ddeep_ref, dhid_ref, sums_ref, sems) = refs
    rows = resid_ref.shape[0]
    base = ROW_F1
    core = coords_ref[2]
    stages = []
    for k, (low, high) in enumerate(((ROW_F1, ROW_F2), (ROW_F2, ROW_U), (ROW_U, ROW_END))):
        stages.append([fetch_rows(w_hbm, low, high, w_ref.at[pl.ds(low - base, high - low)], sems.at[k])])
    stages[2].append(fetch_rows(w_hbm, 0, VOCAB, e_ref, sems.at[3]))
    f1, f2, up, head = ROW_F1 - base, ROW_F2 - base, ROW_U - base, ROW_H - base
    gain2, offset2 = vec_ref[2:3, :], vec_ref[3:4, :]
    gain_f, offset_f = vec_ref[4:5, :], vec_ref[5:6, :]
    wide = 1024
    sums_ref[...] = jnp.zeros_like(sums_ref)

    unit, _ = norm_parts(resid_ref[...])
    normed_ref[...] = (unit * gain2 + offset2).astype(BF16)
    for copy in stages[0]:
        copy.wait()

    def hidden_step(chunk, carry):
        lanes = rows_of(chunk, wide)
        hidden = nt(normed_ref[...], w_ref[pl.ds(pl.multiple_of(f1 + chunk * wide, 16), wide), :])
        act, slope = gelu_parts(hidden)
        act_ref[:, lanes] = act.astype(BF16)
        slope_ref[:, lanes] = slope
        return carry

    lax.fori_loop(0, FF // wide, hidden_step, 0)
    for copy in stages[1]:
        copy.wait()

    def deep_step(block, carry):
        at = rows_of(block, rows // 2)
        deep_ref[at, :] = (resid_ref[at, :] + nn(act_ref[at, :], w_ref[f2 : f2 + FF, :])).astype(BF16)
        return carry

    lax.fori_loop(0, 2, deep_step, 0)
    for copy in stages[2]:
        copy.wait()
    ddeep_ref[...] = jnp.zeros_like(ddeep_ref)
    table_ref[...] = jnp.zeros_like(table_ref)

    def head_step(j, carry):
        there = rows_of(j, rows)
        up_rows = pl.ds(pl.multiple_of(up + j * D, 16), D)
        columns = cols_ref[j]
        joined = nn(one_hot_rows(columns[:, 0:1]), e_ref[0:VOCAB, :]) + nt(deep_ref[...], w_ref[up_rows, :])
        unit, scale = norm_parts(joined)
        final = (unit * gain_f + offset_f).astype(BF16)
        final_ref[there, :] = final
        logits = nt(final, w_ref[head : head + VOCAB, :])
        nexts = columns[:, 2:3]
        lanes = lax.broadcasted_iota(jnp.int32, logits.shape, 1)
        target = jnp.where(lanes == nexts, 1.0, 0.0)
        valid = jnp.where(nexts >= 0, 1.0, 0.0)
        peak = jnp.max(logits, -1, keepdims=True)
        expo = jnp.exp(logits - peak)
        total = jnp.sum(expo, -1, keepdims=True)
        picked = jnp.sum(logits * target, -1, keepdims=True)
        losses = valid * (peak + jnp.log(total) - picked)
        dlogits = ((valid / count) * (expo * (1.0 / total) - target)).astype(BF16)
        dlog_ref[there, :] = dlogits
        dfinal = nn(dlogits, w_ref[head : head + VOCAB, :])
        dup = norm_back(unit, scale, gain_f, dfinal).astype(BF16)
        dup_ref[there, :] = dup
        ddeep_ref[...] += nn(dup, w_ref[up_rows, :])
        sums_ref[4, :, :] += fold_rows(dfinal * unit)
        sums_ref[5, :, :] += fold_rows(dfinal)
        sums_ref[6, :, :] += jnp.broadcast_to(fold_rows(losses), (8, D))
        return carry

    lax.fori_loop(0, POOL, head_step, 0)

    out_f2, out_up, out_head = ROW_F2 - ROW_HALF, ROW_U - ROW_HALF, ROW_H - ROW_HALF
    split_store(keep_ref, send_ref, core, pl.ds(out_head, VOCAB), tn(dlog_ref[...], final_ref[...]))

    def dup_step(j, carry):
        there = rows_of(j, rows)
        dup = dup_ref[there, :]
        out = pl.ds(pl.multiple_of(out_up + j * D, D), D)
        split_store(keep_ref, send_ref, core, out, tn(dup, deep_ref[...]))
        table_ref[...] += nn(one_hot_cols(lines_ref[j, 0:1, :]), dup)
        return carry

    lax.fori_loop(0, POOL, dup_step, 0)

    deep_ref[...] = ddeep_ref[...].astype(BF16)

    def dff_step(chunk, carry):
        lanes = rows_of(chunk, wide)
        dact = nt(deep_ref[...], w_ref[pl.ds(pl.multiple_of(f2 + chunk * wide, 16), wide), :])
        dhid_ref[:, lanes] = (dact * slope_ref[:, lanes]).astype(BF16)
        grad = tn(dhid_ref[:, lanes], normed_ref[...])

        @pl.when(chunk == 0)
        def _():
            split_store(keep_mid, send_mid, core, slice(0, wide), grad)

        @pl.when(chunk > 0)
        def _():
            split_store(keep_ref, send_ref, core, slice(0, wide), grad)

        out = pl.ds(pl.multiple_of(out_f2 + chunk * wide, wide), wide)
        split_store(keep_ref, send_ref, core, out, tn(act_ref[:, lanes], deep_ref[...]))
        return carry

    lax.fori_loop(0, FF // wide, dff_step, 0)
    def dnorm_step(block, carry):
        at = rows_of(block, rows // 2)
        dnormed = nn(dhid_ref[at, :], w_ref[f1 : f1 + FF, :])
        unit, scale = norm_parts(resid_ref[at, :])
        dresid_ref[at, :] = ddeep_ref[at, :] + norm_back(unit, scale, gain2, dnormed)
        sums_ref[2, :, :] += fold_rows(dnormed * unit)
        sums_ref[3, :, :] += fold_rows(dnormed)
        return carry

    lax.fori_loop(0, 2, dnorm_step, 0)
    for k in range(8):
        small_ref[k : k + 1, :] = jnp.sum(sums_ref[k], 0, keepdims=True)


def attend_back_kernel(short_len, coords_ref, lay_ref, dresid_ref, normed_ref, qkv_ref, lse_ref, mixed_ref,
                       w_hbm, *refs):
    (keep_ref, send_ref, dqkv_ref,
     w_ref, dist_ref, mask_ref, dbranch_ref, dmix_ref, sem) = refs
    core = coords_ref[2]
    fetch = fetch_rows(w_hbm, ROW_O, ROW_F1, w_ref, sem)
    dbranch_ref[...] = dresid_ref[...].astype(BF16)
    fetch.wait()
    dmix_ref[...] = nt(dbranch_ref[...], w_ref[...]).astype(BF16)

    left_lanes = lax.broadcasted_iota(jnp.int32, (short_len, 2 * HEAD), 1) < HEAD

    def slot_step(index, carry):
        slot, lower = index // 2, index % 2
        at = rows_of(slot, short_len)

        @pl.when(lower == 0)
        def _():
            attention_bias(lay_ref[slot], short_len, dist_ref, mask_ref)

        for pair in range(HEADS // 4):
            lanes, lanes_k, lanes_v = (pair_lanes(part, lower, pair) for part in range(3))
            queries, keys, values = qkv_ref[at, lanes], qkv_ref[at, lanes_k], qkv_ref[at, lanes_v]
            dmix = dmix_ref[at, lanes]
            scaled = queries * jnp.asarray(0.125, BF16)
            dqueries, dkeys, dvalues = (jnp.zeros((short_len, 2 * HEAD), F32) for _ in range(3))
            for side in range(2):
                head = lower * (HEADS // 2) + pair * 2 + side
                slope = head_slope(lower, pair * 2 + side)
                keys_here = one_side(left_lanes, side, keys)
                scores = nt(keys_here, scaled)
                scores = scores + jnp.minimum(dist_ref[...] * slope, mask_ref[...])
                probs = jnp.exp(scores - lse_ref[slot, head])
                dprobs = nt(one_side(left_lanes, side, values), dmix)
                delta = jnp.sum(dprobs * probs, 0, keepdims=True)
                dscores = (probs * (dprobs - delta) * 0.125).astype(BF16)
                dvalues = dvalues + nn(probs.astype(BF16), one_side(left_lanes, side, dmix))
                dkeys = dkeys + nn(dscores, one_side(left_lanes, side, queries))
                dqueries = dqueries + tn(dscores, keys_here)
            dqkv_ref[at, lanes] = dqueries.astype(BF16)
            dqkv_ref[at, lanes_k] = dkeys.astype(BF16)
            dqkv_ref[at, lanes_v] = dvalues.astype(BF16)
        return carry

    lax.fori_loop(0, 2 * lse_ref.shape[0], slot_step, 0)
    split_store(keep_ref, send_ref, core, pl.ds(3 * D, D), tn(mixed_ref[...], dbranch_ref[...]))

    def dproj_step(part, carry):
        grad = tn(dqkv_ref[:, rows_of(part, D)], normed_ref[...])
        split_store(keep_ref, send_ref, core, rows_of(part, D), grad)
        return carry

    lax.fori_loop(0, 3, dproj_step, 0)


def front_back_kernel(coords_ref, vec_ref, deep_small_ref, lines_ref, dresid_ref, shifted_ref, short_ref, dqkv_ref,
                      table_in, w_hbm, keep_ref, send_ref, small_ref, table_ref, w_ref, dshort_ref, sem):
    core = coords_ref[2]
    fetch = fetch_rows(w_hbm, ROW_P, ROW_O, w_ref, sem)
    gain = vec_ref[0:1, :]
    fetch.wait()
    dnormed = nn(dqkv_ref[...], w_ref[ROW_QKV - ROW_P :, :])
    unit, scale = norm_parts(short_ref[...])
    dshort_ref[...] = (dresid_ref[...] + norm_back(unit, scale, gain, dnormed)).astype(BF16)
    small_ref[...] = deep_small_ref[...]
    for k, values in enumerate((dnormed * unit, dnormed)):
        small_ref[k : k + 1, :] = jnp.sum(fold_rows(values), 0, keepdims=True)
    half = D // 2
    for k in range(2):
        send_ref[ROW_QKV + 16 * k : ROW_QKV + 16 * (k + 1), :] = two_parts(small_ref[:, k * half : (k + 1) * half])
    table_ref[...] = table_in[...]

    def pool_step(j, carry):
        dshift = nt(dshort_ref[...], w_ref[rows_of(j, D), :]).astype(BF16)
        table_ref[...] += nn(one_hot_cols(lines_ref[j, 1:2, :]), dshift)
        out = pl.ds(pl.multiple_of(ROW_P + j * D, 16), D)
        split_store(keep_ref, send_ref, core, out, tn(shifted_ref[:, rows_of(j, D)], dshort_ref[...]))
        return carry

    lax.fori_loop(0, POOL, pool_step, 0)
    split_store(keep_ref, send_ref, core, pl.ds(ROW_E, VOCAB), table_ref[...])


def two_parts(values):
    high = values.astype(BF16)
    low = (values - high.astype(F32)).astype(BF16)
    return jnp.concatenate([high.astype(F32), low.astype(F32)], 0).astype(BF16)


def one_value(parts):
    parts = parts.astype(F32)
    return parts[:8] + parts[8:]


def lay_out(coords_ref, keep_ref, recv_ref, p_refs, q_refs):
    dp, z = coords_ref[0], coords_ref[1]
    quarter = D // 4
    line = 2 * SHARD
    rest = line - SCATTER_CUT

    def total(column, x, zed, begin, size):
        at = pl.ds(pl.multiple_of(x * (4 * line) + zed * line + begin, 16), size)
        lanes = pl.ds(pl.multiple_of(column * quarter, quarter), quarter)
        return (keep_ref[at, lanes].astype(F32) + recv_ref[at, lanes].astype(F32)).astype(BF16)

    def part_step(part, carry):
        for k in range(4):
            there = dp ^ k
            out = pl.ds(pl.multiple_of(part * SCATTER_CUT, 16), SCATTER_CUT)
            p_refs[k][out, :] = total(there // 2, there % 2, part, 0, SCATTER_CUT)
            out = pl.ds(pl.multiple_of(part * rest, 16), rest)
            q_refs[k][out, :] = total(part // 2, part % 2, z ^ k, SCATTER_CUT, rest)
        return carry

    lax.fori_loop(0, 4, part_step, 0)


def core_sum_kernel(coords_ref, keep_ref, recv_ref, *out_refs):
    lay_out(coords_ref, keep_ref, recv_ref, out_refs[:4], out_refs[4:])


def core_sum_front_kernel(coords_ref, keep_front, keep_att, keep_mid, recv_front, recv_att, recv_mid, small_ref, *refs):
    out_refs, (keep_ref, recv_ref, sems) = refs[:8], refs[8:]
    copies = [
        pltpu.make_async_copy(source, target, sems.at[k])
        for k, (source, target) in enumerate((
            (keep_att, keep_ref.at[pl.ds(ROW_QKV, ROW_F1 - ROW_QKV)]),
            (recv_att, recv_ref.at[pl.ds(ROW_QKV, ROW_F1 - ROW_QKV)]),
            (keep_mid, keep_ref.at[pl.ds(ROW_F1, ROW_HALF - ROW_F1)]),
            (recv_mid, recv_ref.at[pl.ds(ROW_F1, ROW_HALF - ROW_F1)]),
            (keep_front, keep_ref.at[pl.ds(0, ROW_QKV)]),
            (recv_front.at[pl.ds(0, ROW_QKV)], recv_ref.at[pl.ds(0, ROW_QKV)]),
            (recv_front.at[pl.ds(ROW_QKV, 32)], recv_ref.at[pl.ds(ROW_HALF, 32)]),
        ))
    ]
    for copy in copies:
        copy.start()
    for copy in copies:
        copy.wait()
    lay_out(coords_ref, keep_ref, recv_ref, out_refs[:4], out_refs[4:])
    quarter = D // 4
    for k in range(2):
        both = small_ref[:, 2 * k * quarter : 2 * (k + 1) * quarter] + one_value(
            recv_ref[ROW_HALF + 16 * k : ROW_HALF + 16 * (k + 1), :]
        )
        for side in range(2):
            parts = two_parts(both[:, side * quarter : (side + 1) * quarter])
            row = 4 * SCATTER_CUT + 16 * (2 * k + side)
            for p_ref in out_refs[:4]:
                p_ref[row : row + 16, :] = parts


def sum_of(refs, row, size):
    at = pl.ds(pl.multiple_of(row, 16), size)
    return (refs[0][at, :].astype(F32) + refs[1][at, :].astype(F32)) + (
        refs[2][at, :].astype(F32) + refs[3][at, :].astype(F32)
    )


def first_sum_kernel(coords_ref, *refs):
    sources = ((refs[0:4], refs[4:8]), (refs[8:12], refs[12:16]))
    s_refs, t_refs = refs[16:20], refs[20:24]
    dp, z = coords_ref[0], coords_ref[1]
    rest = 2 * SHARD - SCATTER_CUT
    for half, (p_refs, q_refs) in enumerate(sources):
        for k in range(4):
            s_refs[k][half * SCATTER_CUT : (half + 1) * SCATTER_CUT, :] = sum_of(
                p_refs, (z ^ k) * SCATTER_CUT, SCATTER_CUT
            ).astype(BF16)
            t_refs[k][half * rest : (half + 1) * rest, :] = sum_of(q_refs, (dp ^ k) * rest, rest).astype(BF16)
    for k in range(4):
        row = 4 * SCATTER_CUT + 16 * k
        value = sum(one_value(ref[row : row + 16, :]) for ref in sources[0][0])
        parts = two_parts(value)
        for s_ref in s_refs:
            s_ref[2 * SCATTER_CUT + 16 * k : 2 * SCATTER_CUT + 16 * (k + 1), :] = parts


def last_sum_kernel(coords_ref, *refs):
    s_refs, t_refs, out_refs, (small_ref, square_ref, sum_ref) = refs[:4], refs[4:8], refs[8:12], refs[12:]
    y, core = coords_ref[0] // 2, coords_ref[2]
    rest = 2 * SHARD - SCATTER_CUT
    squares = jnp.zeros((8, D // 4), F32)
    for k in range(2):
        half = y ^ k
        first = sum_of(s_refs, half * SCATTER_CUT, SCATTER_CUT)
        second = sum_of(t_refs, half * rest, rest)
        squares = squares + fold_rows(first * first) + fold_rows(second * second)
        sum_ref[0:SCATTER_CUT, :] = first
        sum_ref[SCATTER_CUT:, :] = second
        for other in range(2):
            out_refs[2 * other + k][...] = sum_ref[pl.ds(pl.multiple_of((core ^ other) * SHARD, 8), SHARD), :]
    for k in range(4):
        row = 2 * SCATTER_CUT + 16 * k
        small_ref[:, k * (D // 4) : (k + 1) * (D // 4)] = sum(
            one_value(ref[row : row + 16, :]) for ref in s_refs
        )
    square_ref[...] = squares


def adam(param, first_m, second_m, grad, decay):
    first_new = BETA * first_m + (1.0 - BETA) * grad
    second_new = BETA * second_m + (1.0 - BETA) * grad * grad
    correct = 1.0 - BETA**STEP
    update = -RATE * (
        first_new / correct / (jnp.sqrt(second_new / correct) + EPS_ADAM) + decay * param
    )
    return (first_new, second_new, update)


def update_kernel(count, coords_ref, g0, g1, g2, g3, q0, q1, q2, q3, small_ref, w_ref, mw_ref, vw_ref, w_vec, m_vec, v_vec,
                  loss_ref, norm_ref, mw_out, vw_out, uw_out, m_out, v_out, u_out):
    y, core, mine = coords_ref[0] // 2, coords_ref[2], coords_ref[3]
    small = small_ref[...]
    line = lax.broadcasted_iota(jnp.int32, small.shape, 0)
    gradient = jnp.where(line < 6, small, 0.0)
    squares = (q0[...] + q1[...]) + (q2[...] + q3[...])

    def whole(values):
        return jnp.sum(jnp.sum(values, 0, keepdims=True), 1, keepdims=True)

    norm = jnp.sqrt(whole(squares) + whole(gradient * gradient))
    factor = CLIP / jnp.maximum(norm, CLIP)
    norm_ref[...] = norm
    loss_ref[...] = small[6:7, 0:1] / count
    quarter = D // 4
    for k, grad_ref in enumerate((g0, g1, g2, g3)):
        place = (core ^ (k // 2)) * 2 + (y ^ (k % 2))
        lanes = pl.ds(pl.multiple_of(place * quarter, quarter), quarter)
        mw_out[:, lanes], vw_out[:, lanes], uw_out[:, lanes] = adam(
            w_ref[:, lanes], mw_ref[:, lanes], vw_ref[:, lanes], grad_ref[...] * factor, DECAY
        )
    width = w_vec.shape[1]
    owned = pltpu.roll(gradient, lax.rem(small.shape[1] - mine * width, small.shape[1]), 1)[:6, :width]
    m_out[...], v_out[...], u_out[...] = adam(w_vec[...], m_vec[...], v_vec[...], owned * factor, 0.0)


VMEM = pl.BlockSpec(memory_space=pltpu.VMEM)
SMEM = pl.BlockSpec(memory_space=pltpu.SMEM)
ANY = pl.BlockSpec(memory_space=pl.ANY)
MIB = 1024 * 1024
LIMIT = 24 * MIB
LIMIT_ATTEND = 30 * MIB
LIMIT_DEEP = 40 * MIB
LIMIT_BACK = 24 * MIB


def device_grads(pieces, vecs, coords, ids, layouts, count, paired):
    slots = layouts.shape[0]
    rows = ids.shape[1]
    short_len = rows // slots
    shape = jax.ShapeDtypeStruct
    params = pltpu.CompilerParams(vmem_limit_bytes=LIMIT)
    number = len(pieces)
    pieces = [pltpu.with_memory_space_constraint(piece, pltpu.HBM) for piece in pieces]
    jobs = 64 if number > 1 else 1
    more = [] if vecs is None else [vecs]
    half = D // 2
    passed = (
        shape((rows, POOL * D), BF16),
        shape((rows, D), F32),
        shape((rows, D), BF16),
        shape((rows, 3 * D), BF16),
        shape((slots, HEADS, 1, short_len), F32),
        shape((rows, D), BF16),
        shape((rows, D), F32),
        shape((POOL, 8, rows), jnp.int32),
        shape((POOL, rows, 128), jnp.int32),
    )

    gathered = (pltpu.HBM((ROW_END, D), BF16),) if number > 1 else ()
    *gathered, shifted, short, normed, qkv, lse, mixed, resid, lines, cols, vecs = pl.pallas_call(
        partial(attend_kernel, short_len, slots, number),
        out_shape=gathered + passed + (shape((8, D), F32),),
        in_specs=[SMEM, SMEM, VMEM] + [ANY] * number + [VMEM] * len(more),
        out_specs=(ANY,) * len(gathered) + (VMEM,) * 10,
        scratch_shapes=[
            pltpu.VMEM((ROW_END if number > 1 else ROW_F1, D), BF16),
            pltpu.VMEM((short_len, short_len), F32),
            pltpu.VMEM((short_len, short_len), F32),
            pltpu.VMEM((32, 16, D), BF16),
            pltpu.SemaphoreType.DMA((jobs,)),
            pltpu.SemaphoreType.DMA((33,)),
        ],
        compiler_params=pltpu.CompilerParams(vmem_limit_bytes=LIMIT_ATTEND),
        cost_estimate=pl.CostEstimate(flops=9_000_000_000, bytes_accessed=20_000_000, transcendentals=2_400_000),
        name="attend",
    )(coords, layouts, ids, *pieces, *more)
    stacked = pltpu.with_memory_space_constraint(gathered[0], pltpu.HBM) if number > 1 else pieces[0]
    keep_mid, send_mid, keep_deep, send_deep, table, dresid, small_deep = pl.pallas_call(
        partial(deep_kernel, count),
        out_shape=(
            shape((ROW_HALF - ROW_F1, half), BF16),
            shape((ROW_HALF - ROW_F1, half), BF16),
            shape((ROW_END - ROW_HALF, half), BF16),
            shape((ROW_END - ROW_HALF, half), BF16),
            shape((VOCAB, D), F32),
            shape((rows, D), F32),
            shape((8, D), F32),
        ),
        in_specs=[SMEM] + [VMEM] * 4 + [ANY],
        out_specs=(VMEM,) * 7,
        scratch_shapes=[
            pltpu.VMEM((ROW_END - ROW_F1, D), BF16),
            pltpu.VMEM((VOCAB, D), BF16),
            pltpu.VMEM((rows, D), BF16),
            pltpu.VMEM((rows, FF), BF16),
            pltpu.VMEM((rows, FF), F32),
            pltpu.VMEM((rows, D), BF16),
            pltpu.VMEM((POOL * rows, D), BF16),
            pltpu.VMEM((POOL * rows, VOCAB), BF16),
            pltpu.VMEM((POOL * rows, D), BF16),
            pltpu.VMEM((rows, D), F32),
            pltpu.VMEM((rows, FF), BF16),
            pltpu.VMEM((8, 8, D), F32),
            pltpu.SemaphoreType.DMA((4,)),
        ],
        compiler_params=pltpu.CompilerParams(vmem_limit_bytes=LIMIT_DEEP),
        name="deep",
    )(coords, vecs, cols, lines, resid, stacked)
    keep_att, send_att, dqkv = pl.pallas_call(
        partial(attend_back_kernel, short_len),
        out_shape=(
            shape((ROW_F1 - ROW_QKV, half), BF16),
            shape((ROW_F1 - ROW_QKV, half), BF16),
            shape((rows, 3 * D), BF16),
        ),
        in_specs=[SMEM, SMEM] + [VMEM] * 5 + [ANY],
        out_specs=(VMEM,) * 3,
        scratch_shapes=[
            pltpu.VMEM((D, D), BF16),
            pltpu.VMEM((short_len, short_len), F32),
            pltpu.VMEM((short_len, short_len), F32),
            pltpu.VMEM((rows, D), BF16),
            pltpu.VMEM((rows, D), BF16),
            pltpu.SemaphoreType.DMA,
        ],
        compiler_params=pltpu.CompilerParams(vmem_limit_bytes=LIMIT_BACK),
        cost_estimate=pl.CostEstimate(flops=11_000_000_000, bytes_accessed=20_000_000, transcendentals=2_400_000),
        name="attend_back",
    )(coords, layouts, dresid, normed, qkv, lse, mixed, stacked)
    if paired:
        recv_deep, recv_mid = swap_with(send_deep, core=1), swap_with(send_mid, core=1)
        sent = core_sum(coords, keep_deep, recv_deep)
        recv_att = swap_with(send_att, core=1)
        sent, recv_att, recv_mid, dqkv = lax.optimization_barrier((sent, recv_att, recv_mid, dqkv))
        sent = first_exchange(sent)
    keep_front, send_front, small = pl.pallas_call(
        front_back_kernel,
        out_shape=(shape((ROW_QKV, half), BF16), shape((ROW_QKV + 32, half), BF16), shape((8, D), F32)),
        in_specs=[SMEM] + [VMEM] * 8 + [ANY],
        out_specs=(VMEM,) * 3,
        scratch_shapes=[
            pltpu.VMEM((VOCAB, D), F32),
            pltpu.VMEM((ROW_O - ROW_P, D), BF16),
            pltpu.VMEM((rows, D), BF16),
            pltpu.SemaphoreType.DMA,
        ],
        compiler_params=pltpu.CompilerParams(vmem_limit_bytes=LIMIT_BACK),
        cost_estimate=pl.CostEstimate(flops=8_000_000_000, bytes_accessed=20_000_000, transcendentals=0),
        name="front_back",
    )(coords, vecs, small_deep, lines, dresid, shifted, short, dqkv, table, stacked)
    if not paired:
        front = jnp.concatenate([keep_front, send_front[:ROW_QKV]], 1)
        others = [
            jnp.concatenate(pair, 1)
            for pair in ((keep_att, send_att), (keep_mid, send_mid), (keep_deep, send_deep))
        ]
        return jnp.concatenate([front] + others, 0), small
    late = 5
    early = [array for k, array in enumerate(sent) if k != late]
    early, keep_front, send_front, small = lax.optimization_barrier((early, keep_front, send_front, small))
    sent = early[:late] + [sent[late]] + early[late:]
    received = [swap_with(send_front, core=1), recv_att, recv_mid]
    out_p, out_q = exchange_shapes(64)
    parts = pl.pallas_call(
        core_sum_front_kernel,
        out_shape=(out_p,) * 4 + (out_q,) * 4,
        in_specs=[SMEM] + [ANY] * 6 + [VMEM],
        out_specs=(VMEM,) * 8,
        scratch_shapes=[
            pltpu.VMEM((ROW_HALF, half), BF16),
            pltpu.VMEM((ROW_HALF + 32, half), BF16),
            pltpu.SemaphoreType.DMA((7,)),
        ],
        compiler_params=params,
        name="core_sum_front",
    )(coords, keep_front, keep_att, keep_mid, *received, small)
    return first_exchange(parts), sent


def exchange_shapes(extra):
    quarter = D // 4
    return (
        jax.ShapeDtypeStruct((4 * SCATTER_CUT + extra, quarter), BF16),
        jax.ShapeDtypeStruct((4 * (2 * SHARD - SCATTER_CUT), quarter), BF16),
    )


def core_sum(coords, keep, received):
    out_p, out_q = exchange_shapes(0)
    return pl.pallas_call(
        core_sum_kernel,
        out_shape=(out_p,) * 4 + (out_q,) * 4,
        in_specs=[SMEM] + [VMEM] * 2,
        out_specs=(VMEM,) * 8,
        compiler_params=pltpu.CompilerParams(vmem_limit_bytes=LIMIT),
        name="core_sum",
    )(coords, keep, received)


def first_exchange(parts):
    over = [parts[0]] + [swap_with(parts[k], line=k) for k in (1, 2, 3)]
    return over + [parts[4]] + [swap_with(parts[4 + k], zed=k) for k in (1, 2, 3)]


def swap_with(array, line=0, zed=0, core=0):
    lines, rest = lax.axis_size("dp"), lax.axis_size("fsdp")
    pairs = [
        (d * rest + f, (d ^ line) * rest + (f ^ (2 * zed + core)))
        for d in range(lines)
        for f in range(rest)
    ]
    return lax.ppermute(array, AXES, pairs)


def gather_pieces(block, vectors):
    start = lax.axis_index(AXES) * vectors.shape[1]
    own = lax.dynamic_update_slice(jnp.zeros((16, D), BF16), vectors, (0, start))
    first, second = jnp.concatenate([block[:GATHER_CUT], own], 0), block[GATHER_CUT:]
    along = jnp.concatenate([first] + [swap_with(first, zed=k) for k in (1, 2, 3)], 0)
    across = jnp.concatenate([second] + [swap_with(second, line=k) for k in (1, 2, 3)], 0)
    pieces = [along] + [swap_with(along, line=k) for k in (1, 2, 3)]
    pieces += [across] + [swap_with(across, zed=k) for k in (1, 2, 3)]
    return pieces + [swap_with(piece, core=1) for piece in pieces]


def scatter_sum(coords, front, deep):
    shape = jax.ShapeDtypeStruct
    params = pltpu.CompilerParams(vmem_limit_bytes=LIMIT)
    quarter = D // 4
    rest = 2 * SHARD - SCATTER_CUT
    parts = pl.pallas_call(
        first_sum_kernel,
        out_shape=(shape((2 * SCATTER_CUT + 64, quarter), BF16),) * 4 + (shape((2 * rest, quarter), BF16),) * 4,
        in_specs=[SMEM] + [VMEM] * 16,
        out_specs=(VMEM,) * 8,
        compiler_params=params,
        name="first_sum",
    )(coords, *front, *deep)
    second = [parts[0]] + [swap_with(parts[k], zed=k) for k in (1, 2, 3)]
    second += [parts[4]] + [swap_with(parts[4 + k], line=k) for k in (1, 2, 3)]
    *outs, small, squares = pl.pallas_call(
        last_sum_kernel,
        out_shape=(shape((SHARD, quarter), F32),) * 4 + (shape((8, D), F32), shape((8, quarter), F32)),
        in_specs=[SMEM] + [VMEM] * 8,
        out_specs=(VMEM,) * 6,
        scratch_shapes=[pltpu.VMEM((2 * SHARD, quarter), F32)],
        compiler_params=params,
        name="last_sum",
    )(coords, *second)
    squares = squares + swap_with(squares, core=1)
    quarters = [outs[0], swap_with(outs[1], line=2), swap_with(outs[2], core=1), swap_with(outs[3], line=2, core=1)]
    squares = (squares + swap_with(squares, line=1)) + (swap_with(squares, line=2) + swap_with(squares, line=3))
    squares = [squares] + [swap_with(squares, zed=k) for k in (1, 2, 3)]
    return quarters, small, squares


def shards(byte_ids, layouts, weights, vectors, m_weights, v_weights, m_vectors, v_vectors):
    devices = lax.axis_size(AXES)
    micro = byte_ids.shape[0]
    count = float(micro * layouts.shape[1] * devices * byte_ids.shape[2])
    lines, rest = lax.axis_size("dp"), lax.axis_size("fsdp")
    place = lax.axis_index("fsdp")
    coords = jnp.stack([lax.axis_index("dp"), place // 2, place % 2, lax.axis_index(AXES)]).astype(jnp.int32)
    paired = lines == 4 and rest == 8 and weights.shape[0] == SHARD
    weights_low = weights.astype(BF16)
    vectors_low = vectors.astype(BF16)
    width = vectors.shape[1]
    mine = lax.axis_index(AXES) * width
    flat_layouts = layouts.reshape(-1)
    ids = byte_ids.reshape(flat_layouts.shape[0], -1, POOL).transpose(2, 0, 1).reshape(POOL, -1)
    ids = jnp.pad(ids, ((0, 8 - POOL), (0, 0)))
    if paired:
        pieces = gather_pieces(weights_low, vectors_low)
        front, deep = device_grads(
            pieces, None, coords, ids, flat_layouts, count, True
        )
        quarters, small, squares = scatter_sum(coords, front, deep)
        like = [jax.ShapeDtypeStruct((1, 1), F32)] * 2
        like += [jax.ShapeDtypeStruct(weights.shape, F32)] * 3 + [jax.ShapeDtypeStruct(vectors.shape, F32)] * 3
        loss, grad_norm, *updated = pl.pallas_call(
            partial(update_kernel, count),
            out_shape=like,
            in_specs=[SMEM] + [VMEM] * 15,
            out_specs=[VMEM] * 8,
            compiler_params=pltpu.CompilerParams(vmem_limit_bytes=LIMIT),
            name="update",
        )(coords, *quarters, *squares, small, weights, m_weights, v_weights, vectors, m_vectors, v_vectors)
        return (loss[0, 0], grad_norm[0, 0], *updated)
    coords = coords * 0
    pieces = [lax.all_gather(weights_low, AXES, axis=0, tiled=True)]
    vecs = lax.all_gather(vectors_low, AXES, axis=1, tiled=True)
    vecs = jnp.pad(vecs.astype(F32), ((0, 2), (0, 0)))
    local, small = device_grads(pieces, vecs, coords, ids, flat_layouts, count, False)
    owned = lax.psum_scatter(local.astype(F32), AXES, scatter_dimension=0, tiled=True)
    small, squares = lax.psum((small, jnp.sum(owned * owned)), AXES)
    loss = small[6, 0] / count
    vec_grads = small[:6]
    owned_vecs = lax.dynamic_slice(vec_grads, (0, mine), (6, width))
    squares = squares + jnp.sum(vec_grads * vec_grads)
    grad_norm = jnp.sqrt(squares)
    factor = CLIP / jnp.maximum(grad_norm, CLIP)
    first_w, second_w, update_w = adam(weights, m_weights, v_weights, owned * factor, DECAY)
    first_v, second_v, update_v = adam(vectors, m_vectors, v_vectors, owned_vecs * factor, 0.0)
    return (loss, grad_norm, first_w, second_w, update_w, first_v, second_v, update_v)


def solution(mesh):
    in_specs = (
        P(None, AXES, None),
        P(None, AXES),
        P(AXES, None),
        P(None, AXES),
        P(AXES, None),
        P(AXES, None),
        P(None, AXES),
        P(None, AXES),
    )
    out_specs = (
        P(),
        P(),
        P(AXES, None),
        P(AXES, None),
        P(AXES, None),
        P(None, AXES),
        P(None, AXES),
        P(None, AXES),
    )
    return jax.shard_map(shards, mesh=mesh, in_specs=in_specs, out_specs=out_specs, check_vma=False)
```

profile of v0, /device:TPU:0, one launch (start us, length us, event | category | flops | bytes accessed | tf_op | source)
XLA Modules:
  0.0 239.6 jit_solution(8389284375316592505)
XLA Ops:
  1.8 4.0 %collective-permute-start.8 = (bf16[96,512]{1,0:T(8,128)(2,1)S(1)}, bf16[96,512]{1,0:T(8,128)(2,1)S(1)}, u32[]{:S(2)}, u32[]{:S(2)}) collective-permute-start(bf16[96,512]{1,0:T(8,128)(2,1)S(1)} %slice.9), channel_id=1, source_target_pairs={{0,24},{1,25},{2,26},{3,27},{4,28},{5,29},{6,30},{7,31},{8,16},{9,... | collective-permute-start | bytes 294920 | tf_op jit(solution)/shard_map/ppermute | solution.py:833
  7.4 4.3 %collective-permute-start.2 = (bf16[224,512]{1,0:T(8,128)(2,1)S(1)}, bf16[224,512]{1,0:T(8,128)(2,1)S(1)}, u32[]{:S(2)}, u32[]{:S(2)}) collective-permute-start(bf16[224,512]{1,0:T(8,128)(2,1)S(1)} %pad_maximum_fusion.1), channel_id=1, source_target_pairs={{0,6},{1,7},{2,4},{3,5},{4,2},{5,3},{6,0},{7,1},{8,14},{9,15},{10,... | collective-permute-start | bytes 688136 | tf_op jit(solution)/shard_map/ppermute | solution.py:833
  12.5 10.2 %collective-permute-done = bf16[224,512]{1,0:T(8,128)(2,1)S(1)} collective-permute-done((bf16[224,512]{1,0:T(8,128)(2,1)S(1)}, bf16[224,512]{1,0:T(8,128)(2,1)S(1)}, u32[]{:S(2)}, u32[]{:S(2)}) %collective-permute-start) | collective-permute-done | bytes 229408 | tf_op jit(solution)/shard_map/ppermute | solution.py:833
  22.7 7.7 %collective-permute-done.1 = bf16[224,512]{1,0:T(8,128)(2,1)S(1)} collective-permute-done((bf16[224,512]{1,0:T(8,128)(2,1)S(1)}, bf16[224,512]{1,0:T(8,128)(2,1)S(1)}, u32[]{:S(2)}, u32[]{:S(2)}) %collective-permute-start.1) | collective-permute-done | bytes 229408 | tf_op jit(solution)/shard_map/ppermute | solution.py:833
  30.5 2.5 %collective-permute-start.5 = (bf16[896,512]{1,0:T(8,128)(2,1)S(1)}, bf16[896,512]{1,0:T(8,128)(2,1)S(1)}, u32[]{:S(2)}, u32[]{:S(2)}) collective-permute-start(bf16[896,512]{1,0:T(8,128)(2,1)S(1)} %constant_dynamic-update-slice_fusion.refs_0_), channel_id=1, source_target_pairs={{0,24},{1,25},{2,26},{3,27},{4,28},{5,29},{6,30},{7,31},{8,16},{9,... | collective-permute-start | bytes 2752520 | tf_op jit(solution)/shard_map/ppermute | solution.py:833
  34.0 2.5 %collective-permute-start.11 = (bf16[384,512]{1,0:T(8,128)(2,1)S(1)}, bf16[384,512]{1,0:T(8,128)(2,1)S(1)}, u32[]{:S(2)}, u32[]{:S(2)}) collective-permute-start(bf16[384,512]{1,0:T(8,128)(2,1)S(1)} %pad_maximum_fusion.refs_4_), channel_id=1, source_target_pairs={{0,6},{1,7},{2,4},{3,5},{4,2},{5,3},{6,0},{7,1},{8,14},{9,15},{10,... | collective-permute-start | bytes 1179656 | tf_op jit(solution)/shard_map/ppermute | solution.py:833
  36.5 11.4 %collective-permute-done.11.refs_7_ = bf16[384,512]{1,0:T(8,128)(2,1)S(1)} collective-permute-done((bf16[384,512]{1,0:T(8,128)(2,1)S(1)}, bf16[384,512]{1,0:T(8,128)(2,1)S(1)}, u32[]{:S(2)}, u32[]{:S(2)}) %collective-permute-start.11) | collective-permute-done | bytes 393248 | tf_op jit(solution)/shard_map/ppermute | solution.py:833
  47.9 14.7 %collective-permute-start.9 = (bf16[384,512]{1,0:T(8,128)(2,1)S(1)}, bf16[384,512]{1,0:T(8,128)(2,1)}, u32[]{:S(2)}, u32[]{:S(2)}) collective-permute-start(bf16[384,512]{1,0:T(8,128)(2,1)S(1)} %pad_maximum_fusion.refs_4_), channel_id=1, source_target_pairs={{0,2},{1,3},{2,0},{3,1},{4,6},{5,7},{6,4},{7,5},{8,10},{9,11},{10,... | collective-permute-start | bytes 1179656 | tf_op jit(solution)/shard_map/ppermute | solution.py:833
  62.6 4.2 %collective-permute-done.10.refs_6_ = bf16[384,512]{1,0:T(8,128)(2,1)S(1)} collective-permute-done((bf16[384,512]{1,0:T(8,128)(2,1)S(1)}, bf16[384,512]{1,0:T(8,128)(2,1)S(1)}, u32[]{:S(2)}, u32[]{:S(2)}) %collective-permute-start.10) | collective-permute-done | bytes 393248 | tf_op jit(solution)/shard_map/ppermute | solution.py:833
  66.8 5.4 %collective-permute-done.9.refs_5_ = bf16[384,512]{1,0:T(8,128)(2,1)} collective-permute-done((bf16[384,512]{1,0:T(8,128)(2,1)S(1)}, bf16[384,512]{1,0:T(8,128)(2,1)}, u32[]{:S(2)}, u32[]{:S(2)}) %collective-permute-start.9) | collective-permute-done | bytes 393248 | tf_op jit(solution)/shard_map/ppermute | solution.py:833
  73.4 3.0 %collective-permute-done.18.refs_14_ = bf16[384,512]{1,0:T(8,128)(2,1)S(1)} collective-permute-done((bf16[384,512]{1,0:T(8,128)(2,1)S(1)}, bf16[384,512]{1,0:T(8,128)(2,1)S(1)}, u32[]{:S(2)}, u32[]{:S(2)}) %collective-permute-start.18) | collective-permute-done | bytes 393248 | tf_op jit(solution)/shard_map/ppermute | solution.py:833
  77.8 2.2 collective-permute-done.17.refs_13_
  80.2 16.6 %attend.1 = (bf16[9728,512]{1,0:T(8,128)(2,1)}, bf16[768,1536]{1,0:T(8,128)(2,1)S(1)}, f32[768,512]{1,0:T(8,128)S(1)}, bf16[768,512]{1,0:T(8,128)(2,1)S(1)}, bf1...) custom-call(s32[4]{0:T(128)S(1)} %pad_add_fusion.coords_ref, ...), custom_call_target="tpu_custom_call" | custom-call | flops 8999999488 | bytes 20000000 | tf_op jit(solution)/shard_map/attend/pallas_call | solution.py:681
  96.8 31.4 %deep.1 = (bf16[1024,256]{1,0:T(8,128)(2,1)S(1)}, bf16[1024,256]{1,0:T(8,128)(2,1)S(1)}, bf16[4864,256]{1,0:T(8,128)(2,1)S(1)}, bf16[4864,256]{1,0:T(8,128)(2,1)...) custom-call(s32[4]{0:T(128)S(1)} %pad_add_fusion.coords_ref, ...), custom_call_target="tpu_custom_call" | custom-call | tf_op jit(solution)/shard_map/deep/pallas_call | solution.py:699
  128.4 13.6 %attend_back.1 = (bf16[2048,256]{1,0:T(8,128)(2,1)S(1)}, bf16[2048,256]{1,0:T(8,128)(2,1)S(1)}, bf16[768,1536]{1,0:T(8,128)(2,1)S(1)}) custom-call(s32[4]{0:T(128)S(1)} %pad_add_fusion.coords_ref, s32[2]{0:T(128)S(1)} %bitcast.11, f32[768,512]{1,0:T(8,128)S(1)} %get-tuple-element.106.dresid_ref, bf16[768,512]{1,0:T(8,128)(2,1)S(1)} %get-tuple-element.107.normed_ref, ...), custom_call_target="tpu_custom_call" | custom-call | flops 11000000512 | bytes 20000000 | tf_op jit(solution)/shard_map/attend_back/pallas_call | solution.py:730
  142.6 1.4 core_sum.1
  144.0 1.5 collective-permute-done.22.recv_mid
  145.5 1.4 collective-permute-start.26
  146.8 2.0 collective-permute-start.27
  148.8 1.5 collective-permute-start.23
  150.3 1.5 collective-permute-start.24
  152.3 8.2 %front_back.1 = (bf16[1792,256]{1,0:T(8,128)(2,1)S(1)}, bf16[1824,256]{1,0:T(8,128)(2,1)S(1)}, f32[8,512]{1,0:T(8,128)S(1)}) custom-call(s32[4]{0:T(128)S(1)} %pad_add_fusion.coords_ref, f32[8,512]{1,0:T(8,128)S(1)} %get-tuple-element.91.vec_ref, f32[8,512]{1,0:T(8,128)S(1)} %get-tuple-element.121.deep_small_ref, ...), custom_call_target="tpu_custom_call" | custom-call | flops 8000000000 | bytes 20000000 | tf_op jit(solution)/shard_map/front_back/pallas_call | solution.py:757
  160.6 3.0 %collective-permute-done.26.refs_14_ = bf16[832,128]{1,0:T(8,128)(2,1)S(1)} collective-permute-done((bf16[832,128]{1,0:T(8,128)(2,1)S(1)}, bf16[832,128]{1,0:T(8,128)(2,1)S(1)}, u32[]{:S(2)}, u32[]{:S(2)}) %collective-permute-start.26) | collective-permute-done | bytes 213024 | tf_op jit(solution)/shard_map/ppermute | solution.py:833
  163.6 6.7 %collective-permute-done.24.refs_10_ = bf16[1600,128]{1,0:T(8,128)(2,1)S(1)} collective-permute-done((bf16[1600,128]{1,0:T(8,128)(2,1)S(1)}, bf16[1600,128]{1,0:T(8,128)(2,1)S(1)}, u32[]{:S(2)}, u32[]{:S(2)}) %collective-permute-start.24) | collective-permute-done | bytes 409632 | tf_op jit(solution)/shard_map/ppermute | solution.py:833
  170.8 1.9 collective-permute-done.28.recv_front
  172.8 1.9 core_sum_front.1
  175.3 1.2 collective-permute-start.29
  177.4 1.4 collective-permute-start.31
  178.8 1.5 collective-permute-start.33
  180.4 4.6 %collective-permute-done.32.refs_5_ = bf16[832,128]{1,0:T(8,128)(2,1)S(1)} collective-permute-done((bf16[832,128]{1,0:T(8,128)(2,1)S(1)}, bf16[832,128]{1,0:T(8,128)(2,1)S(1)}, u32[]{:S(2)}, u32[]{:S(2)}) %collective-permute-start.32) | collective-permute-done | bytes 213024 | tf_op jit(solution)/shard_map/ppermute | solution.py:833
  184.9 12.1 %collective-permute-done.33.refs_6_ = bf16[832,128]{1,0:T(8,128)(2,1)S(1)} collective-permute-done((bf16[832,128]{1,0:T(8,128)(2,1)S(1)}, bf16[832,128]{1,0:T(8,128)(2,1)S(1)}, u32[]{:S(2)}, u32[]{:S(2)}) %collective-permute-start.33) | collective-permute-done | bytes 213024 | tf_op jit(solution)/shard_map/ppermute | solution.py:833
  197.1 1.2 first_sum.1
  198.3 3.2 %collective-permute-start.36 = (bf16[864,128]{1,0:T(8,128)(2,1)S(1)}, bf16[864,128]{1,0:T(8,128)(2,1)S(1)}, u32[]{:S(2)}, u32[]{:S(2)}) collective-permute-start(bf16[864,128]{1,0:T(8,128)(2,1)S(1)} %get-tuple-element.153), channel_id=1, source_target_pairs={{0,2},{1,3},{2,0},{3,1},{4,6},{5,7},{6,4},{7,5},{8,10},{9,11},{10,... | collective-permute-start | bytes 663560 | tf_op jit(solution)/shard_map/ppermute | solution.py:833
  201.5 1.2 collective-permute-start.37
  202.8 1.4 collective-permute-start.38
  204.1 1.2 collective-permute-start.39
  206.2 2.6 %collective-permute-done.39.refs_5_ = bf16[416,128]{1,0:T(8,128)(2,1)S(1)} collective-permute-done((bf16[416,128]{1,0:T(8,128)(2,1)S(1)}, bf16[416,128]{1,0:T(8,128)(2,1)S(1)}, u32[]{:S(2)}, u32[]{:S(2)}) %collective-permute-start.39) | collective-permute-done | bytes 106528 | tf_op jit(solution)/shard_map/ppermute | solution.py:833
  208.8 1.5 collective-permute-start.41
  211.2 3.2 %collective-permute-done.41.refs_7_ = bf16[416,128]{1,0:T(8,128)(2,1)S(1)} collective-permute-done((bf16[416,128]{1,0:T(8,128)(2,1)S(1)}, bf16[416,128]{1,0:T(8,128)(2,1)S(1)}, u32[]{:S(2)}, u32[]{:S(2)}) %collective-permute-start.41) | collective-permute-done | bytes 106528 | tf_op jit(solution)/shard_map/ppermute | solution.py:833
  214.4 5.2 %collective-permute-done.37.refs_2_ = bf16[864,128]{1,0:T(8,128)(2,1)S(1)} collective-permute-done((bf16[864,128]{1,0:T(8,128)(2,1)S(1)}, bf16[864,128]{1,0:T(8,128)(2,1)S(1)}, u32[]{:S(2)}, u32[]{:S(2)}) %collective-permute-start.37) | collective-permute-done | bytes 221216 | tf_op jit(solution)/shard_map/ppermute | solution.py:833
  221.7 1.5 collective-permute-start.48
  223.3 1.2 collective-permute-start.47
  225.2 1.5 collective-permute-start.42
  228.1 2.0 collective-permute-start.51
  230.1 2.9 %collective-permute-start.50 = (f32[8,128]{1,0:T(8,128)S(1)}, f32[8,128]{1,0:T(8,128)S(1)}, u32[]{:S(2)}, u32[]{:S(2)}) collective-permute-start(f32[8,128]{1,0:T(8,128)S(1)} %add_add_fusion.q0), channel_id=1, source_target_pairs={{0,4},{1,5},{2,6},{3,7},{4,0},{5,1},{6,2},{7,3},{8,12},{9,13},{10,... | collective-permute-start | bytes 12296 | tf_op jit(solution)/shard_map/ppermute | solution.py:833
  233.5 1.5 collective-permute-start.49
  235.0 2.1 collective-permute-done.49.q1
  237.1 2.5 %update.1 = (f32[1,1]{1,0:T(1,128)}, f32[1,1]{1,0:T(1,128)}, f32[304,512]{1,0:T(8,128)}, f32[304,512]{1,0:T(8,128)}, f32[304,512]{1,0:T(8,128)}, /*index=5*/f32[...) custom-call(s32[4]{0:T(128)S(1)} %pad_add_fusion.coords_ref, f32[304,128]{1,0:T(8,128)S(1)} %get-tuple-element.160.g0, ...), custom_call_target="tpu_custom_call" | custom-call | tf_op jit(solution)/shard_map/update/pallas_call | solution.py:901
  (116 shorter events, 17.1 us)
Async XLA Ops:
  1.8 9.9 %collective-permute-start.8 = (bf16[96,512]{1,0:T(8,128)(2,1)S(1)}, bf16[96,512]{1,0:T(8,128)(2,1)S(1)}, u32[]{:S(2)}, u32[]{:S(2)}) collective-permute-start(bf16[96,512]{1,0:T(8,128)(2,1)S(1)} %slice.9), channel_id=1, source_target_pairs={{0,24},{1,25},{2,26},{3,27},{4,28},{5,29},{6,30},{7,31},{8,16},{9,... | collective-permute-start | bytes 294920 | tf_op jit(solution)/shard_map/ppermute | solution.py:833
  5.8 6.6 %collective-permute-start.7 = (bf16[96,512]{1,0:T(8,128)(2,1)S(1)}, bf16[96,512]{1,0:T(8,128)(2,1)S(1)}, u32[]{:S(2)}, u32[]{:S(2)}) collective-permute-start(bf16[96,512]{1,0:T(8,128)(2,1)S(1)} %slice.9), channel_id=1, source_target_pairs={{0,16},{1,17},{2,18},{3,19},{4,20},{5,21},{6,22},{7,23},{8,24},{9,... | collective-permute-start | bytes 294920 | tf_op jit(solution)/shard_map/ppermute | solution.py:833
  6.3 6.1 %collective-permute-start.6 = (bf16[96,512]{1,0:T(8,128)(2,1)S(1)}, bf16[96,512]{1,0:T(8,128)(2,1)S(1)}, u32[]{:S(2)}, u32[]{:S(2)}) collective-permute-start(bf16[96,512]{1,0:T(8,128)(2,1)S(1)} %slice.9), channel_id=1, source_target_pairs={{0,8},{1,9},{2,10},{3,11},{4,12},{5,13},{6,14},{7,15},{8,0},{9,1},... | collective-permute-start | bytes 294920 | tf_op jit(solution)/shard_map/ppermute | solution.py:833
  7.4 23.0 %collective-permute-start.2 = (bf16[224,512]{1,0:T(8,128)(2,1)S(1)}, bf16[224,512]{1,0:T(8,128)(2,1)S(1)}, u32[]{:S(2)}, u32[]{:S(2)}) collective-permute-start(bf16[224,512]{1,0:T(8,128)(2,1)S(1)} %pad_maximum_fusion.1), channel_id=1, source_target_pairs={{0,6},{1,7},{2,4},{3,5},{4,2},{5,3},{6,0},{7,1},{8,14},{9,15},{10,... | collective-permute-start | bytes 688136 | tf_op jit(solution)/shard_map/ppermute | solution.py:833
  11.7 11.0 %collective-permute-start = (bf16[224,512]{1,0:T(8,128)(2,1)S(1)}, bf16[224,512]{1,0:T(8,128)(2,1)S(1)}, u32[]{:S(2)}, u32[]{:S(2)}) collective-permute-start(bf16[224,512]{1,0:T(8,128)(2,1)S(1)} %pad_maximum_fusion.1), channel_id=1, source_target_pairs={{0,2},{1,3},{2,0},{3,1},{4,6},{5,7},{6,4},{7,5},{8,10},{9,11},{10,... | collective-permute-start | bytes 688136 | tf_op jit(solution)/shard_map/ppermute | solution.py:833
  11.7 18.6 %collective-permute-start.1 = (bf16[224,512]{1,0:T(8,128)(2,1)S(1)}, bf16[224,512]{1,0:T(8,128)(2,1)S(1)}, u32[]{:S(2)}, u32[]{:S(2)}) collective-permute-start(bf16[224,512]{1,0:T(8,128)(2,1)S(1)} %pad_maximum_fusion.1), channel_id=1, source_target_pairs={{0,4},{1,5},{2,6},{3,7},{4,0},{5,1},{6,2},{7,3},{8,12},{9,13},{10,... | collective-permute-start | bytes 688136 | tf_op jit(solution)/shard_map/ppermute | solution.py:833
  12.4 24.1 %collective-permute-start.16 = (bf16[384,512]{1,0:T(8,128)(2,1)S(1)}, bf16[384,512]{1,0:T(8,128)(2,1)S(1)}, u32[]{:S(2)}, u32[]{:S(2)}) collective-permute-start(bf16[384,512]{1,0:T(8,128)(2,1)S(1)} %pad_maximum_fusion.refs_4_), channel_id=1, source_target_pairs={{0,1},{1,0},{2,3},{3,2},{4,5},{5,4},{6,7},{7,6},{8,9},{9,8},{10,11... | collective-permute-start | bytes 1179656 | tf_op jit(solution)/shard_map/ppermute | solution.py:833
  30.5 41.8 %collective-permute-start.5 = (bf16[896,512]{1,0:T(8,128)(2,1)S(1)}, bf16[896,512]{1,0:T(8,128)(2,1)S(1)}, u32[]{:S(2)}, u32[]{:S(2)}) collective-permute-start(bf16[896,512]{1,0:T(8,128)(2,1)S(1)} %constant_dynamic-update-slice_fusion.refs_0_), channel_id=1, source_target_pairs={{0,24},{1,25},{2,26},{3,27},{4,28},{5,29},{6,30},{7,31},{8,16},{9,... | collective-permute-start | bytes 2752520 | tf_op jit(solution)/shard_map/ppermute | solution.py:833
  32.9 39.8 %collective-permute-start.4 = (bf16[896,512]{1,0:T(8,128)(2,1)S(1)}, bf16[896,512]{1,0:T(8,128)(2,1)}, u32[]{:S(2)}, u32[]{:S(2)}) collective-permute-start(bf16[896,512]{1,0:T(8,128)(2,1)S(1)} %constant_dynamic-update-slice_fusion.refs_0_), channel_id=1, source_target_pairs={{0,16},{1,17},{2,18},{3,19},{4,20},{5,21},{6,22},{7,23},{8,24},{9,... | collective-permute-start | bytes 2752520 | tf_op jit(solution)/shard_map/ppermute | solution.py:833
  33.5 39.3 %collective-permute-start.3 = (bf16[896,512]{1,0:T(8,128)(2,1)S(1)}, bf16[896,512]{1,0:T(8,128)(2,1)}, u32[]{:S(2)}, u32[]{:S(2)}) collective-permute-start(bf16[896,512]{1,0:T(8,128)(2,1)S(1)} %constant_dynamic-update-slice_fusion.refs_0_), channel_id=1, source_target_pairs={{0,8},{1,9},{2,10},{3,11},{4,12},{5,13},{6,14},{7,15},{8,0},{9,1},... | collective-permute-start | bytes 2752520 | tf_op jit(solution)/shard_map/ppermute | solution.py:833
  34.0 13.9 %collective-permute-start.11 = (bf16[384,512]{1,0:T(8,128)(2,1)S(1)}, bf16[384,512]{1,0:T(8,128)(2,1)S(1)}, u32[]{:S(2)}, u32[]{:S(2)}) collective-permute-start(bf16[384,512]{1,0:T(8,128)(2,1)S(1)} %pad_maximum_fusion.refs_4_), channel_id=1, source_target_pairs={{0,6},{1,7},{2,4},{3,5},{4,2},{5,3},{6,0},{7,1},{8,14},{9,15},{10,... | collective-permute-start | bytes 1179656 | tf_op jit(solution)/shard_map/ppermute | solution.py:833
  36.5 30.3 %collective-permute-start.10 = (bf16[384,512]{1,0:T(8,128)(2,1)S(1)}, bf16[384,512]{1,0:T(8,128)(2,1)S(1)}, u32[]{:S(2)}, u32[]{:S(2)}) collective-permute-start(bf16[384,512]{1,0:T(8,128)(2,1)S(1)} %pad_maximum_fusion.refs_4_), channel_id=1, source_target_pairs={{0,4},{1,5},{2,6},{3,7},{4,0},{5,1},{6,2},{7,3},{8,12},{9,13},{10,... | collective-permute-start | bytes 1179656 | tf_op jit(solution)/shard_map/ppermute | solution.py:833
  47.9 24.3 %collective-permute-start.9 = (bf16[384,512]{1,0:T(8,128)(2,1)S(1)}, bf16[384,512]{1,0:T(8,128)(2,1)}, u32[]{:S(2)}, u32[]{:S(2)}) collective-permute-start(bf16[384,512]{1,0:T(8,128)(2,1)S(1)} %pad_maximum_fusion.refs_4_), channel_id=1, source_target_pairs={{0,2},{1,3},{2,0},{3,1},{4,6},{5,7},{6,4},{7,5},{8,10},{9,11},{10,... | collective-permute-start | bytes 1179656 | tf_op jit(solution)/shard_map/ppermute | solution.py:833
  66.8 6.5 %collective-permute-start.19 = (bf16[384,512]{1,0:T(8,128)(2,1)S(1)}, bf16[384,512]{1,0:T(8,128)(2,1)S(1)}, u32[]{:S(2)}, u32[]{:S(2)}) collective-permute-start(bf16[384,512]{1,0:T(8,128)(2,1)S(1)} %collective-permute-done.11.refs_7_), channel_id=1, source_target_pairs={{0,1},{1,0},{2,3},{3,2},{4,5},{5,4},{6,7},{7,6},{8,9},{9,8},{10,11... | collective-permute-start | bytes 1179656 | tf_op jit(solution)/shard_map/ppermute | solution.py:833
  72.2 7.9 %collective-permute-start.12 = (bf16[896,512]{1,0:T(8,128)(2,1)S(1)}, bf16[896,512]{1,0:T(8,128)(2,1)}, u32[]{:S(2)}, u32[]{:S(2)}) collective-permute-start(bf16[896,512]{1,0:T(8,128)(2,1)S(1)} %constant_dynamic-update-slice_fusion.refs_0_), channel_id=1, source_target_pairs={{0,1},{1,0},{2,3},{3,2},{4,5},{5,4},{6,7},{7,6},{8,9},{9,8},{10,11... | collective-permute-start | bytes 2752520 | tf_op jit(solution)/shard_map/ppermute | solution.py:833
  72.2 7.9 %collective-permute-start.15 = (bf16[896,512]{1,0:T(8,128)(2,1)S(1)}, bf16[896,512]{1,0:T(8,128)(2,1)}, u32[]{:S(2)}, u32[]{:S(2)}) collective-permute-start(bf16[896,512]{1,0:T(8,128)(2,1)S(1)} %collective-permute-done.5.refs_3_), channel_id=1, source_target_pairs={{0,1},{1,0},{2,3},{3,2},{4,5},{5,4},{6,7},{7,6},{8,9},{9,8},{10,11... | collective-permute-start | bytes 2752520 | tf_op jit(solution)/shard_map/ppermute | solution.py:833
  72.7 7.4 %collective-permute-start.14 = (bf16[896,512]{1,0:T(8,128)(2,1)}, bf16[896,512]{1,0:T(8,128)(2,1)}, u32[]{:S(2)}, u32[]{:S(2)}) collective-permute-start(bf16[896,512]{1,0:T(8,128)(2,1)} %collective-permute-done.4.refs_2_), channel_id=1, source_target_pairs={{0,1},{1,0},{2,3},{3,2},{4,5},{5,4},{6,7},{7,6},{8,9},{9,8},{10,11... | collective-permute-start | bytes 2752520 | tf_op jit(solution)/shard_map/ppermute | solution.py:833
  72.8 7.3 %collective-permute-start.13 = (bf16[896,512]{1,0:T(8,128)(2,1)}, bf16[896,512]{1,0:T(8,128)(2,1)}, u32[]{:S(2)}, u32[]{:S(2)}) collective-permute-start(bf16[896,512]{1,0:T(8,128)(2,1)} %collective-permute-done.3.refs_1_), channel_id=1, source_target_pairs={{0,1},{1,0},{2,3},{3,2},{4,5},{5,4},{6,7},{7,6},{8,9},{9,8},{10,11... | collective-permute-start | bytes 2752520 | tf_op jit(solution)/shard_map/ppermute | solution.py:833
  73.2 3.1 %collective-permute-start.18 = (bf16[384,512]{1,0:T(8,128)(2,1)S(1)}, bf16[384,512]{1,0:T(8,128)(2,1)S(1)}, u32[]{:S(2)}, u32[]{:S(2)}) collective-permute-start(bf16[384,512]{1,0:T(8,128)(2,1)S(1)} %collective-permute-done.10.refs_6_), channel_id=1, source_target_pairs={{0,1},{1,0},{2,3},{3,2},{4,5},{5,4},{6,7},{7,6},{8,9},{9,8},{10,11... | collective-permute-start | bytes 1179656 | tf_op jit(solution)/shard_map/ppermute | solution.py:833
  128.2 14.4 %collective-permute-start.20 = (bf16[4864,256]{1,0:T(8,128)(2,1)S(1)}, bf16[4864,256]{1,0:T(8,128)(2,1)S(1)}, u32[]{:S(2)}, u32[]{:S(2)}) collective-permute-start(bf16[4864,256]{1,0:T(8,128)(2,1)S(1)} %get-tuple-element.97), channel_id=1, source_target_pairs={{0,1},{1,0},{2,3},{3,2},{4,5},{5,4},{6,7},{7,6},{8,9},{9,8},{10,11... | collective-permute-start | bytes 7471112 | tf_op jit(solution)/shard_map/ppermute | solution.py:833
  142.0 3.5 %collective-permute-start.21 = (bf16[2048,256]{1,0:T(8,128)(2,1)S(1)}, bf16[2048,256]{1,0:T(8,128)(2,1)S(1)}, u32[]{:S(2)}, u32[]{:S(2)}) collective-permute-start(bf16[2048,256]{1,0:T(8,128)(2,1)S(1)} %get-tuple-element.111), channel_id=1, source_target_pairs={{0,1},{1,0},{2,3},{3,2},{4,5},{5,4},{6,7},{7,6},{8,9},{9,8},{10,11... | collective-permute-start | bytes 3145736 | tf_op jit(solution)/shard_map/ppermute | solution.py:833
  145.5 18.1 %collective-permute-start.26 = (bf16[832,128]{1,0:T(8,128)(2,1)S(1)}, bf16[832,128]{1,0:T(8,128)(2,1)S(1)}, u32[]{:S(2)}, u32[]{:S(2)}) collective-permute-start(bf16[832,128]{1,0:T(8,128)(2,1)S(1)} %get-tuple-element.119), channel_id=1, source_target_pairs={{0,4},{1,5},{2,6},{3,7},{4,0},{5,1},{6,2},{7,3},{8,12},{9,13},{10,... | collective-permute-start | bytes 638984 | tf_op jit(solution)/shard_map/ppermute | solution.py:833
  146.8 16.7 %collective-permute-start.27 = (bf16[832,128]{1,0:T(8,128)(2,1)S(1)}, bf16[832,128]{1,0:T(8,128)(2,1)S(1)}, u32[]{:S(2)}, u32[]{:S(2)}) collective-permute-start(bf16[832,128]{1,0:T(8,128)(2,1)S(1)} %get-tuple-element.120), channel_id=1, source_target_pairs={{0,6},{1,7},{2,4},{3,5},{4,2},{5,3},{6,0},{7,1},{8,14},{9,15},{10,... | collective-permute-start | bytes 638984 | tf_op jit(solution)/shard_map/ppermute | solution.py:833
  148.8 14.7 %collective-permute-start.23 = (bf16[1600,128]{1,0:T(8,128)(2,1)S(1)}, bf16[1600,128]{1,0:T(8,128)(2,1)S(1)}, u32[]{:S(2)}, u32[]{:S(2)}) collective-permute-start(bf16[1600,128]{1,0:T(8,128)(2,1)S(1)} %get-tuple-element.115), channel_id=1, source_target_pairs={{0,8},{1,9},{2,10},{3,11},{4,12},{5,13},{6,14},{7,15},{8,0},{9,1},... | collective-permute-start | bytes 1228808 | tf_op jit(solution)/shard_map/ppermute | solution.py:833
  150.3 19.9 %collective-permute-start.24 = (bf16[1600,128]{1,0:T(8,128)(2,1)S(1)}, bf16[1600,128]{1,0:T(8,128)(2,1)S(1)}, u32[]{:S(2)}, u32[]{:S(2)}) collective-permute-start(bf16[1600,128]{1,0:T(8,128)(2,1)S(1)} %get-tuple-element.116), channel_id=1, source_target_pairs={{0,16},{1,17},{2,18},{3,19},{4,20},{5,21},{6,22},{7,23},{8,24},{9,... | collective-permute-start | bytes 1228808 | tf_op jit(solution)/shard_map/ppermute | solution.py:833
  151.9 18.4 %collective-permute-start.25 = (bf16[1600,128]{1,0:T(8,128)(2,1)S(1)}, bf16[1600,128]{1,0:T(8,128)(2,1)S(1)}, u32[]{:S(2)}, u32[]{:S(2)}) collective-permute-start(bf16[1600,128]{1,0:T(8,128)(2,1)S(1)} %get-tuple-element.117), channel_id=1, source_target_pairs={{0,24},{1,25},{2,26},{3,27},{4,28},{5,29},{6,30},{7,31},{8,16},{9,... | collective-permute-start | bytes 1228808 | tf_op jit(solution)/shard_map/ppermute | solution.py:833
  170.3 8.5 %collective-permute-start.35 = (bf16[832,128]{1,0:T(8,128)(2,1)S(1)}, bf16[832,128]{1,0:T(8,128)(2,1)S(1)}, u32[]{:S(2)}, u32[]{:S(2)}) collective-permute-start(bf16[832,128]{1,0:T(8,128)(2,1)S(1)} %get-tuple-element.149), channel_id=1, source_target_pairs={{0,2},{1,3},{2,0},{3,1},{4,6},{5,7},{6,4},{7,5},{8,10},{9,11},{10,... | collective-permute-start | bytes 638984 | tf_op jit(solution)/shard_map/ppermute | solution.py:833
  174.7 10.2 %collective-permute-start.32 = (bf16[832,128]{1,0:T(8,128)(2,1)S(1)}, bf16[832,128]{1,0:T(8,128)(2,1)S(1)}, u32[]{:S(2)}, u32[]{:S(2)}) collective-permute-start(bf16[832,128]{1,0:T(8,128)(2,1)S(1)} %get-tuple-element.141), channel_id=1, source_target_pairs={{0,2},{1,3},{2,0},{3,1},{4,6},{5,7},{6,4},{7,5},{8,10},{9,11},{10,... | collective-permute-start | bytes 638984 | tf_op jit(solution)/shard_map/ppermute | solution.py:833
  175.3 21.7 %collective-permute-start.29 = (bf16[1664,128]{1,0:T(8,128)(2,1)S(1)}, bf16[1664,128]{1,0:T(8,128)(2,1)S(1)}, u32[]{:S(2)}, u32[]{:S(2)}) collective-permute-start(bf16[1664,128]{1,0:T(8,128)(2,1)S(1)} %get-tuple-element.137), channel_id=1, source_target_pairs={{0,8},{1,9},{2,10},{3,11},{4,12},{5,13},{6,14},{7,15},{8,0},{9,1},... | collective-permute-start | bytes 1277960 | tf_op jit(solution)/shard_map/ppermute | solution.py:833
  176.6 20.5 %collective-permute-start.30 = (bf16[1664,128]{1,0:T(8,128)(2,1)S(1)}, bf16[1664,128]{1,0:T(8,128)(2,1)S(1)}, u32[]{:S(2)}, u32[]{:S(2)}) collective-permute-start(bf16[1664,128]{1,0:T(8,128)(2,1)S(1)} %get-tuple-element.138), channel_id=1, source_target_pairs={{0,16},{1,17},{2,18},{3,19},{4,20},{5,21},{6,22},{7,23},{8,24},{9,... | collective-permute-start | bytes 1277960 | tf_op jit(solution)/shard_map/ppermute | solution.py:833
  177.4 19.6 %collective-permute-start.31 = (bf16[1664,128]{1,0:T(8,128)(2,1)S(1)}, bf16[1664,128]{1,0:T(8,128)(2,1)S(1)}, u32[]{:S(2)}, u32[]{:S(2)}) collective-permute-start(bf16[1664,128]{1,0:T(8,128)(2,1)S(1)} %get-tuple-element.139), channel_id=1, source_target_pairs={{0,24},{1,25},{2,26},{3,27},{4,28},{5,29},{6,30},{7,31},{8,16},{9,... | collective-permute-start | bytes 1277960 | tf_op jit(solution)/shard_map/ppermute | solution.py:833
  178.8 18.2 %collective-permute-start.33 = (bf16[832,128]{1,0:T(8,128)(2,1)S(1)}, bf16[832,128]{1,0:T(8,128)(2,1)S(1)}, u32[]{:S(2)}, u32[]{:S(2)}) collective-permute-start(bf16[832,128]{1,0:T(8,128)(2,1)S(1)} %get-tuple-element.142), channel_id=1, source_target_pairs={{0,4},{1,5},{2,6},{3,7},{4,0},{5,1},{6,2},{7,3},{8,12},{9,13},{10,... | collective-permute-start | bytes 638984 | tf_op jit(solution)/shard_map/ppermute | solution.py:833
  184.9 12.1 %collective-permute-start.34 = (bf16[832,128]{1,0:T(8,128)(2,1)S(1)}, bf16[832,128]{1,0:T(8,128)(2,1)S(1)}, u32[]{:S(2)}, u32[]{:S(2)}) collective-permute-start(bf16[832,128]{1,0:T(8,128)(2,1)S(1)} %get-tuple-element.143), channel_id=1, source_target_pairs={{0,6},{1,7},{2,4},{3,5},{4,2},{5,3},{6,0},{7,1},{8,14},{9,15},{10,... | collective-permute-start | bytes 638984 | tf_op jit(solution)/shard_map/ppermute | solution.py:833
  198.3 16.1 %collective-permute-start.36 = (bf16[864,128]{1,0:T(8,128)(2,1)S(1)}, bf16[864,128]{1,0:T(8,128)(2,1)S(1)}, u32[]{:S(2)}, u32[]{:S(2)}) collective-permute-start(bf16[864,128]{1,0:T(8,128)(2,1)S(1)} %get-tuple-element.153), channel_id=1, source_target_pairs={{0,2},{1,3},{2,0},{3,1},{4,6},{5,7},{6,4},{7,5},{8,10},{9,11},{10,... | collective-permute-start | bytes 663560 | tf_op jit(solution)/shard_map/ppermute | solution.py:833
  201.5 18.1 %collective-permute-start.37 = (bf16[864,128]{1,0:T(8,128)(2,1)S(1)}, bf16[864,128]{1,0:T(8,128)(2,1)S(1)}, u32[]{:S(2)}, u32[]{:S(2)}) collective-permute-start(bf16[864,128]{1,0:T(8,128)(2,1)S(1)} %get-tuple-element.154), channel_id=1, source_target_pairs={{0,4},{1,5},{2,6},{3,7},{4,0},{5,1},{6,2},{7,3},{8,12},{9,13},{10,... | collective-permute-start | bytes 663560 | tf_op jit(solution)/shard_map/ppermute | solution.py:833
  202.8 16.9 %collective-permute-start.38 = (bf16[864,128]{1,0:T(8,128)(2,1)S(1)}, bf16[864,128]{1,0:T(8,128)(2,1)S(1)}, u32[]{:S(2)}, u32[]{:S(2)}) collective-permute-start(bf16[864,128]{1,0:T(8,128)(2,1)S(1)} %get-tuple-element.155), channel_id=1, source_target_pairs={{0,6},{1,7},{2,4},{3,5},{4,2},{5,3},{6,0},{7,1},{8,14},{9,15},{10,... | collective-permute-start | bytes 663560 | tf_op jit(solution)/shard_map/ppermute | solution.py:833
  204.1 4.7 %collective-permute-start.39 = (bf16[416,128]{1,0:T(8,128)(2,1)S(1)}, bf16[416,128]{1,0:T(8,128)(2,1)S(1)}, u32[]{:S(2)}, u32[]{:S(2)}) collective-permute-start(bf16[416,128]{1,0:T(8,128)(2,1)S(1)} %get-tuple-element.157), channel_id=1, source_target_pairs={{0,8},{1,9},{2,10},{3,11},{4,12},{5,13},{6,14},{7,15},{8,0},{9,1},... | collective-permute-start | bytes 319496 | tf_op jit(solution)/shard_map/ppermute | solution.py:833
  205.4 5.8 %collective-permute-start.40 = (bf16[416,128]{1,0:T(8,128)(2,1)S(1)}, bf16[416,128]{1,0:T(8,128)(2,1)S(1)}, u32[]{:S(2)}, u32[]{:S(2)}) collective-permute-start(bf16[416,128]{1,0:T(8,128)(2,1)S(1)} %get-tuple-element.158), channel_id=1, source_target_pairs={{0,16},{1,17},{2,18},{3,19},{4,20},{5,21},{6,22},{7,23},{8,24},{9,... | collective-permute-start | bytes 319496 | tf_op jit(solution)/shard_map/ppermute | solution.py:833
  208.8 5.6 %collective-permute-start.41 = (bf16[416,128]{1,0:T(8,128)(2,1)S(1)}, bf16[416,128]{1,0:T(8,128)(2,1)S(1)}, u32[]{:S(2)}, u32[]{:S(2)}) collective-permute-start(bf16[416,128]{1,0:T(8,128)(2,1)S(1)} %get-tuple-element.159), channel_id=1, source_target_pairs={{0,24},{1,25},{2,26},{3,27},{4,28},{5,29},{6,30},{7,31},{8,16},{9,... | collective-permute-start | bytes 319496 | tf_op jit(solution)/shard_map/ppermute | solution.py:833
  221.7 5.0 %collective-permute-start.48 = (f32[8,128]{1,0:T(8,128)S(1)}, f32[8,128]{1,0:T(8,128)S(1)}, u32[]{:S(2)}, u32[]{:S(2)}) collective-permute-start(f32[8,128]{1,0:T(8,128)S(1)} %add.29), channel_id=1, source_target_pairs={{0,24},{1,25},{2,26},{3,27},{4,28},{5,29},{6,30},{7,31},{8,16},{9,... | collective-permute-start | bytes 12296 | tf_op jit(solution)/shard_map/ppermute | solution.py:833
  223.3 4.1 %collective-permute-start.47 = (f32[8,128]{1,0:T(8,128)S(1)}, f32[8,128]{1,0:T(8,128)S(1)}, u32[]{:S(2)}, u32[]{:S(2)}) collective-permute-start(f32[8,128]{1,0:T(8,128)S(1)} %add.29), channel_id=1, source_target_pairs={{0,16},{1,17},{2,18},{3,19},{4,20},{5,21},{6,22},{7,23},{8,24},{9,... | collective-permute-start | bytes 12296 | tf_op jit(solution)/shard_map/ppermute | solution.py:833
  224.4 3.6 %collective-permute-start.46 = (f32[8,128]{1,0:T(8,128)S(1)}, f32[8,128]{1,0:T(8,128)S(1)}, u32[]{:S(2)}, u32[]{:S(2)}) collective-permute-start(f32[8,128]{1,0:T(8,128)S(1)} %add.29), channel_id=1, source_target_pairs={{0,8},{1,9},{2,10},{3,11},{4,12},{5,13},{6,14},{7,15},{8,0},{9,1},... | collective-permute-start | bytes 12296 | tf_op jit(solution)/shard_map/ppermute | solution.py:833
  225.2 11.8 %collective-permute-start.42 = (f32[304,128]{1,0:T(8,128)S(1)}, f32[304,128]{1,0:T(8,128)S(1)}, u32[]{:S(2)}, u32[]{:S(2)}) collective-permute-start(f32[304,128]{1,0:T(8,128)S(1)} %get-tuple-element.161), channel_id=1, source_target_pairs={{0,16},{1,17},{2,18},{3,19},{4,20},{5,21},{6,22},{7,23},{8,24},{9,... | collective-permute-start | bytes 466952 | tf_op jit(solution)/shard_map/ppermute | solution.py:833
  226.8 10.3 %collective-permute-start.43 = (f32[304,128]{1,0:T(8,128)S(1)}, f32[304,128]{1,0:T(8,128)S(1)}, u32[]{:S(2)}, u32[]{:S(2)}) collective-permute-start(f32[304,128]{1,0:T(8,128)S(1)} %get-tuple-element.162), channel_id=1, source_target_pairs={{0,1},{1,0},{2,3},{3,2},{4,5},{5,4},{6,7},{7,6},{8,9},{9,8},{10,11... | collective-permute-start | bytes 466952 | tf_op jit(solution)/shard_map/ppermute | solution.py:833
  226.8 10.3 %collective-permute-start.44 = (f32[304,128]{1,0:T(8,128)S(1)}, f32[304,128]{1,0:T(8,128)S(1)}, u32[]{:S(2)}, u32[]{:S(2)}) collective-permute-start(f32[304,128]{1,0:T(8,128)S(1)} %get-tuple-element.163), channel_id=1, source_target_pairs={{0,17},{1,16},{2,19},{3,18},{4,21},{5,20},{6,23},{7,22},{8,25},{9,... | collective-permute-start | bytes 466952 | tf_op jit(solution)/shard_map/ppermute | solution.py:833
  228.1 5.4 %collective-permute-start.51 = (f32[8,128]{1,0:T(8,128)S(1)}, f32[8,128]{1,0:T(8,128)S(1)}, u32[]{:S(2)}, u32[]{:S(2)}) collective-permute-start(f32[8,128]{1,0:T(8,128)S(1)} %add_add_fusion.q0), channel_id=1, source_target_pairs={{0,6},{1,7},{2,4},{3,5},{4,2},{5,3},{6,0},{7,1},{8,14},{9,15},{10,... | collective-permute-start | bytes 12296 | tf_op jit(solution)/shard_map/ppermute | solution.py:833
  230.1 4.9 %collective-permute-start.50 = (f32[8,128]{1,0:T(8,128)S(1)}, f32[8,128]{1,0:T(8,128)S(1)}, u32[]{:S(2)}, u32[]{:S(2)}) collective-permute-start(f32[8,128]{1,0:T(8,128)S(1)} %add_add_fusion.q0), channel_id=1, source_target_pairs={{0,4},{1,5},{2,6},{3,7},{4,0},{5,1},{6,2},{7,3},{8,12},{9,13},{10,... | collective-permute-start | bytes 12296 | tf_op jit(solution)/shard_map/ppermute | solution.py:833
  233.5 3.6 %collective-permute-start.49 = (f32[8,128]{1,0:T(8,128)S(1)}, f32[8,128]{1,0:T(8,128)S(1)}, u32[]{:S(2)}, u32[]{:S(2)}) collective-permute-start(f32[8,128]{1,0:T(8,128)S(1)} %add_add_fusion.q0), channel_id=1, source_target_pairs={{0,2},{1,3},{2,0},{3,1},{4,6},{5,7},{6,4},{7,5},{8,10},{9,11},{10,... | collective-permute-start | bytes 12296 | tf_op jit(solution)/shard_map/ppermute | solution.py:833
  (20 other events, 609.0 us)
where the time goes:
time: 240 us
  waiting for transfers between devices  90.2 us (38%)
  Pallas kernels  77.7 us (32%)
  starting transfers between devices  67 us (28%)
    ppermute x52, waiting for transfers between devices, swap_with(): return lax.ppermute(array, AXES, pairs)  90.2 us
    ppermute x52, starting transfers between devices, swap_with(): return lax.ppermute(array, AXES, pairs)  67 us
    pallas_call x1, Pallas kernels, device_grads(): pl.pallas_call(partial(deep_kernel, count), out_shape=(shape((ROW_HALF -...  31.4 us
    pallas_call x1, Pallas kernels, device_grads(): pl.pallas_call(partial(attend_kernel, short_len, slots, number), out_shap...  16.6 us
    pallas_call x1, Pallas kernels, device_grads(): pl.pallas_call(partial(attend_back_kernel, short_len), out_shape=(shape((...  13.6 us
    pallas_call x1, Pallas kernels, device_grads(): pl.pallas_call(front_back_kernel, out_shape=(shape((ROW_QKV, half), BF16)...  8.25 us
  transfers between devices with their start and end apart: 52, of which 21 were waited for; matrix products, arithmetic and copies ran while one was open for 1% of the time, Pallas kernels for 11%

commit v1 on v0

--- a/solution.py
+++ b/solution.py
@@ -407,15 +407,16 @@
         small_ref[k : k + 1, :] = jnp.sum(sums_ref[k], 0, keepdims=True)
 
 
-def attend_back_kernel(short_len, coords_ref, lay_ref, dresid_ref, normed_ref, qkv_ref, lse_ref, mixed_ref,
-                       w_hbm, *refs):
-    (keep_ref, send_ref, dqkv_ref,
-     w_ref, dist_ref, mask_ref, dbranch_ref, dmix_ref, sem) = refs
+def back_kernel(short_len, coords_ref, lay_ref, vec_ref, deep_small_ref, lines_ref, dresid_ref, normed_ref, qkv_ref, lse_ref,
+                mixed_ref, shifted_ref, short_ref, table_in, w_hbm, *refs):
+    (keep_ref, send_ref, small_ref,
+     table_ref, w_ref, dist_ref, mask_ref, dbranch_ref, dmix_ref, dqkv_ref, dshort_ref, sem) = refs
     core = coords_ref[2]
-    fetch = fetch_rows(w_hbm, ROW_O, ROW_F1, w_ref, sem)
+    rows = dresid_ref.shape[0]
+    fetch = fetch_rows(w_hbm, ROW_P, ROW_F1, w_ref, sem)
     dbranch_ref[...] = dresid_ref[...].astype(BF16)
     fetch.wait()
-    dmix_ref[...] = nt(dbranch_ref[...], w_ref[...]).astype(BF16)
+    dmix_ref[...] = nt(dbranch_ref[...], w_ref[ROW_O - ROW_P :, :]).astype(BF16)
 
     left_lanes = lax.broadcasted_iota(jnp.int32, (short_len, 2 * HEAD), 1) < HEAD
 
@@ -452,23 +453,17 @@
         return carry
 
     lax.fori_loop(0, 2 * lse_ref.shape[0], slot_step, 0)
-    split_store(keep_ref, send_ref, core, pl.ds(3 * D, D), tn(mixed_ref[...], dbranch_ref[...]))
+    split_store(keep_ref, send_ref, core, pl.ds(ROW_O, D), tn(mixed_ref[...], dbranch_ref[...]))
 
     def dproj_step(part, carry):
         grad = tn(dqkv_ref[:, rows_of(part, D)], normed_ref[...])
-        split_store(keep_ref, send_ref, core, rows_of(part, D), grad)
+        split_store(keep_ref, send_ref, core, pl.ds(pl.multiple_of(ROW_QKV + part * D, 16), D), grad)
         return carry
 
     lax.fori_loop(0, 3, dproj_step, 0)
 
-
-def front_back_kernel(coords_ref, vec_ref, deep_small_ref, lines_ref, dresid_ref, shifted_ref, short_ref, dqkv_ref,
-                      table_in, w_hbm, keep_ref, send_ref, small_ref, table_ref, w_ref, dshort_ref, sem):
-    core = coords_ref[2]
-    fetch = fetch_rows(w_hbm, ROW_P, ROW_O, w_ref, sem)
     gain = vec_ref[0:1, :]
-    fetch.wait()
-    dnormed = nn(dqkv_ref[...], w_ref[ROW_QKV - ROW_P :, :])
+    dnormed = nn(dqkv_ref[...], w_ref[ROW_QKV - ROW_P : ROW_O - ROW_P, :])
     unit, scale = norm_parts(short_ref[...])
     dshort_ref[...] = (dresid_ref[...] + norm_back(unit, scale, gain, dnormed)).astype(BF16)
     small_ref[...] = deep_small_ref[...]
@@ -476,7 +471,7 @@
         small_ref[k : k + 1, :] = jnp.sum(fold_rows(values), 0, keepdims=True)
     half = D // 2
     for k in range(2):
-        send_ref[ROW_QKV + 16 * k : ROW_QKV + 16 * (k + 1), :] = two_parts(small_ref[:, k * half : (k + 1) * half])
+        send_ref[ROW_F1 + 16 * k : ROW_F1 + 16 * (k + 1), :] = two_parts(small_ref[:, k * half : (k + 1) * half])
     table_ref[...] = table_in[...]
 
     def pool_step(j, carry):
@@ -528,18 +523,16 @@
     lay_out(coords_ref, keep_ref, recv_ref, out_refs[:4], out_refs[4:])
 
 
-def core_sum_front_kernel(coords_ref, keep_front, keep_att, keep_mid, recv_front, recv_att, recv_mid, small_ref, *refs):
+def core_sum_front_kernel(coords_ref, keep_front, keep_mid, recv_front, recv_mid, small_ref, *refs):
     out_refs, (keep_ref, recv_ref, sems) = refs[:8], refs[8:]
     copies = [
         pltpu.make_async_copy(source, target, sems.at[k])
         for k, (source, target) in enumerate((
-            (keep_att, keep_ref.at[pl.ds(ROW_QKV, ROW_F1 - ROW_QKV)]),
-            (recv_att, recv_ref.at[pl.ds(ROW_QKV, ROW_F1 - ROW_QKV)]),
             (keep_mid, keep_ref.at[pl.ds(ROW_F1, ROW_HALF - ROW_F1)]),
             (recv_mid, recv_ref.at[pl.ds(ROW_F1, ROW_HALF - ROW_F1)]),
-            (keep_front, keep_ref.at[pl.ds(0, ROW_QKV)]),
-            (recv_front.at[pl.ds(0, ROW_QKV)], recv_ref.at[pl.ds(0, ROW_QKV)]),
-            (recv_front.at[pl.ds(ROW_QKV, 32)], recv_ref.at[pl.ds(ROW_HALF, 32)]),
+            (keep_front, keep_ref.at[pl.ds(0, ROW_F1)]),
+            (recv_front.at[pl.ds(0, ROW_F1)], recv_ref.at[pl.ds(0, ROW_F1)]),
+            (recv_front.at[pl.ds(ROW_F1, 32)], recv_ref.at[pl.ds(ROW_HALF, 32)]),
         ))
     ]
     for copy in copies:
@@ -727,74 +720,57 @@
         compiler_params=pltpu.CompilerParams(vmem_limit_bytes=LIMIT_DEEP),
         name="deep",
     )(coords, vecs, cols, lines, resid, stacked)
-    keep_att, send_att, dqkv = pl.pallas_call(
-        partial(attend_back_kernel, short_len),
-        out_shape=(
-            shape((ROW_F1 - ROW_QKV, half), BF16),
-            shape((ROW_F1 - ROW_QKV, half), BF16),
-            shape((rows, 3 * D), BF16),
-        ),
-        in_specs=[SMEM, SMEM] + [VMEM] * 5 + [ANY],
+    if paired:
+        recv_mid, recv_deep = swap_with(send_mid, core=1), swap_with(send_deep, core=1)
+        sent = core_sum(coords, keep_deep, recv_deep)
+        sent, recv_mid, dresid = lax.optimization_barrier((sent, recv_mid, dresid))
+        sent = first_exchange(sent)
+    keep_front, send_front, small = pl.pallas_call(
+        partial(back_kernel, short_len),
+        out_shape=(shape((ROW_F1, half), BF16), shape((ROW_F1 + 32, half), BF16), shape((8, D), F32)),
+        in_specs=[SMEM, SMEM] + [VMEM] * 11 + [ANY],
         out_specs=(VMEM,) * 3,
         scratch_shapes=[
-            pltpu.VMEM((D, D), BF16),
+            pltpu.VMEM((VOCAB, D), F32),
+            pltpu.VMEM((ROW_F1 - ROW_P, D), BF16),
             pltpu.VMEM((short_len, short_len), F32),
             pltpu.VMEM((short_len, short_len), F32),
             pltpu.VMEM((rows, D), BF16),
             pltpu.VMEM((rows, D), BF16),
-            pltpu.SemaphoreType.DMA,
-        ],
-        compiler_params=pltpu.CompilerParams(vmem_limit_bytes=LIMIT_BACK),
-        cost_estimate=pl.CostEstimate(flops=11_000_000_000, bytes_accessed=20_000_000, transcendentals=2_400_000),
-        name="attend_back",
-    )(coords, layouts, dresid, normed, qkv, lse, mixed, stacked)
-    if paired:
-        recv_deep, recv_mid = swap_with(send_deep, core=1), swap_with(send_mid, core=1)
-        sent = core_sum(coords, keep_deep, recv_deep)
-        recv_att = swap_with(send_att, core=1)
-        sent, recv_att, recv_mid, dqkv = lax.optimization_barrier((sent, recv_att, recv_mid, dqkv))
-        sent = first_exchange(sent)
-    keep_front, send_front, small = pl.pallas_call(
-        front_back_kernel,
-        out_shape=(shape((ROW_QKV, half), BF16), shape((ROW_QKV + 32, half), BF16), shape((8, D), F32)),
-        in_specs=[SMEM] + [VMEM] * 8 + [ANY],
-        out_specs=(VMEM,) * 3,
-        scratch_shapes=[
-            pltpu.VMEM((VOCAB, D), F32),
-            pltpu.VMEM((ROW_O - ROW_P, D), BF16),
+            pltpu.VMEM((rows, 3 * D), BF16),
             pltpu.VMEM((rows, D), BF16),
             pltpu.SemaphoreType.DMA,
         ],
         compiler_params=pltpu.CompilerParams(vmem_limit_bytes=LIMIT_BACK),
-        cost_estimate=pl.CostEstimate(flops=8_000_000_000, bytes_accessed=20_000_000, transcendentals=0),
-        name="front_back",
-    )(coords, vecs, small_deep, lines, dresid, shifted, short, dqkv, table, stacked)
+        cost_estimate=pl.CostEstimate(flops=19_000_000_000, bytes_accessed=20_000_000, transcendentals=2_400_000),
+        name="back",
+    )(coords, layouts, vecs, small_deep, lines, dresid, normed, qkv, lse, mixed, shifted, short, table, stacked)
     if not paired:
-        front = jnp.concatenate([keep_front, send_front[:ROW_QKV]], 1)
+        front = jnp.concatenate([keep_front, send_front[:ROW_F1]], 1)
         others = [
             jnp.concatenate(pair, 1)
-            for pair in ((keep_att, send_att), (keep_mid, send_mid), (keep_deep, send_deep))
+            for pair in ((keep_mid, send_mid), (keep_deep, send_deep))
         ]
         return jnp.concatenate([front] + others, 0), small
     late = 5
     early = [array for k, array in enumerate(sent) if k != late]
     early, keep_front, send_front, small = lax.optimization_barrier((early, keep_front, send_front, small))
     sent = early[:late] + [sent[late]] + early[late:]
-    received = [swap_with(send_front, core=1), recv_att, recv_mid]
+    received = [swap_with(send_front, core=1), recv_mid]
     out_p, out_q = exchange_shapes(64)
     parts = pl.pallas_call(
         core_sum_front_kernel,
         out_shape=(out_p,) * 4 + (out_q,) * 4,
-        in_specs=[SMEM] + [ANY] * 6 + [VMEM],
+        in_specs=[SMEM] + [ANY] * 4 + [VMEM],
         out_specs=(VMEM,) * 8,
         scratch_shapes=[
             pltpu.VMEM((ROW_HALF, half), BF16),
             pltpu.VMEM((ROW_HALF + 32, half), BF16),
-            pltpu.SemaphoreType.DMA((7,)),
+            pltpu.SemaphoreType.DMA((5,)),
         ],
         compiler_params=params,
         name="core_sum_front",
-    )(coords, keep_front, keep_att, keep_mid, *received, small)
+    )(coords, keep_front, keep_mid, *received, small)
     return first_exchange(parts), sent
 
 

time: 240 us -> 234 us (0.975)
  waiting for transfers between devices: 90.2 us -> 83.1 us
  starting transfers between devices: 67 us -> 69.6 us
    ppermute x52 -> x51, waiting for transfers between devices: 90.2 us -> 83.1 us  [swap_with(): return lax.ppermute(array, AXES, pairs)]
    ppermute x52 -> x51, starting transfers between devices: 67 us -> 69.6 us  [swap_with(): return lax.ppermute(array, AXES, pairs)]
    pallas_call x2 -> x1, Pallas kernels: 21.8 us -> 20.5 us  [device_grads(): pl.pallas_call(partial(back_kernel, short_len), out_shape=(shape((ROW_F1,...]
  transfers between devices with their start and end apart: 52 -> 51, of which waited for: 21 -> 20; matrix products, arithmetic and copies ran while one was open for 1% -> 1% of each run, Pallas kernels for 11% -> 10%
where the time goes in v1:
time: 234 us; the launch traced here: 233 us
  waiting for transfers between devices  83.1 us (36%)
  Pallas kernels  76.2 us (33%)
  starting transfers between devices  69.6 us (30%)
    ppermute x51, waiting for transfers between devices, swap_with(): return lax.ppermute(array, AXES, pairs)  83.1 us
    ppermute x51, starting transfers between devices, swap_with(): return lax.ppermute(array, AXES, pairs)  69.6 us
    pallas_call x1, Pallas kernels, device_grads(): pl.pallas_call(partial(deep_kernel, count), out_shape=(shape((ROW_HALF -...  31.4 us
    pallas_call x1, Pallas kernels, device_grads(): pl.pallas_call(partial(back_kernel, short_len), out_shape=(shape((ROW_F1,...  20.5 us
    pallas_call x1, Pallas kernels, device_grads(): pl.pallas_call(partial(attend_kernel, short_len, slots, number), out_shap...  16.6 us
  transfers between devices with their start and end apart: 51, of which 20 were waited for; matrix products, arithmetic and copies ran while one was open for 1% of the time, Pallas kernels for 10%

profile of v1, /device:TPU:0, one launch (start us, length us, event | category | flops | bytes accessed | tf_op | source)
XLA Modules:
  0.0 233.5 jit_solution(16834058937698386742)
XLA Ops:
  0.6 1.1 convert_element_type.6
  1.8 4.0 %collective-permute-start.8 = (bf16[96,512]{1,0:T(8,128)(2,1)S(1)}, bf16[96,512]{1,0:T(8,128)(2,1)S(1)}, u32[]{:S(2)}, u32[]{:S(2)}) collective-permute-start(bf16[96,512]{1,0:T(8,128)(2,1)S(1)} %slice.9), channel_id=1, source_target_pairs={{0,24},{1,25},{2,26},{3,27},{4,28},{5,29},{6,30},{7,31},{8,16},{9,... | collective-permute-start | bytes 294920 | tf_op jit(solution)/shard_map/ppermute | solution.py:809
  7.4 4.3 %collective-permute-start.2 = (bf16[224,512]{1,0:T(8,128)(2,1)S(1)}, bf16[224,512]{1,0:T(8,128)(2,1)S(1)}, u32[]{:S(2)}, u32[]{:S(2)}) collective-permute-start(bf16[224,512]{1,0:T(8,128)(2,1)S(1)} %pad_maximum_fusion.1), channel_id=1, source_target_pairs={{0,6},{1,7},{2,4},{3,5},{4,2},{5,3},{6,0},{7,1},{8,14},{9,15},{10,... | collective-permute-start | bytes 688136 | tf_op jit(solution)/shard_map/ppermute | solution.py:809
  12.5 10.2 %collective-permute-done = bf16[224,512]{1,0:T(8,128)(2,1)S(1)} collective-permute-done((bf16[224,512]{1,0:T(8,128)(2,1)S(1)}, bf16[224,512]{1,0:T(8,128)(2,1)S(1)}, u32[]{:S(2)}, u32[]{:S(2)}) %collective-permute-start) | collective-permute-done | bytes 229408 | tf_op jit(solution)/shard_map/ppermute | solution.py:809
  22.7 7.7 %collective-permute-done.1 = bf16[224,512]{1,0:T(8,128)(2,1)S(1)} collective-permute-done((bf16[224,512]{1,0:T(8,128)(2,1)S(1)}, bf16[224,512]{1,0:T(8,128)(2,1)S(1)}, u32[]{:S(2)}, u32[]{:S(2)}) %collective-permute-start.1) | collective-permute-done | bytes 229408 | tf_op jit(solution)/shard_map/ppermute | solution.py:809
  30.4 2.5 %collective-permute-start.5 = (bf16[896,512]{1,0:T(8,128)(2,1)S(1)}, bf16[896,512]{1,0:T(8,128)(2,1)S(1)}, u32[]{:S(2)}, u32[]{:S(2)}) collective-permute-start(bf16[896,512]{1,0:T(8,128)(2,1)S(1)} %constant_dynamic-update-slice_fusion.refs_0_), channel_id=1, source_target_pairs={{0,24},{1,25},{2,26},{3,27},{4,28},{5,29},{6,30},{7,31},{8,16},{9,... | collective-permute-start | bytes 2752520 | tf_op jit(solution)/shard_map/ppermute | solution.py:809
  34.0 2.5 %collective-permute-start.11 = (bf16[384,512]{1,0:T(8,128)(2,1)S(1)}, bf16[384,512]{1,0:T(8,128)(2,1)S(1)}, u32[]{:S(2)}, u32[]{:S(2)}) collective-permute-start(bf16[384,512]{1,0:T(8,128)(2,1)S(1)} %pad_maximum_fusion.refs_4_), channel_id=1, source_target_pairs={{0,6},{1,7},{2,4},{3,5},{4,2},{5,3},{6,0},{7,1},{8,14},{9,15},{10,... | collective-permute-start | bytes 1179656 | tf_op jit(solution)/shard_map/ppermute | solution.py:809
  36.5 11.4 %collective-permute-done.11.refs_7_ = bf16[384,512]{1,0:T(8,128)(2,1)S(1)} collective-permute-done((bf16[384,512]{1,0:T(8,128)(2,1)S(1)}, bf16[384,512]{1,0:T(8,128)(2,1)S(1)}, u32[]{:S(2)}, u32[]{:S(2)}) %collective-permute-start.11) | collective-permute-done | bytes 393248 | tf_op jit(solution)/shard_map/ppermute | solution.py:809
  47.9 14.7 %collective-permute-start.9 = (bf16[384,512]{1,0:T(8,128)(2,1)S(1)}, bf16[384,512]{1,0:T(8,128)(2,1)}, u32[]{:S(2)}, u32[]{:S(2)}) collective-permute-start(bf16[384,512]{1,0:T(8,128)(2,1)S(1)} %pad_maximum_fusion.refs_4_), channel_id=1, source_target_pairs={{0,2},{1,3},{2,0},{3,1},{4,6},{5,7},{6,4},{7,5},{8,10},{9,11},{10,... | collective-permute-start | bytes 1179656 | tf_op jit(solution)/shard_map/ppermute | solution.py:809
  62.6 4.2 %collective-permute-done.10.refs_6_ = bf16[384,512]{1,0:T(8,128)(2,1)S(1)} collective-permute-done((bf16[384,512]{1,0:T(8,128)(2,1)S(1)}, bf16[384,512]{1,0:T(8,128)(2,1)S(1)}, u32[]{:S(2)}, u32[]{:S(2)}) %collective-permute-start.10) | collective-permute-done | bytes 393248 | tf_op jit(solution)/shard_map/ppermute | solution.py:809
  66.7 5.4 %collective-permute-done.9.refs_5_ = bf16[384,512]{1,0:T(8,128)(2,1)} collective-permute-done((bf16[384,512]{1,0:T(8,128)(2,1)S(1)}, bf16[384,512]{1,0:T(8,128)(2,1)}, u32[]{:S(2)}, u32[]{:S(2)}) %collective-permute-start.9) | collective-permute-done | bytes 393248 | tf_op jit(solution)/shard_map/ppermute | solution.py:809
  73.4 3.0 %collective-permute-done.18.refs_14_ = bf16[384,512]{1,0:T(8,128)(2,1)S(1)} collective-permute-done((bf16[384,512]{1,0:T(8,128)(2,1)S(1)}, bf16[384,512]{1,0:T(8,128)(2,1)S(1)}, u32[]{:S(2)}, u32[]{:S(2)}) %collective-permute-start.18) | collective-permute-done | bytes 393248 | tf_op jit(solution)/shard_map/ppermute | solution.py:809
  77.8 2.2 collective-permute-done.17.refs_13_
  80.1 16.6 %attend.1 = (bf16[9728,512]{1,0:T(8,128)(2,1)}, bf16[768,1536]{1,0:T(8,128)(2,1)S(1)}, f32[768,512]{1,0:T(8,128)S(1)}, bf16[768,512]{1,0:T(8,128)(2,1)S(1)}, bf1...) custom-call(s32[4]{0:T(128)S(1)} %pad_add_fusion.coords_ref, ...), custom_call_target="tpu_custom_call" | custom-call | flops 8999999488 | bytes 20000000 | tf_op jit(solution)/shard_map/attend/pallas_call | solution.py:674
  96.8 31.4 %deep.1 = (bf16[1024,256]{1,0:T(8,128)(2,1)S(1)}, bf16[1024,256]{1,0:T(8,128)(2,1)S(1)}, bf16[4864,256]{1,0:T(8,128)(2,1)S(1)}, bf16[4864,256]{1,0:T(8,128)(2,1)...) custom-call(s32[4]{0:T(128)S(1)} %pad_add_fusion.coords_ref, ...), custom_call_target="tpu_custom_call" | custom-call | tf_op jit(solution)/shard_map/deep/pallas_call | solution.py:692
  128.8 4.2 %collective-permute-done.20.recv_ref = bf16[4864,256]{1,0:T(8,128)(2,1)S(1)} collective-permute-done((bf16[4864,256]{1,0:T(8,128)(2,1)S(1)}, bf16[4864,256]{1,0:T(8,128)(2,1)S(1)}, u32[]{:S(2)}, u32[]{:S(2)}) %collective-permute-start.20) | collective-permute-done | bytes 2490400 | tf_op jit(solution)/shard_map/ppermute | solution.py:809
  133.0 1.2 core_sum.1
  134.2 1.4 collective-permute-start.25
  135.6 2.1 collective-permute-start.26
  137.7 1.5 collective-permute-start.22
  139.2 1.5 collective-permute-start.23
  141.2 20.5 %back.1 = (bf16[3840,256]{1,0:T(8,128)(2,1)S(1)}, bf16[3872,256]{1,0:T(8,128)(2,1)S(1)}, f32[8,512]{1,0:T(8,128)S(1)}) custom-call(s32[4]{0:T(128)S(1)} %pad_add_fusion.coords_ref, s32[2]{0:T(128)S(1)} %bitcast.11, f32[8,512]{1,0:T(8,128)S(1)} %get-tuple-element.87.vec_ref, f32[8,512]{1,0:T(8,128)S(1)} %get-tuple-element.111.deep_small_ref, ...), custom_call_target="tpu_custom_call" | custom-call | flops 19000000512 | bytes 20000000 | tf_op jit(solution)/shard_map/back/pallas_call | solution.py:728
  162.4 3.5 %collective-permute-done.27.recv_front = bf16[3872,256]{1,0:T(8,128)(2,1)S(1)} collective-permute-done((bf16[3872,256]{1,0:T(8,128)(2,1)S(1)}, bf16[3872,256]{1,0:T(8,128)(2,1)S(1)}, u32[]{:S(2)}, u32[]{:S(2)}) %collective-permute-start.27) | collective-permute-done | bytes 1982496 | tf_op jit(solution)/shard_map/ppermute | solution.py:809
  165.9 1.9 core_sum_front.1
  168.3 1.5 collective-permute-start.28
  169.8 1.5 collective-permute-start.29
  171.8 1.8 collective-permute-start.32
  173.6 3.7 %collective-permute-done.31.refs_5_ = bf16[832,128]{1,0:T(8,128)(2,1)S(1)} collective-permute-done((bf16[832,128]{1,0:T(8,128)(2,1)S(1)}, bf16[832,128]{1,0:T(8,128)(2,1)S(1)}, u32[]{:S(2)}, u32[]{:S(2)}) %collective-permute-start.31) | collective-permute-done | bytes 213024 | tf_op jit(solution)/shard_map/ppermute | solution.py:809
  177.3 12.4 %collective-permute-done.32.refs_6_ = bf16[832,128]{1,0:T(8,128)(2,1)S(1)} collective-permute-done((bf16[832,128]{1,0:T(8,128)(2,1)S(1)}, bf16[832,128]{1,0:T(8,128)(2,1)S(1)}, u32[]{:S(2)}, u32[]{:S(2)}) %collective-permute-start.32) | collective-permute-done | bytes 213024 | tf_op jit(solution)/shard_map/ppermute | solution.py:809
  190.3 1.2 first_sum.1
  191.5 3.0 %collective-permute-start.35 = (bf16[864,128]{1,0:T(8,128)(2,1)S(1)}, bf16[864,128]{1,0:T(8,128)(2,1)S(1)}, u32[]{:S(2)}, u32[]{:S(2)}) collective-permute-start(bf16[864,128]{1,0:T(8,128)(2,1)S(1)} %get-tuple-element.145), channel_id=1, source_target_pairs={{0,2},{1,3},{2,0},{3,1},{4,6},{5,7},{6,4},{7,5},{8,10},{9,11},{10,... | collective-permute-start | bytes 663560 | tf_op jit(solution)/shard_map/ppermute | solution.py:809
  194.5 1.4 collective-permute-start.36
  195.9 1.4 collective-permute-start.37
  197.3 1.5 collective-permute-start.38
  198.8 1.5 collective-permute-start.39
  200.3 1.7 collective-permute-done.38.refs_5_
  202.0 2.4 %collective-permute-start.40 = (bf16[416,128]{1,0:T(8,128)(2,1)S(1)}, bf16[416,128]{1,0:T(8,128)(2,1)S(1)}, u32[]{:S(2)}, u32[]{:S(2)}) collective-permute-start(bf16[416,128]{1,0:T(8,128)(2,1)S(1)} %get-tuple-element.151), channel_id=1, source_target_pairs={{0,24},{1,25},{2,26},{3,27},{4,28},{5,29},{6,30},{7,31},{8,16},{9,... | collective-permute-start | bytes 319496 | tf_op jit(solution)/shard_map/ppermute | solution.py:809
  204.5 3.2 %collective-permute-done.40.refs_7_ = bf16[416,128]{1,0:T(8,128)(2,1)S(1)} collective-permute-done((bf16[416,128]{1,0:T(8,128)(2,1)S(1)}, bf16[416,128]{1,0:T(8,128)(2,1)S(1)}, u32[]{:S(2)}, u32[]{:S(2)}) %collective-permute-start.40) | collective-permute-done | bytes 106528 | tf_op jit(solution)/shard_map/ppermute | solution.py:809
  207.6 5.6 %collective-permute-done.36.refs_2_ = bf16[864,128]{1,0:T(8,128)(2,1)S(1)} collective-permute-done((bf16[864,128]{1,0:T(8,128)(2,1)S(1)}, bf16[864,128]{1,0:T(8,128)(2,1)S(1)}, u32[]{:S(2)}, u32[]{:S(2)}) %collective-permute-start.36) | collective-permute-done | bytes 221216 | tf_op jit(solution)/shard_map/ppermute | solution.py:809
  213.2 0.9 last_sum.1
  214.2 1.2 collective-permute-done.44
  215.3 2.5 %collective-permute-start.47 = (f32[8,128]{1,0:T(8,128)S(1)}, f32[8,128]{1,0:T(8,128)S(1)}, u32[]{:S(2)}, u32[]{:S(2)}) collective-permute-start(f32[8,128]{1,0:T(8,128)S(1)} %add.29), channel_id=1, source_target_pairs={{0,24},{1,25},{2,26},{3,27},{4,28},{5,29},{6,30},{7,31},{8,16},{9,... | collective-permute-start | bytes 12296 | tf_op jit(solution)/shard_map/ppermute | solution.py:809
  218.8 1.6 collective-permute-start.41
  221.9 2.4 %collective-permute-start.50 = (f32[8,128]{1,0:T(8,128)S(1)}, f32[8,128]{1,0:T(8,128)S(1)}, u32[]{:S(2)}, u32[]{:S(2)}) collective-permute-start(f32[8,128]{1,0:T(8,128)S(1)} %add_add_fusion.q0), channel_id=1, source_target_pairs={{0,6},{1,7},{2,4},{3,5},{4,2},{5,3},{6,0},{7,1},{8,14},{9,15},{10,... | collective-permute-start | bytes 12296 | tf_op jit(solution)/shard_map/ppermute | solution.py:809
  224.3 2.8 %collective-permute-start.49 = (f32[8,128]{1,0:T(8,128)S(1)}, f32[8,128]{1,0:T(8,128)S(1)}, u32[]{:S(2)}, u32[]{:S(2)}) collective-permute-start(f32[8,128]{1,0:T(8,128)S(1)} %add_add_fusion.q0), channel_id=1, source_target_pairs={{0,4},{1,5},{2,6},{3,7},{4,0},{5,1},{6,2},{7,3},{8,12},{9,13},{10,... | collective-permute-start | bytes 12296 | tf_op jit(solution)/shard_map/ppermute | solution.py:809
  227.3 1.8 collective-permute-start.48
  229.2 1.8 collective-permute-done.48.q1
  231.0 2.5 %update.1 = (f32[1,1]{1,0:T(1,128)}, f32[1,1]{1,0:T(1,128)}, f32[304,512]{1,0:T(8,128)}, f32[304,512]{1,0:T(8,128)}, f32[304,512]{1,0:T(8,128)}, /*index=5*/f32[...) custom-call(s32[4]{0:T(128)S(1)} %pad_add_fusion.coords_ref, f32[304,128]{1,0:T(8,128)S(1)} %get-tuple-element.152.g0, ...), custom_call_target="tpu_custom_call" | custom-call | tf_op jit(solution)/shard_map/update/pallas_call | solution.py:877
  (113 shorter events, 12.3 us)
Async XLA Ops:
  1.8 9.9 %collective-permute-start.8 = (bf16[96,512]{1,0:T(8,128)(2,1)S(1)}, bf16[96,512]{1,0:T(8,128)(2,1)S(1)}, u32[]{:S(2)}, u32[]{:S(2)}) collective-permute-start(bf16[96,512]{1,0:T(8,128)(2,1)S(1)} %slice.9), channel_id=1, source_target_pairs={{0,24},{1,25},{2,26},{3,27},{4,28},{5,29},{6,30},{7,31},{8,16},{9,... | collective-permute-start | bytes 294920 | tf_op jit(solution)/shard_map/ppermute | solution.py:809
  5.7 6.6 %collective-permute-start.7 = (bf16[96,512]{1,0:T(8,128)(2,1)S(1)}, bf16[96,512]{1,0:T(8,128)(2,1)S(1)}, u32[]{:S(2)}, u32[]{:S(2)}) collective-permute-start(bf16[96,512]{1,0:T(8,128)(2,1)S(1)} %slice.9), channel_id=1, source_target_pairs={{0,16},{1,17},{2,18},{3,19},{4,20},{5,21},{6,22},{7,23},{8,24},{9,... | collective-permute-start | bytes 294920 | tf_op jit(solution)/shard_map/ppermute | solution.py:809
  6.2 6.1 %collective-permute-start.6 = (bf16[96,512]{1,0:T(8,128)(2,1)S(1)}, bf16[96,512]{1,0:T(8,128)(2,1)S(1)}, u32[]{:S(2)}, u32[]{:S(2)}) collective-permute-start(bf16[96,512]{1,0:T(8,128)(2,1)S(1)} %slice.9), channel_id=1, source_target_pairs={{0,8},{1,9},{2,10},{3,11},{4,12},{5,13},{6,14},{7,15},{8,0},{9,1},... | collective-permute-start | bytes 294920 | tf_op jit(solution)/shard_map/ppermute | solution.py:809
  7.4 23.0 %collective-permute-start.2 = (bf16[224,512]{1,0:T(8,128)(2,1)S(1)}, bf16[224,512]{1,0:T(8,128)(2,1)S(1)}, u32[]{:S(2)}, u32[]{:S(2)}) collective-permute-start(bf16[224,512]{1,0:T(8,128)(2,1)S(1)} %pad_maximum_fusion.1), channel_id=1, source_target_pairs={{0,6},{1,7},{2,4},{3,5},{4,2},{5,3},{6,0},{7,1},{8,14},{9,15},{10,... | collective-permute-start | bytes 688136 | tf_op jit(solution)/shard_map/ppermute | solution.py:809
  11.7 11.0 %collective-permute-start = (bf16[224,512]{1,0:T(8,128)(2,1)S(1)}, bf16[224,512]{1,0:T(8,128)(2,1)S(1)}, u32[]{:S(2)}, u32[]{:S(2)}) collective-permute-start(bf16[224,512]{1,0:T(8,128)(2,1)S(1)} %pad_maximum_fusion.1), channel_id=1, source_target_pairs={{0,2},{1,3},{2,0},{3,1},{4,6},{5,7},{6,4},{7,5},{8,10},{9,11},{10,... | collective-permute-start | bytes 688136 | tf_op jit(solution)/shard_map/ppermute | solution.py:809
  11.7 18.6 %collective-permute-start.1 = (bf16[224,512]{1,0:T(8,128)(2,1)S(1)}, bf16[224,512]{1,0:T(8,128)(2,1)S(1)}, u32[]{:S(2)}, u32[]{:S(2)}) collective-permute-start(bf16[224,512]{1,0:T(8,128)(2,1)S(1)} %pad_maximum_fusion.1), channel_id=1, source_target_pairs={{0,4},{1,5},{2,6},{3,7},{4,0},{5,1},{6,2},{7,3},{8,12},{9,13},{10,... | collective-permute-start | bytes 688136 | tf_op jit(solution)/shard_map/ppermute | solution.py:809
  12.4 24.1 %collective-permute-start.16 = (bf16[384,512]{1,0:T(8,128)(2,1)S(1)}, bf16[384,512]{1,0:T(8,128)(2,1)S(1)}, u32[]{:S(2)}, u32[]{:S(2)}) collective-permute-start(bf16[384,512]{1,0:T(8,128)(2,1)S(1)} %pad_maximum_fusion.refs_4_), channel_id=1, source_target_pairs={{0,1},{1,0},{2,3},{3,2},{4,5},{5,4},{6,7},{7,6},{8,9},{9,8},{10,11... | collective-permute-start | bytes 1179656 | tf_op jit(solution)/shard_map/ppermute | solution.py:809
  30.4 41.8 %collective-permute-start.5 = (bf16[896,512]{1,0:T(8,128)(2,1)S(1)}, bf16[896,512]{1,0:T(8,128)(2,1)S(1)}, u32[]{:S(2)}, u32[]{:S(2)}) collective-permute-start(bf16[896,512]{1,0:T(8,128)(2,1)S(1)} %constant_dynamic-update-slice_fusion.refs_0_), channel_id=1, source_target_pairs={{0,24},{1,25},{2,26},{3,27},{4,28},{5,29},{6,30},{7,31},{8,16},{9,... | collective-permute-start | bytes 2752520 | tf_op jit(solution)/shard_map/ppermute | solution.py:809
  32.9 39.8 %collective-permute-start.4 = (bf16[896,512]{1,0:T(8,128)(2,1)S(1)}, bf16[896,512]{1,0:T(8,128)(2,1)}, u32[]{:S(2)}, u32[]{:S(2)}) collective-permute-start(bf16[896,512]{1,0:T(8,128)(2,1)S(1)} %constant_dynamic-update-slice_fusion.refs_0_), channel_id=1, source_target_pairs={{0,16},{1,17},{2,18},{3,19},{4,20},{5,21},{6,22},{7,23},{8,24},{9,... | collective-permute-start | bytes 2752520 | tf_op jit(solution)/shard_map/ppermute | solution.py:809
  33.5 39.3 %collective-permute-start.3 = (bf16[896,512]{1,0:T(8,128)(2,1)S(1)}, bf16[896,512]{1,0:T(8,128)(2,1)}, u32[]{:S(2)}, u32[]{:S(2)}) collective-permute-start(bf16[896,512]{1,0:T(8,128)(2,1)S(1)} %constant_dynamic-update-slice_fusion.refs_0_), channel_id=1, source_target_pairs={{0,8},{1,9},{2,10},{3,11},{4,12},{5,13},{6,14},{7,15},{8,0},{9,1},... | collective-permute-start | bytes 2752520 | tf_op jit(solution)/shard_map/ppermute | solution.py:809
  34.0 13.9 %collective-permute-start.11 = (bf16[384,512]{1,0:T(8,128)(2,1)S(1)}, bf16[384,512]{1,0:T(8,128)(2,1)S(1)}, u32[]{:S(2)}, u32[]{:S(2)}) collective-permute-start(bf16[384,512]{1,0:T(8,128)(2,1)S(1)} %pad_maximum_fusion.refs_4_), channel_id=1, source_target_pairs={{0,6},{1,7},{2,4},{3,5},{4,2},{5,3},{6,0},{7,1},{8,14},{9,15},{10,... | collective-permute-start | bytes 1179656 | tf_op jit(solution)/shard_map/ppermute | solution.py:809
  36.5 30.3 %collective-permute-start.10 = (bf16[384,512]{1,0:T(8,128)(2,1)S(1)}, bf16[384,512]{1,0:T(8,128)(2,1)S(1)}, u32[]{:S(2)}, u32[]{:S(2)}) collective-permute-start(bf16[384,512]{1,0:T(8,128)(2,1)S(1)} %pad_maximum_fusion.refs_4_), channel_id=1, source_target_pairs={{0,4},{1,5},{2,6},{3,7},{4,0},{5,1},{6,2},{7,3},{8,12},{9,13},{10,... | collective-permute-start | bytes 1179656 | tf_op jit(solution)/shard_map/ppermute | solution.py:809
  47.9 24.3 %collective-permute-start.9 = (bf16[384,512]{1,0:T(8,128)(2,1)S(1)}, bf16[384,512]{1,0:T(8,128)(2,1)}, u32[]{:S(2)}, u32[]{:S(2)}) collective-permute-start(bf16[384,512]{1,0:T(8,128)(2,1)S(1)} %pad_maximum_fusion.refs_4_), channel_id=1, source_target_pairs={{0,2},{1,3},{2,0},{3,1},{4,6},{5,7},{6,4},{7,5},{8,10},{9,11},{10,... | collective-permute-start | bytes 1179656 | tf_op jit(solution)/shard_map/ppermute | solution.py:809
  66.7 6.5 %collective-permute-start.19 = (bf16[384,512]{1,0:T(8,128)(2,1)S(1)}, bf16[384,512]{1,0:T(8,128)(2,1)S(1)}, u32[]{:S(2)}, u32[]{:S(2)}) collective-permute-start(bf16[384,512]{1,0:T(8,128)(2,1)S(1)} %collective-permute-done.11.refs_7_), channel_id=1, source_target_pairs={{0,1},{1,0},{2,3},{3,2},{4,5},{5,4},{6,7},{7,6},{8,9},{9,8},{10,11... | collective-permute-start | bytes 1179656 | tf_op jit(solution)/shard_map/ppermute | solution.py:809
  72.2 7.9 %collective-permute-start.12 = (bf16[896,512]{1,0:T(8,128)(2,1)S(1)}, bf16[896,512]{1,0:T(8,128)(2,1)}, u32[]{:S(2)}, u32[]{:S(2)}) collective-permute-start(bf16[896,512]{1,0:T(8,128)(2,1)S(1)} %constant_dynamic-update-slice_fusion.refs_0_), channel_id=1, source_target_pairs={{0,1},{1,0},{2,3},{3,2},{4,5},{5,4},{6,7},{7,6},{8,9},{9,8},{10,11... | collective-permute-start | bytes 2752520 | tf_op jit(solution)/shard_map/ppermute | solution.py:809
  72.2 7.9 %collective-permute-start.15 = (bf16[896,512]{1,0:T(8,128)(2,1)S(1)}, bf16[896,512]{1,0:T(8,128)(2,1)}, u32[]{:S(2)}, u32[]{:S(2)}) collective-permute-start(bf16[896,512]{1,0:T(8,128)(2,1)S(1)} %collective-permute-done.5.refs_3_), channel_id=1, source_target_pairs={{0,1},{1,0},{2,3},{3,2},{4,5},{5,4},{6,7},{7,6},{8,9},{9,8},{10,11... | collective-permute-start | bytes 2752520 | tf_op jit(solution)/shard_map/ppermute | solution.py:809
  72.7 7.4 %collective-permute-start.14 = (bf16[896,512]{1,0:T(8,128)(2,1)}, bf16[896,512]{1,0:T(8,128)(2,1)}, u32[]{:S(2)}, u32[]{:S(2)}) collective-permute-start(bf16[896,512]{1,0:T(8,128)(2,1)} %collective-permute-done.4.refs_2_), channel_id=1, source_target_pairs={{0,1},{1,0},{2,3},{3,2},{4,5},{5,4},{6,7},{7,6},{8,9},{9,8},{10,11... | collective-permute-start | bytes 2752520 | tf_op jit(solution)/shard_map/ppermute | solution.py:809
  72.8 7.3 %collective-permute-start.13 = (bf16[896,512]{1,0:T(8,128)(2,1)}, bf16[896,512]{1,0:T(8,128)(2,1)}, u32[]{:S(2)}, u32[]{:S(2)}) collective-permute-start(bf16[896,512]{1,0:T(8,128)(2,1)} %collective-permute-done.3.refs_1_), channel_id=1, source_target_pairs={{0,1},{1,0},{2,3},{3,2},{4,5},{5,4},{6,7},{7,6},{8,9},{9,8},{10,11... | collective-permute-start | bytes 2752520 | tf_op jit(solution)/shard_map/ppermute | solution.py:809
  128.2 4.8 %collective-permute-start.20 = (bf16[4864,256]{1,0:T(8,128)(2,1)S(1)}, bf16[4864,256]{1,0:T(8,128)(2,1)S(1)}, u32[]{:S(2)}, u32[]{:S(2)}) collective-permute-start(bf16[4864,256]{1,0:T(8,128)(2,1)S(1)} %get-tuple-element.93), channel_id=1, source_target_pairs={{0,1},{1,0},{2,3},{3,2},{4,5},{5,4},{6,7},{7,6},{8,9},{9,8},{10,11... | collective-permute-start | bytes 7471112 | tf_op jit(solution)/shard_map/ppermute | solution.py:809
  128.4 5.8 %collective-permute-start.21 = (bf16[1024,256]{1,0:T(8,128)(2,1)S(1)}, bf16[1024,256]{1,0:T(8,128)(2,1)S(1)}, u32[]{:S(2)}, u32[]{:S(2)}) collective-permute-start(bf16[1024,256]{1,0:T(8,128)(2,1)S(1)} %get-tuple-element.102), channel_id=1, source_target_pairs={{0,1},{1,0},{2,3},{3,2},{4,5},{5,4},{6,7},{7,6},{8,9},{9,8},{10,11... | collective-permute-start | bytes 1572872 | tf_op jit(solution)/shard_map/ppermute | solution.py:809
  134.2 27.5 %collective-permute-start.25 = (bf16[832,128]{1,0:T(8,128)(2,1)S(1)}, bf16[832,128]{1,0:T(8,128)(2,1)S(1)}, u32[]{:S(2)}, u32[]{:S(2)}) collective-permute-start(bf16[832,128]{1,0:T(8,128)(2,1)S(1)} %get-tuple-element.109), channel_id=1, source_target_pairs={{0,4},{1,5},{2,6},{3,7},{4,0},{5,1},{6,2},{7,3},{8,12},{9,13},{10,... | collective-permute-start | bytes 638984 | tf_op jit(solution)/shard_map/ppermute | solution.py:809
  135.6 26.1 %collective-permute-start.26 = (bf16[832,128]{1,0:T(8,128)(2,1)S(1)}, bf16[832,128]{1,0:T(8,128)(2,1)S(1)}, u32[]{:S(2)}, u32[]{:S(2)}) collective-permute-start(bf16[832,128]{1,0:T(8,128)(2,1)S(1)} %get-tuple-element.110), channel_id=1, source_target_pairs={{0,6},{1,7},{2,4},{3,5},{4,2},{5,3},{6,0},{7,1},{8,14},{9,15},{10,... | collective-permute-start | bytes 638984 | tf_op jit(solution)/shard_map/ppermute | solution.py:809
  137.7 24.0 %collective-permute-start.22 = (bf16[1600,128]{1,0:T(8,128)(2,1)S(1)}, bf16[1600,128]{1,0:T(8,128)(2,1)S(1)}, u32[]{:S(2)}, u32[]{:S(2)}) collective-permute-start(bf16[1600,128]{1,0:T(8,128)(2,1)S(1)} %get-tuple-element.105), channel_id=1, source_target_pairs={{0,8},{1,9},{2,10},{3,11},{4,12},{5,13},{6,14},{7,15},{8,0},{9,1},... | collective-permute-start | bytes 1228808 | tf_op jit(solution)/shard_map/ppermute | solution.py:809
  139.2 22.5 %collective-permute-start.23 = (bf16[1600,128]{1,0:T(8,128)(2,1)S(1)}, bf16[1600,128]{1,0:T(8,128)(2,1)S(1)}, u32[]{:S(2)}, u32[]{:S(2)}) collective-permute-start(bf16[1600,128]{1,0:T(8,128)(2,1)S(1)} %get-tuple-element.106), channel_id=1, source_target_pairs={{0,16},{1,17},{2,18},{3,19},{4,20},{5,21},{6,22},{7,23},{8,24},{9,... | collective-permute-start | bytes 1228808 | tf_op jit(solution)/shard_map/ppermute | solution.py:809
  140.7 21.0 %collective-permute-start.24 = (bf16[1600,128]{1,0:T(8,128)(2,1)S(1)}, bf16[1600,128]{1,0:T(8,128)(2,1)S(1)}, u32[]{:S(2)}, u32[]{:S(2)}) collective-permute-start(bf16[1600,128]{1,0:T(8,128)(2,1)S(1)} %get-tuple-element.107), channel_id=1, source_target_pairs={{0,24},{1,25},{2,26},{3,27},{4,28},{5,29},{6,30},{7,31},{8,16},{9,... | collective-permute-start | bytes 1228808 | tf_op jit(solution)/shard_map/ppermute | solution.py:809
  161.8 4.1 %collective-permute-start.27 = (bf16[3872,256]{1,0:T(8,128)(2,1)S(1)}, bf16[3872,256]{1,0:T(8,128)(2,1)S(1)}, u32[]{:S(2)}, u32[]{:S(2)}) collective-permute-start(bf16[3872,256]{1,0:T(8,128)(2,1)S(1)} %get-tuple-element.125), channel_id=1, source_target_pairs={{0,1},{1,0},{2,3},{3,2},{4,5},{5,4},{6,7},{7,6},{8,9},{9,8},{10,11... | collective-permute-start | bytes 5947400 | tf_op jit(solution)/shard_map/ppermute | solution.py:809
  161.9 9.9 %collective-permute-start.34 = (bf16[832,128]{1,0:T(8,128)(2,1)S(1)}, bf16[832,128]{1,0:T(8,128)(2,1)S(1)}, u32[]{:S(2)}, u32[]{:S(2)}) collective-permute-start(bf16[832,128]{1,0:T(8,128)(2,1)S(1)} %get-tuple-element.141), channel_id=1, source_target_pairs={{0,2},{1,3},{2,0},{3,1},{4,6},{5,7},{6,4},{7,5},{8,10},{9,11},{10,... | collective-permute-start | bytes 638984 | tf_op jit(solution)/shard_map/ppermute | solution.py:809
  167.8 9.5 %collective-permute-start.31 = (bf16[832,128]{1,0:T(8,128)(2,1)S(1)}, bf16[832,128]{1,0:T(8,128)(2,1)S(1)}, u32[]{:S(2)}, u32[]{:S(2)}) collective-permute-start(bf16[832,128]{1,0:T(8,128)(2,1)S(1)} %get-tuple-element.133), channel_id=1, source_target_pairs={{0,2},{1,3},{2,0},{3,1},{4,6},{5,7},{6,4},{7,5},{8,10},{9,11},{10,... | collective-permute-start | bytes 638984 | tf_op jit(solution)/shard_map/ppermute | solution.py:809
  168.3 21.4 %collective-permute-start.28 = (bf16[1664,128]{1,0:T(8,128)(2,1)S(1)}, bf16[1664,128]{1,0:T(8,128)(2,1)S(1)}, u32[]{:S(2)}, u32[]{:S(2)}) collective-permute-start(bf16[1664,128]{1,0:T(8,128)(2,1)S(1)} %get-tuple-element.129), channel_id=1, source_target_pairs={{0,8},{1,9},{2,10},{3,11},{4,12},{5,13},{6,14},{7,15},{8,0},{9,1},... | collective-permute-start | bytes 1277960 | tf_op jit(solution)/shard_map/ppermute | solution.py:809
  169.8 20.4 %collective-permute-start.29 = (bf16[1664,128]{1,0:T(8,128)(2,1)S(1)}, bf16[1664,128]{1,0:T(8,128)(2,1)S(1)}, u32[]{:S(2)}, u32[]{:S(2)}) collective-permute-start(bf16[1664,128]{1,0:T(8,128)(2,1)S(1)} %get-tuple-element.130), channel_id=1, source_target_pairs={{0,16},{1,17},{2,18},{3,19},{4,20},{5,21},{6,22},{7,23},{8,24},{9,... | collective-permute-start | bytes 1277960 | tf_op jit(solution)/shard_map/ppermute | solution.py:809
  171.3 18.9 %collective-permute-start.30 = (bf16[1664,128]{1,0:T(8,128)(2,1)S(1)}, bf16[1664,128]{1,0:T(8,128)(2,1)S(1)}, u32[]{:S(2)}, u32[]{:S(2)}) collective-permute-start(bf16[1664,128]{1,0:T(8,128)(2,1)S(1)} %get-tuple-element.131), channel_id=1, source_target_pairs={{0,24},{1,25},{2,26},{3,27},{4,28},{5,29},{6,30},{7,31},{8,16},{9,... | collective-permute-start | bytes 1277960 | tf_op jit(solution)/shard_map/ppermute | solution.py:809
  171.8 17.9 %collective-permute-start.32 = (bf16[832,128]{1,0:T(8,128)(2,1)S(1)}, bf16[832,128]{1,0:T(8,128)(2,1)S(1)}, u32[]{:S(2)}, u32[]{:S(2)}) collective-permute-start(bf16[832,128]{1,0:T(8,128)(2,1)S(1)} %get-tuple-element.134), channel_id=1, source_target_pairs={{0,4},{1,5},{2,6},{3,7},{4,0},{5,1},{6,2},{7,3},{8,12},{9,13},{10,... | collective-permute-start | bytes 638984 | tf_op jit(solution)/shard_map/ppermute | solution.py:809
  177.3 12.4 %collective-permute-start.33 = (bf16[832,128]{1,0:T(8,128)(2,1)S(1)}, bf16[832,128]{1,0:T(8,128)(2,1)S(1)}, u32[]{:S(2)}, u32[]{:S(2)}) collective-permute-start(bf16[832,128]{1,0:T(8,128)(2,1)S(1)} %get-tuple-element.135), channel_id=1, source_target_pairs={{0,6},{1,7},{2,4},{3,5},{4,2},{5,3},{6,0},{7,1},{8,14},{9,15},{10,... | collective-permute-start | bytes 638984 | tf_op jit(solution)/shard_map/ppermute | solution.py:809
  191.5 16.2 %collective-permute-start.35 = (bf16[864,128]{1,0:T(8,128)(2,1)S(1)}, bf16[864,128]{1,0:T(8,128)(2,1)S(1)}, u32[]{:S(2)}, u32[]{:S(2)}) collective-permute-start(bf16[864,128]{1,0:T(8,128)(2,1)S(1)} %get-tuple-element.145), channel_id=1, source_target_pairs={{0,2},{1,3},{2,0},{3,1},{4,6},{5,7},{6,4},{7,5},{8,10},{9,11},{10,... | collective-permute-start | bytes 663560 | tf_op jit(solution)/shard_map/ppermute | solution.py:809
  194.5 18.7 %collective-permute-start.36 = (bf16[864,128]{1,0:T(8,128)(2,1)S(1)}, bf16[864,128]{1,0:T(8,128)(2,1)S(1)}, u32[]{:S(2)}, u32[]{:S(2)}) collective-permute-start(bf16[864,128]{1,0:T(8,128)(2,1)S(1)} %get-tuple-element.146), channel_id=1, source_target_pairs={{0,4},{1,5},{2,6},{3,7},{4,0},{5,1},{6,2},{7,3},{8,12},{9,13},{10,... | collective-permute-start | bytes 663560 | tf_op jit(solution)/shard_map/ppermute | solution.py:809
  195.9 17.3 %collective-permute-start.37 = (bf16[864,128]{1,0:T(8,128)(2,1)S(1)}, bf16[864,128]{1,0:T(8,128)(2,1)S(1)}, u32[]{:S(2)}, u32[]{:S(2)}) collective-permute-start(bf16[864,128]{1,0:T(8,128)(2,1)S(1)} %get-tuple-element.147), channel_id=1, source_target_pairs={{0,6},{1,7},{2,4},{3,5},{4,2},{5,3},{6,0},{7,1},{8,14},{9,15},{10,... | collective-permute-start | bytes 663560 | tf_op jit(solution)/shard_map/ppermute | solution.py:809
  197.3 4.7 %collective-permute-start.38 = (bf16[416,128]{1,0:T(8,128)(2,1)S(1)}, bf16[416,128]{1,0:T(8,128)(2,1)S(1)}, u32[]{:S(2)}, u32[]{:S(2)}) collective-permute-start(bf16[416,128]{1,0:T(8,128)(2,1)S(1)} %get-tuple-element.149), channel_id=1, source_target_pairs={{0,8},{1,9},{2,10},{3,11},{4,12},{5,13},{6,14},{7,15},{8,0},{9,1},... | collective-permute-start | bytes 319496 | tf_op jit(solution)/shard_map/ppermute | solution.py:809
  198.8 5.7 %collective-permute-start.39 = (bf16[416,128]{1,0:T(8,128)(2,1)S(1)}, bf16[416,128]{1,0:T(8,128)(2,1)S(1)}, u32[]{:S(2)}, u32[]{:S(2)}) collective-permute-start(bf16[416,128]{1,0:T(8,128)(2,1)S(1)} %get-tuple-element.150), channel_id=1, source_target_pairs={{0,16},{1,17},{2,18},{3,19},{4,20},{5,21},{6,22},{7,23},{8,24},{9,... | collective-permute-start | bytes 319496 | tf_op jit(solution)/shard_map/ppermute | solution.py:809
  202.0 5.6 %collective-permute-start.40 = (bf16[416,128]{1,0:T(8,128)(2,1)S(1)}, bf16[416,128]{1,0:T(8,128)(2,1)S(1)}, u32[]{:S(2)}, u32[]{:S(2)}) collective-permute-start(bf16[416,128]{1,0:T(8,128)(2,1)S(1)} %get-tuple-element.151), channel_id=1, source_target_pairs={{0,24},{1,25},{2,26},{3,27},{4,28},{5,29},{6,30},{7,31},{8,16},{9,... | collective-permute-start | bytes 319496 | tf_op jit(solution)/shard_map/ppermute | solution.py:809
  215.3 5.1 %collective-permute-start.47 = (f32[8,128]{1,0:T(8,128)S(1)}, f32[8,128]{1,0:T(8,128)S(1)}, u32[]{:S(2)}, u32[]{:S(2)}) collective-permute-start(f32[8,128]{1,0:T(8,128)S(1)} %add.29), channel_id=1, source_target_pairs={{0,24},{1,25},{2,26},{3,27},{4,28},{5,29},{6,30},{7,31},{8,16},{9,... | collective-permute-start | bytes 12296 | tf_op jit(solution)/shard_map/ppermute | solution.py:809
  217.8 3.6 %collective-permute-start.46 = (f32[8,128]{1,0:T(8,128)S(1)}, f32[8,128]{1,0:T(8,128)S(1)}, u32[]{:S(2)}, u32[]{:S(2)}) collective-permute-start(f32[8,128]{1,0:T(8,128)S(1)} %add.29), channel_id=1, source_target_pairs={{0,16},{1,17},{2,18},{3,19},{4,20},{5,21},{6,22},{7,23},{8,24},{9,... | collective-permute-start | bytes 12296 | tf_op jit(solution)/shard_map/ppermute | solution.py:809
  218.3 3.6 %collective-permute-start.45 = (f32[8,128]{1,0:T(8,128)S(1)}, f32[8,128]{1,0:T(8,128)S(1)}, u32[]{:S(2)}, u32[]{:S(2)}) collective-permute-start(f32[8,128]{1,0:T(8,128)S(1)} %add.29), channel_id=1, source_target_pairs={{0,8},{1,9},{2,10},{3,11},{4,12},{5,13},{6,14},{7,15},{8,0},{9,1},... | collective-permute-start | bytes 12296 | tf_op jit(solution)/shard_map/ppermute | solution.py:809
  218.8 12.1 %collective-permute-start.41 = (f32[304,128]{1,0:T(8,128)S(1)}, f32[304,128]{1,0:T(8,128)S(1)}, u32[]{:S(2)}, u32[]{:S(2)}) collective-permute-start(f32[304,128]{1,0:T(8,128)S(1)} %get-tuple-element.153), channel_id=1, source_target_pairs={{0,16},{1,17},{2,18},{3,19},{4,20},{5,21},{6,22},{7,23},{8,24},{9,... | collective-permute-start | bytes 466952 | tf_op jit(solution)/shard_map/ppermute | solution.py:809
  220.4 10.6 %collective-permute-start.42 = (f32[304,128]{1,0:T(8,128)S(1)}, f32[304,128]{1,0:T(8,128)S(1)}, u32[]{:S(2)}, u32[]{:S(2)}) collective-permute-start(f32[304,128]{1,0:T(8,128)S(1)} %get-tuple-element.154), channel_id=1, source_target_pairs={{0,1},{1,0},{2,3},{3,2},{4,5},{5,4},{6,7},{7,6},{8,9},{9,8},{10,11... | collective-permute-start | bytes 466952 | tf_op jit(solution)/shard_map/ppermute | solution.py:809
  220.4 10.5 %collective-permute-start.43 = (f32[304,128]{1,0:T(8,128)S(1)}, f32[304,128]{1,0:T(8,128)S(1)}, u32[]{:S(2)}, u32[]{:S(2)}) collective-permute-start(f32[304,128]{1,0:T(8,128)S(1)} %get-tuple-element.155), channel_id=1, source_target_pairs={{0,17},{1,16},{2,19},{3,18},{4,21},{5,20},{6,23},{7,22},{8,25},{9,... | collective-permute-start | bytes 466952 | tf_op jit(solution)/shard_map/ppermute | solution.py:809
  221.9 5.4 %collective-permute-start.50 = (f32[8,128]{1,0:T(8,128)S(1)}, f32[8,128]{1,0:T(8,128)S(1)}, u32[]{:S(2)}, u32[]{:S(2)}) collective-permute-start(f32[8,128]{1,0:T(8,128)S(1)} %add_add_fusion.q0), channel_id=1, source_target_pairs={{0,6},{1,7},{2,4},{3,5},{4,2},{5,3},{6,0},{7,1},{8,14},{9,15},{10,... | collective-permute-start | bytes 12296 | tf_op jit(solution)/shard_map/ppermute | solution.py:809
  224.3 4.8 %collective-permute-start.49 = (f32[8,128]{1,0:T(8,128)S(1)}, f32[8,128]{1,0:T(8,128)S(1)}, u32[]{:S(2)}, u32[]{:S(2)}) collective-permute-start(f32[8,128]{1,0:T(8,128)S(1)} %add_add_fusion.q0), channel_id=1, source_target_pairs={{0,4},{1,5},{2,6},{3,7},{4,0},{5,1},{6,2},{7,3},{8,12},{9,13},{10,... | collective-permute-start | bytes 12296 | tf_op jit(solution)/shard_map/ppermute | solution.py:809
  227.3 3.6 %collective-permute-start.48 = (f32[8,128]{1,0:T(8,128)S(1)}, f32[8,128]{1,0:T(8,128)S(1)}, u32[]{:S(2)}, u32[]{:S(2)}) collective-permute-start(f32[8,128]{1,0:T(8,128)S(1)} %add_add_fusion.q0), channel_id=1, source_target_pairs={{0,2},{1,3},{2,0},{3,1},{4,6},{5,7},{6,4},{7,5},{8,10},{9,11},{10,... | collective-permute-start | bytes 12296 | tf_op jit(solution)/shard_map/ppermute | solution.py:809
  (19 other events, 605.2 us)

commit v2 on v1

--- a/solution.py
+++ b/solution.py
@@ -40,7 +40,7 @@
 
 AXES = ("dp", "fsdp")
 SHARD = ROW_END // 32
-GATHER_CUT = 208
+GATHER_CUT = 240
 SCATTER_CUT = 400
 
 
@@ -91,18 +91,33 @@
 def gathered_parts(coords_ref):
     dp, z, core = coords_ref[0], coords_ref[1], coords_ref[2]
     for side in range(2):
-        for k in range(4):
-            for part in range(4):
-                for kind in range(2):
-                    d, e = (k, part) if kind == 0 else (part, k)
-                    yield side * 8 + kind * 4 + k, part, kind, (dp ^ d) * 8 + (z ^ e) * 2 + (core ^ side)
+        for d in range(4):
+            for e in range(4):
+                shard = (dp ^ d) * 8 + (z ^ e) * 2 + (core ^ side)
+                yield side * 10 + e % 2 * 4 + d, e // 2, 0, shard
+                yield side * 10 + 8 + e % 2, e // 2 * 4 + d, 1, shard
+
+
+def place_vectors(part_ref, coords_ref):
+    lines = lax.broadcasted_iota(jnp.int32, (8, D), 0)
+    width = D // 32
+    mine = lax.broadcasted_iota(jnp.int32, (8, D), 1) // width == lines
+    total = jnp.zeros((8, D), F32)
+    for piece, part, kind, shard in gathered_parts(coords_ref):
+        if kind == 0:
+            rows = part_ref[piece // 10 * 8 + piece % 10].astype(F32)
+            line = jnp.where(mine, jnp.broadcast_to(rows[part : part + 1, :], (8, D)), 0.0)
+            total = total + pltpu.roll(line, shard * width, 1)
+    return jnp.concatenate(
+        [pltpu.roll(total[k : k + 1, :], (D - k * width) % D, 1) for k in range(8)], 0
+    )
 
 
 class FetchGathered:
     def __init__(self, pieces, coords_ref, w_ref, sems, high):
         self.jobs = []
         for number, (piece, part, kind, shard) in enumerate(gathered_parts(coords_ref)):
-            begin, size, step = ((0, GATHER_CUT, GATHER_CUT + 16), (GATHER_CUT, SHARD - GATHER_CUT, SHARD - GATHER_CUT))[kind]
+            begin, size, step = ((0, GATHER_CUT, GATHER_CUT), (GATHER_CUT, SHARD - GATHER_CUT, SHARD - GATHER_CUT))[kind]
             copy = pltpu.make_async_copy(
                 pieces[piece].at[pl.ds(part * step, size)],
                 w_ref.at[pl.ds(pl.multiple_of(shard * SHARD + begin, 16), size)],
@@ -141,13 +156,10 @@
         fetch = fetch_rows(w_hbm[0], 0, ROW_F1, w_ref, sems.at[0])
     copies = []
     if pieces > 1:
-        for piece, part, kind, _ in gathered_parts(coords_ref):
-            if kind == 0:
-                place = pl.ds(part * (GATHER_CUT + 16) + GATHER_CUT, 16)
-                number = len(copies)
-                copies.append(
-                    pltpu.make_async_copy(w_hbm[piece].at[place], part_ref.at[number], part_sems.at[number])
-                )
+        for number in range(16):
+            piece = w_hbm[number // 8 * 10 + number % 8]
+            place = pl.ds(2 * GATHER_CUT, 16)
+            copies.append(pltpu.make_async_copy(piece.at[place], part_ref.at[number], part_sems.at[number]))
         for copy in copies:
             copy.start()
 
@@ -175,10 +187,7 @@
     for copy in copies:
         copy.wait()
     if pieces > 1:
-        both = part_ref[0].astype(F32)
-        for k in range(1, len(copies)):
-            both = both + part_ref[k].astype(F32)
-        vec_ref[...] = both[:8]
+        vec_ref[...] = place_vectors(part_ref, coords_ref)
         fetch.wait(True)
         fetch.start(False)
     else:
@@ -680,9 +689,9 @@
             pltpu.VMEM((ROW_END if number > 1 else ROW_F1, D), BF16),
             pltpu.VMEM((short_len, short_len), F32),
             pltpu.VMEM((short_len, short_len), F32),
-            pltpu.VMEM((32, 16, D), BF16),
+            pltpu.VMEM((16, 16, D), BF16),
             pltpu.SemaphoreType.DMA((jobs,)),
-            pltpu.SemaphoreType.DMA((33,)),
+            pltpu.SemaphoreType.DMA((17,)),
         ],
         compiler_params=pltpu.CompilerParams(vmem_limit_bytes=LIMIT_ATTEND),
         cost_estimate=pl.CostEstimate(flops=9_000_000_000, bytes_accessed=20_000_000, transcendentals=2_400_000),
@@ -810,13 +819,24 @@
 
 
 def gather_pieces(block, vectors):
-    start = lax.axis_index(AXES) * vectors.shape[1]
-    own = lax.dynamic_update_slice(jnp.zeros((16, D), BF16), vectors, (0, start))
+    own = jnp.pad(vectors.reshape(1, -1), ((0, 0), (0, D - vectors.size)))
     first, second = jnp.concatenate([block[:GATHER_CUT], own], 0), block[GATHER_CUT:]
-    along = jnp.concatenate([first] + [swap_with(first, zed=k) for k in (1, 2, 3)], 0)
+    parts = [first, swap_with(first, zed=2)]
     across = jnp.concatenate([second] + [swap_with(second, line=k) for k in (1, 2, 3)], 0)
-    pieces = [along] + [swap_with(along, line=k) for k in (1, 2, 3)]
-    pieces += [across] + [swap_with(across, zed=k) for k in (1, 2, 3)]
+    both = jnp.concatenate(
+        [part[:GATHER_CUT] for part in parts] + [part[GATHER_CUT:] for part in parts] + [jnp.zeros((14, D), BF16)], 0
+    )
+    both, across = lax.optimization_barrier((both, across))
+    other = swap_with(both, zed=1)
+    by_x, by_y = swap_with(both, line=1), swap_with(both, line=2)
+    other, by_x, by_y, across = lax.optimization_barrier((other, by_x, by_y, across))
+    away = swap_with(across, zed=2)
+    other_x, other_y = swap_with(other, line=1), swap_with(other, line=2)
+    pieces = [both, by_x, by_y, swap_with(by_x, line=2)]
+    other_x, other_y, away, across = lax.optimization_barrier((other_x, other_y, away, across))
+    pieces += [other, other_x, other_y, swap_with(other_y, line=1)]
+    across = jnp.concatenate([across, away], 0)
+    pieces += [across, swap_with(across, zed=1)]
     return pieces + [swap_with(piece, core=1) for piece in pieces]
 
 

time: 234 us -> 228 us (0.974)
  starting transfers between devices: 69.6 us -> 59.6 us
  waiting for transfers between devices: 83.1 us -> 86.9 us
    ppermute x51 -> x54, starting transfers between devices: 69.6 us -> 59.6 us  [swap_with(): return lax.ppermute(array, AXES, pairs)]
    ppermute x51 -> x54, waiting for transfers between devices: 83.1 us -> 86.9 us  [swap_with(): return lax.ppermute(array, AXES, pairs)]
  transfers between devices with their start and end apart: 51 -> 54, of which waited for: 20 -> 23; matrix products, arithmetic and copies ran while one was open for 1% -> 0% of each run, Pallas kernels for 10% -> 10%
where the time goes in v2:
time: 228 us
  waiting for transfers between devices  86.9 us (38%)
  Pallas kernels  76.1 us (33%)
  starting transfers between devices  59.6 us (26%)
    ppermute x54, waiting for transfers between devices, swap_with(): return lax.ppermute(array, AXES, pairs)  86.9 us
    ppermute x54, starting transfers between devices, swap_with(): return lax.ppermute(array, AXES, pairs)  59.6 us
    pallas_call x1, Pallas kernels, device_grads(): pl.pallas_call(partial(deep_kernel, count), out_shape=(shape((ROW_HALF -...  31.4 us
    pallas_call x1, Pallas kernels, device_grads(): pl.pallas_call(partial(back_kernel, short_len), out_shape=(shape((ROW_F1,...  20.5 us
    pallas_call x1, Pallas kernels, device_grads(): pl.pallas_call(partial(attend_kernel, short_len, slots, number), out_shap...  16.6 us
  transfers between devices with their start and end apart: 54, of which 23 were waited for; matrix products, arithmetic and copies ran while one was open for 0% of the time, Pallas kernels for 10%

profile of v2, /device:TPU:0, one launch (start us, length us, event | category | flops | bytes accessed | tf_op | source)
XLA Modules:
  0.0 227.7 jit_solution(15577598998621694780)
XLA Ops:
  1.4 1.1 convert_element_type.8
  2.6 4.1 %collective-permute-start = (bf16[241,512]{1,0:T(8,128)(2,1)S(1)}, bf16[241,512]{1,0:T(8,128)(2,1)S(1)}, u32[]{:S(2)}, u32[]{:S(2)}) collective-permute-start(bf16[241,512]{1,0:T(8,128)(2,1)S(1)} %pad_maximum_fusion.1), channel_id=1, source_target_pairs={{0,4},{1,5},{2,6},{3,7},{4,0},{5,1},{6,2},{7,3},{8,12},{9,13},{10,... | collective-permute-start | bytes 740360 | tf_op jit(solution)/shard_map/ppermute | solution.py:818
  6.7 2.5 %collective-permute-start.3 = (bf16[64,512]{1,0:T(8,128)(2,1)S(1)}, bf16[64,512]{1,0:T(8,128)(2,1)S(1)}, u32[]{:S(2)}, u32[]{:S(2)}) collective-permute-start(bf16[64,512]{1,0:T(8,128)(2,1)S(1)} %slice.19), channel_id=1, source_target_pairs={{0,24},{1,25},{2,26},{3,27},{4,28},{5,29},{6,30},{7,31},{8,16},{9,... | collective-permute-start | bytes 196616 | tf_op jit(solution)/shard_map/ppermute | solution.py:818
  10.3 1.8 collective-permute-done.3
  12.1 1.4 collective-permute-done.2
  14.0 4.3 %collective-permute-done = bf16[241,512]{1,0:T(8,128)(2,1)S(1)} collective-permute-done((bf16[241,512]{1,0:T(8,128)(2,1)S(1)}, bf16[241,512]{1,0:T(8,128)(2,1)S(1)}, u32[]{:S(2)}, u32[]{:S(2)}) %collective-permute-start) | collective-permute-done | bytes 246816 | tf_op jit(solution)/shard_map/ppermute | solution.py:818
  18.7 1.6 collective-permute-start.6
  20.3 1.5 collective-permute-start.5
  22.5 9.0 %collective-permute-done.6.refs_2_ = bf16[496,512]{1,0:T(8,128)(2,1)S(1)} collective-permute-done((bf16[496,512]{1,0:T(8,128)(2,1)S(1)}, bf16[496,512]{1,0:T(8,128)(2,1)S(1)}, u32[]{:S(2)}, u32[]{:S(2)}) %collective-permute-start.6) | collective-permute-done | bytes 507936 | tf_op jit(solution)/shard_map/ppermute | solution.py:818
  32.5 1.2 collective-permute-done.4.refs_4_
  35.0 3.1 %collective-permute-start.10 = (bf16[256,512]{1,0:T(8,128)(2,1)S(1)}, bf16[256,512]{1,0:T(8,128)(2,1)S(1)}, u32[]{:S(2)}, u32[]{:S(2)}) collective-permute-start(bf16[256,512]{1,0:T(8,128)(2,1)S(1)} %pad_maximum_fusion), channel_id=1, source_target_pairs={{0,4},{1,5},{2,6},{3,7},{4,0},{5,1},{6,2},{7,3},{8,12},{9,13},{10,... | collective-permute-start | bytes 786440 | tf_op jit(solution)/shard_map/ppermute | solution.py:818
  38.1 1.5 collective-permute-start.7
  39.6 8.8 %collective-permute-done.10 = bf16[256,512]{1,0:T(8,128)(2,1)S(1)} collective-permute-done((bf16[256,512]{1,0:T(8,128)(2,1)S(1)}, bf16[256,512]{1,0:T(8,128)(2,1)S(1)}, u32[]{:S(2)}, u32[]{:S(2)}) %collective-permute-start.10) | collective-permute-done | bytes 262176 | tf_op jit(solution)/shard_map/ppermute | solution.py:818
  48.6 1.6 collective-permute-start.12
  50.7 5.2 %collective-permute-done.7.refs_3_ = bf16[496,512]{1,0:T(8,128)(2,1)S(1)} collective-permute-done((bf16[496,512]{1,0:T(8,128)(2,1)S(1)}, bf16[496,512]{1,0:T(8,128)(2,1)S(1)}, u32[]{:S(2)}, u32[]{:S(2)}) %collective-permute-start.7) | collective-permute-done | bytes 507936 | tf_op jit(solution)/shard_map/ppermute | solution.py:818
  56.6 6.3 %collective-permute-done.12.refs_9_ = bf16[512,512]{1,0:T(8,128)(2,1)S(1)} collective-permute-done((bf16[512,512]{1,0:T(8,128)(2,1)S(1)}, bf16[512,512]{1,0:T(8,128)(2,1)S(1)}, u32[]{:S(2)}, u32[]{:S(2)}) %collective-permute-start.12) | collective-permute-done | bytes 524320 | tf_op jit(solution)/shard_map/ppermute | solution.py:818
  63.7 6.5 %collective-permute-done.11.refs_7_ = bf16[496,512]{1,0:T(8,128)(2,1)} collective-permute-done((bf16[496,512]{1,0:T(8,128)(2,1)}, bf16[496,512]{1,0:T(8,128)(2,1)}, u32[]{:S(2)}, u32[]{:S(2)}) %collective-permute-start.11) | collective-permute-done | bytes 507936 | tf_op jit(solution)/shard_map/ppermute | solution.py:818
  70.8 1.6 collective-permute-done.20.refs_17_
  73.2 16.6 %attend.1 = (bf16[9728,512]{1,0:T(8,128)(2,1)}, bf16[768,1536]{1,0:T(8,128)(2,1)S(1)}, f32[768,512]{1,0:T(8,128)S(1)}, bf16[768,512]{1,0:T(8,128)(2,1)S(1)}, bf1...) custom-call(s32[4]{0:T(128)S(1)} %pad_add_fusion.coords_ref, ...), custom_call_target="tpu_custom_call" | custom-call | flops 8999999488 | bytes 20000000 | tf_op jit(solution)/shard_map/attend/pallas_call | solution.py:683
  89.8 31.4 %deep.1 = (bf16[1024,256]{1,0:T(8,128)(2,1)S(1)}, bf16[1024,256]{1,0:T(8,128)(2,1)S(1)}, bf16[4864,256]{1,0:T(8,128)(2,1)S(1)}, bf16[4864,256]{1,0:T(8,128)(2,1)...) custom-call(s32[4]{0:T(128)S(1)} %pad_add_fusion.coords_ref, ...), custom_call_target="tpu_custom_call" | custom-call | tf_op jit(solution)/shard_map/deep/pallas_call | solution.py:701
  121.8 4.2 %collective-permute-done.23.recv_ref = bf16[4864,256]{1,0:T(8,128)(2,1)S(1)} collective-permute-done((bf16[4864,256]{1,0:T(8,128)(2,1)S(1)}, bf16[4864,256]{1,0:T(8,128)(2,1)S(1)}, u32[]{:S(2)}, u32[]{:S(2)}) %collective-permute-start.23) | collective-permute-done | bytes 2490400 | tf_op jit(solution)/shard_map/ppermute | solution.py:818
  126.0 1.2 core_sum.1
  127.2 4.5 %collective-permute-start.28 = (bf16[832,128]{1,0:T(8,128)(2,1)S(1)}, bf16[832,128]{1,0:T(8,128)(2,1)S(1)}, u32[]{:S(2)}, u32[]{:S(2)}) collective-permute-start(bf16[832,128]{1,0:T(8,128)(2,1)S(1)} %get-tuple-element.129), channel_id=1, source_target_pairs={{0,4},{1,5},{2,6},{3,7},{4,0},{5,1},{6,2},{7,3},{8,12},{9,13},{10,... | collective-permute-start | bytes 638984 | tf_op jit(solution)/shard_map/ppermute | solution.py:818
  134.0 2.2 collective-permute-start.27
  136.2 20.5 %back.1 = (bf16[3840,256]{1,0:T(8,128)(2,1)S(1)}, bf16[3872,256]{1,0:T(8,128)(2,1)S(1)}, f32[8,512]{1,0:T(8,128)S(1)}) custom-call(s32[4]{0:T(128)S(1)} %pad_add_fusion.coords_ref, s32[2]{0:T(128)S(1)} %bitcast.11, f32[8,512]{1,0:T(8,128)S(1)} %get-tuple-element.107.vec_ref, f32[8,512]{1,0:T(8,128)S(1)} %get-tuple-element.131.deep_small_ref, ...), custom_call_target="tpu_custom_call" | custom-call | flops 19000000512 | bytes 20000000 | tf_op jit(solution)/shard_map/back/pallas_call | solution.py:737
  157.3 3.5 %collective-permute-done.30.recv_front = bf16[3872,256]{1,0:T(8,128)(2,1)S(1)} collective-permute-done((bf16[3872,256]{1,0:T(8,128)(2,1)S(1)}, bf16[3872,256]{1,0:T(8,128)(2,1)S(1)}, u32[]{:S(2)}, u32[]{:S(2)}) %collective-permute-start.30) | collective-permute-done | bytes 1982496 | tf_op jit(solution)/shard_map/ppermute | solution.py:818
  160.8 1.9 core_sum_front.1
  164.6 2.1 collective-permute-start.33
  166.7 2.9 %collective-permute-start.35 = (bf16[832,128]{1,0:T(8,128)(2,1)S(1)}, bf16[832,128]{1,0:T(8,128)(2,1)S(1)}, u32[]{:S(2)}, u32[]{:S(2)}) collective-permute-start(bf16[832,128]{1,0:T(8,128)(2,1)S(1)} %get-tuple-element.154), channel_id=1, source_target_pairs={{0,4},{1,5},{2,6},{3,7},{4,0},{5,1},{6,2},{7,3},{8,12},{9,13},{10,... | collective-permute-start | bytes 638984 | tf_op jit(solution)/shard_map/ppermute | solution.py:818
  169.7 1.9 collective-permute-done.34.refs_5_
  171.6 2.3 %collective-permute-start.36 = (bf16[832,128]{1,0:T(8,128)(2,1)S(1)}, bf16[832,128]{1,0:T(8,128)(2,1)S(1)}, u32[]{:S(2)}, u32[]{:S(2)}) collective-permute-start(bf16[832,128]{1,0:T(8,128)(2,1)S(1)} %get-tuple-element.155), channel_id=1, source_target_pairs={{0,6},{1,7},{2,4},{3,5},{4,2},{5,3},{6,0},{7,1},{8,14},{9,15},{10,... | collective-permute-start | bytes 638984 | tf_op jit(solution)/shard_map/ppermute | solution.py:818
  173.9 10.8 %collective-permute-done.35.refs_6_ = bf16[832,128]{1,0:T(8,128)(2,1)S(1)} collective-permute-done((bf16[832,128]{1,0:T(8,128)(2,1)S(1)}, bf16[832,128]{1,0:T(8,128)(2,1)S(1)}, u32[]{:S(2)}, u32[]{:S(2)}) %collective-permute-start.35) | collective-permute-done | bytes 213024 | tf_op jit(solution)/shard_map/ppermute | solution.py:818
  184.8 1.2 first_sum.1
  186.0 3.8 %collective-permute-start.38 = (bf16[864,128]{1,0:T(8,128)(2,1)S(1)}, bf16[864,128]{1,0:T(8,128)(2,1)S(1)}, u32[]{:S(2)}, u32[]{:S(2)}) collective-permute-start(bf16[864,128]{1,0:T(8,128)(2,1)S(1)} %get-tuple-element.165), channel_id=1, source_target_pairs={{0,2},{1,3},{2,0},{3,1},{4,6},{5,7},{6,4},{7,5},{8,10},{9,11},{10,... | collective-permute-start | bytes 663560 | tf_op jit(solution)/shard_map/ppermute | solution.py:818
  189.7 1.2 collective-permute-start.39
  191.0 1.4 collective-permute-start.40
  193.6 3.4 %collective-permute-done.41.refs_5_ = bf16[416,128]{1,0:T(8,128)(2,1)S(1)} collective-permute-done((bf16[416,128]{1,0:T(8,128)(2,1)S(1)}, bf16[416,128]{1,0:T(8,128)(2,1)S(1)}, u32[]{:S(2)}, u32[]{:S(2)}) %collective-permute-start.41) | collective-permute-done | bytes 106528 | tf_op jit(solution)/shard_map/ppermute | solution.py:818
  197.8 4.9 %collective-permute-done.43.refs_7_ = bf16[416,128]{1,0:T(8,128)(2,1)S(1)} collective-permute-done((bf16[416,128]{1,0:T(8,128)(2,1)S(1)}, bf16[416,128]{1,0:T(8,128)(2,1)S(1)}, u32[]{:S(2)}, u32[]{:S(2)}) %collective-permute-start.43) | collective-permute-done | bytes 106528 | tf_op jit(solution)/shard_map/ppermute | solution.py:818
  202.7 5.6 %collective-permute-done.39.refs_2_ = bf16[864,128]{1,0:T(8,128)(2,1)S(1)} collective-permute-done((bf16[864,128]{1,0:T(8,128)(2,1)S(1)}, bf16[864,128]{1,0:T(8,128)(2,1)S(1)}, u32[]{:S(2)}, u32[]{:S(2)}) %collective-permute-start.39) | collective-permute-done | bytes 221216 | tf_op jit(solution)/shard_map/ppermute | solution.py:818
  209.2 1.2 collective-permute-done.47
  210.9 1.5 collective-permute-start.49
  212.3 1.5 collective-permute-start.48
  214.9 1.1 collective-permute-start.46
  216.1 2.1 collective-permute-start.53
  218.1 2.5 %collective-permute-start.52 = (f32[8,128]{1,0:T(8,128)S(1)}, f32[8,128]{1,0:T(8,128)S(1)}, u32[]{:S(2)}, u32[]{:S(2)}) collective-permute-start(f32[8,128]{1,0:T(8,128)S(1)} %add_add_fusion.q0), channel_id=1, source_target_pairs={{0,4},{1,5},{2,6},{3,7},{4,0},{5,1},{6,2},{7,3},{8,12},{9,13},{10,... | collective-permute-start | bytes 12296 | tf_op jit(solution)/shard_map/ppermute | solution.py:818
  221.5 1.2 collective-permute-start.51
  222.7 2.4 %collective-permute-done.51.q1 = f32[8,128]{1,0:T(8,128)S(1)} collective-permute-done((f32[8,128]{1,0:T(8,128)S(1)}, f32[8,128]{1,0:T(8,128)S(1)}, u32[]{:S(2)}, u32[]{:S(2)}) %collective-permute-start.51) | collective-permute-done | bytes 4128 | tf_op jit(solution)/shard_map/ppermute | solution.py:818
  225.2 2.5 %update.1 = (f32[1,1]{1,0:T(1,128)}, f32[1,1]{1,0:T(1,128)}, f32[304,512]{1,0:T(8,128)}, f32[304,512]{1,0:T(8,128)}, f32[304,512]{1,0:T(8,128)}, /*index=5*/f32[...) custom-call(s32[4]{0:T(128)S(1)} %pad_add_fusion.coords_ref, f32[304,128]{1,0:T(8,128)S(1)} %get-tuple-element.172.g0, ...), custom_call_target="tpu_custom_call" | custom-call | tf_op jit(solution)/shard_map/update/pallas_call | solution.py:897
  (133 shorter events, 19.9 us)
Async XLA Ops:
  2.6 15.7 %collective-permute-start = (bf16[241,512]{1,0:T(8,128)(2,1)S(1)}, bf16[241,512]{1,0:T(8,128)(2,1)S(1)}, u32[]{:S(2)}, u32[]{:S(2)}) collective-permute-start(bf16[241,512]{1,0:T(8,128)(2,1)S(1)} %pad_maximum_fusion.1), channel_id=1, source_target_pairs={{0,4},{1,5},{2,6},{3,7},{4,0},{5,1},{6,2},{7,3},{8,12},{9,13},{10,... | collective-permute-start | bytes 740360 | tf_op jit(solution)/shard_map/ppermute | solution.py:818
  6.7 5.3 %collective-permute-start.3 = (bf16[64,512]{1,0:T(8,128)(2,1)S(1)}, bf16[64,512]{1,0:T(8,128)(2,1)S(1)}, u32[]{:S(2)}, u32[]{:S(2)}) collective-permute-start(bf16[64,512]{1,0:T(8,128)(2,1)S(1)} %slice.19), channel_id=1, source_target_pairs={{0,24},{1,25},{2,26},{3,27},{4,28},{5,29},{6,30},{7,31},{8,16},{9,... | collective-permute-start | bytes 196616 | tf_op jit(solution)/shard_map/ppermute | solution.py:818
  9.2 4.3 %collective-permute-start.2 = (bf16[64,512]{1,0:T(8,128)(2,1)S(1)}, bf16[64,512]{1,0:T(8,128)(2,1)S(1)}, u32[]{:S(2)}, u32[]{:S(2)}) collective-permute-start(bf16[64,512]{1,0:T(8,128)(2,1)S(1)} %slice.19), channel_id=1, source_target_pairs={{0,16},{1,17},{2,18},{3,19},{4,20},{5,21},{6,22},{7,23},{8,24},{9,... | collective-permute-start | bytes 196616 | tf_op jit(solution)/shard_map/ppermute | solution.py:818
  18.7 12.8 %collective-permute-start.6 = (bf16[496,512]{1,0:T(8,128)(2,1)S(1)}, bf16[496,512]{1,0:T(8,128)(2,1)S(1)}, u32[]{:S(2)}, u32[]{:S(2)}) collective-permute-start(bf16[496,512]{1,0:T(8,128)(2,1)S(1)} %concatenate.13.refs_0_), channel_id=1, source_target_pairs={{0,16},{1,17},{2,18},{3,19},{4,20},{5,21},{6,22},{7,23},{8,24},{9,... | collective-permute-start | bytes 1523720 | tf_op jit(solution)/shard_map/ppermute | solution.py:818
  20.3 12.2 %collective-permute-start.5 = (bf16[496,512]{1,0:T(8,128)(2,1)S(1)}, bf16[496,512]{1,0:T(8,128)(2,1)S(1)}, u32[]{:S(2)}, u32[]{:S(2)}) collective-permute-start(bf16[496,512]{1,0:T(8,128)(2,1)S(1)} %concatenate.13.refs_0_), channel_id=1, source_target_pairs={{0,8},{1,9},{2,10},{3,11},{4,12},{5,13},{6,14},{7,15},{8,0},{9,1},... | collective-permute-start | bytes 1523720 | tf_op jit(solution)/shard_map/ppermute | solution.py:818
  21.8 11.9 %collective-permute-start.4 = (bf16[496,512]{1,0:T(8,128)(2,1)S(1)}, bf16[496,512]{1,0:T(8,128)(2,1)S(1)}, u32[]{:S(2)}, u32[]{:S(2)}) collective-permute-start(bf16[496,512]{1,0:T(8,128)(2,1)S(1)} %concatenate.13.refs_0_), channel_id=1, source_target_pairs={{0,2},{1,3},{2,0},{3,1},{4,6},{5,7},{6,4},{7,5},{8,10},{9,11},{10,... | collective-permute-start | bytes 1523720 | tf_op jit(solution)/shard_map/ppermute | solution.py:818
  33.7 14.8 %collective-permute-start.9 = (bf16[496,512]{1,0:T(8,128)(2,1)S(1)}, bf16[496,512]{1,0:T(8,128)(2,1)}, u32[]{:S(2)}, u32[]{:S(2)}) collective-permute-start(bf16[496,512]{1,0:T(8,128)(2,1)S(1)} %collective-permute-done.4.refs_4_), channel_id=1, source_target_pairs={{0,16},{1,17},{2,18},{3,19},{4,20},{5,21},{6,22},{7,23},{8,24},{9,... | collective-permute-start | bytes 1523720 | tf_op jit(solution)/shard_map/ppermute | solution.py:818
  34.2 14.3 %collective-permute-start.8 = (bf16[496,512]{1,0:T(8,128)(2,1)S(1)}, bf16[496,512]{1,0:T(8,128)(2,1)}, u32[]{:S(2)}, u32[]{:S(2)}) collective-permute-start(bf16[496,512]{1,0:T(8,128)(2,1)S(1)} %collective-permute-done.4.refs_4_), channel_id=1, source_target_pairs={{0,8},{1,9},{2,10},{3,11},{4,12},{5,13},{6,14},{7,15},{8,0},{9,1},... | collective-permute-start | bytes 1523720 | tf_op jit(solution)/shard_map/ppermute | solution.py:818
  35.0 13.5 %collective-permute-start.10 = (bf16[256,512]{1,0:T(8,128)(2,1)S(1)}, bf16[256,512]{1,0:T(8,128)(2,1)S(1)}, u32[]{:S(2)}, u32[]{:S(2)}) collective-permute-start(bf16[256,512]{1,0:T(8,128)(2,1)S(1)} %pad_maximum_fusion), channel_id=1, source_target_pairs={{0,4},{1,5},{2,6},{3,7},{4,0},{5,1},{6,2},{7,3},{8,12},{9,13},{10,... | collective-permute-start | bytes 786440 | tf_op jit(solution)/shard_map/ppermute | solution.py:818
  38.1 12.1 %collective-permute-start.13 = (bf16[496,512]{1,0:T(8,128)(2,1)S(1)}, bf16[496,512]{1,0:T(8,128)(2,1)S(1)}, u32[]{:S(2)}, u32[]{:S(2)}) collective-permute-start(bf16[496,512]{1,0:T(8,128)(2,1)S(1)} %concatenate.13.refs_0_), channel_id=1, source_target_pairs={{0,1},{1,0},{2,3},{3,2},{4,5},{5,4},{6,7},{7,6},{8,9},{9,8},{10,11... | collective-permute-start | bytes 1523720 | tf_op jit(solution)/shard_map/ppermute | solution.py:818
  38.1 17.7 %collective-permute-start.7 = (bf16[496,512]{1,0:T(8,128)(2,1)S(1)}, bf16[496,512]{1,0:T(8,128)(2,1)S(1)}, u32[]{:S(2)}, u32[]{:S(2)}) collective-permute-start(bf16[496,512]{1,0:T(8,128)(2,1)S(1)} %collective-permute-done.5.refs_1_), channel_id=1, source_target_pairs={{0,16},{1,17},{2,18},{3,19},{4,20},{5,21},{6,22},{7,23},{8,24},{9,... | collective-permute-start | bytes 1523720 | tf_op jit(solution)/shard_map/ppermute | solution.py:818
  48.5 7.4 %collective-permute-start.15 = (bf16[496,512]{1,0:T(8,128)(2,1)S(1)}, bf16[496,512]{1,0:T(8,128)(2,1)S(1)}, u32[]{:S(2)}, u32[]{:S(2)}) collective-permute-start(bf16[496,512]{1,0:T(8,128)(2,1)S(1)} %collective-permute-done.6.refs_2_), channel_id=1, source_target_pairs={{0,1},{1,0},{2,3},{3,2},{4,5},{5,4},{6,7},{7,6},{8,9},{9,8},{10,11... | collective-permute-start | bytes 1523720 | tf_op jit(solution)/shard_map/ppermute | solution.py:818
  48.6 14.4 %collective-permute-start.12 = (bf16[512,512]{1,0:T(8,128)(2,1)S(1)}, bf16[512,512]{1,0:T(8,128)(2,1)S(1)}, u32[]{:S(2)}, u32[]{:S(2)}) collective-permute-start(bf16[512,512]{1,0:T(8,128)(2,1)S(1)} %constant_dynamic-update-slice_fusion.refs_8_), channel_id=1, source_target_pairs={{0,2},{1,3},{2,0},{3,1},{4,6},{5,7},{6,4},{7,5},{8,10},{9,11},{10,... | collective-permute-start | bytes 1572872 | tf_op jit(solution)/shard_map/ppermute | solution.py:818
  50.2 6.3 %collective-permute-start.14 = (bf16[496,512]{1,0:T(8,128)(2,1)S(1)}, bf16[496,512]{1,0:T(8,128)(2,1)S(1)}, u32[]{:S(2)}, u32[]{:S(2)}) collective-permute-start(bf16[496,512]{1,0:T(8,128)(2,1)S(1)} %collective-permute-done.5.refs_1_), channel_id=1, source_target_pairs={{0,1},{1,0},{2,3},{3,2},{4,5},{5,4},{6,7},{7,6},{8,9},{9,8},{10,11... | collective-permute-start | bytes 1523720 | tf_op jit(solution)/shard_map/ppermute | solution.py:818
  50.2 12.8 %collective-permute-start.17 = (bf16[496,512]{1,0:T(8,128)(2,1)S(1)}, bf16[496,512]{1,0:T(8,128)(2,1)S(1)}, u32[]{:S(2)}, u32[]{:S(2)}) collective-permute-start(bf16[496,512]{1,0:T(8,128)(2,1)S(1)} %collective-permute-done.4.refs_4_), channel_id=1, source_target_pairs={{0,1},{1,0},{2,3},{3,2},{4,5},{5,4},{6,7},{7,6},{8,9},{9,8},{10,11... | collective-permute-start | bytes 1523720 | tf_op jit(solution)/shard_map/ppermute | solution.py:818
  55.8 7.7 %collective-permute-start.16 = (bf16[496,512]{1,0:T(8,128)(2,1)S(1)}, bf16[496,512]{1,0:T(8,128)(2,1)S(1)}, u32[]{:S(2)}, u32[]{:S(2)}) collective-permute-start(bf16[496,512]{1,0:T(8,128)(2,1)S(1)} %collective-permute-done.7.refs_3_), channel_id=1, source_target_pairs={{0,1},{1,0},{2,3},{3,2},{4,5},{5,4},{6,7},{7,6},{8,9},{9,8},{10,11... | collective-permute-start | bytes 1523720 | tf_op jit(solution)/shard_map/ppermute | solution.py:818
  55.9 14.3 %collective-permute-start.11 = (bf16[496,512]{1,0:T(8,128)(2,1)}, bf16[496,512]{1,0:T(8,128)(2,1)}, u32[]{:S(2)}, u32[]{:S(2)}) collective-permute-start(bf16[496,512]{1,0:T(8,128)(2,1)} %collective-permute-done.9.refs_6_), channel_id=1, source_target_pairs={{0,8},{1,9},{2,10},{3,11},{4,12},{5,13},{6,14},{7,15},{8,0},{9,1},... | collective-permute-start | bytes 1523720 | tf_op jit(solution)/shard_map/ppermute | solution.py:818
  56.5 14.3 %collective-permute-start.21 = (bf16[512,512]{1,0:T(8,128)(2,1)S(1)}, bf16[512,512]{1,0:T(8,128)(2,1)S(1)}, u32[]{:S(2)}, u32[]{:S(2)}) collective-permute-start(bf16[512,512]{1,0:T(8,128)(2,1)S(1)} %constant_dynamic-update-slice_fusion.refs_8_), channel_id=1, source_target_pairs={{0,1},{1,0},{2,3},{3,2},{4,5},{5,4},{6,7},{7,6},{8,9},{9,8},{10,11... | collective-permute-start | bytes 1572872 | tf_op jit(solution)/shard_map/ppermute | solution.py:818
  63.0 9.4 %collective-permute-start.22 = (bf16[512,512]{1,0:T(8,128)(2,1)S(1)}, bf16[512,512]{1,0:T(8,128)(2,1)S(1)}, u32[]{:S(2)}, u32[]{:S(2)}) collective-permute-start(bf16[512,512]{1,0:T(8,128)(2,1)S(1)} %collective-permute-done.12.refs_9_), channel_id=1, source_target_pairs={{0,1},{1,0},{2,3},{3,2},{4,5},{5,4},{6,7},{7,6},{8,9},{9,8},{10,11... | collective-permute-start | bytes 1572872 | tf_op jit(solution)/shard_map/ppermute | solution.py:818
  63.0 7.8 %collective-permute-start.18 = (bf16[496,512]{1,0:T(8,128)(2,1)}, bf16[496,512]{1,0:T(8,128)(2,1)}, u32[]{:S(2)}, u32[]{:S(2)}) collective-permute-start(bf16[496,512]{1,0:T(8,128)(2,1)} %collective-permute-done.8.refs_5_), channel_id=1, source_target_pairs={{0,1},{1,0},{2,3},{3,2},{4,5},{5,4},{6,7},{7,6},{8,9},{9,8},{10,11... | collective-permute-start | bytes 1523720 | tf_op jit(solution)/shard_map/ppermute | solution.py:818
  63.6 7.2 %collective-permute-start.19 = (bf16[496,512]{1,0:T(8,128)(2,1)}, bf16[496,512]{1,0:T(8,128)(2,1)}, u32[]{:S(2)}, u32[]{:S(2)}) collective-permute-start(bf16[496,512]{1,0:T(8,128)(2,1)} %collective-permute-done.9.refs_6_), channel_id=1, source_target_pairs={{0,1},{1,0},{2,3},{3,2},{4,5},{5,4},{6,7},{7,6},{8,9},{9,8},{10,11... | collective-permute-start | bytes 1523720 | tf_op jit(solution)/shard_map/ppermute | solution.py:818
  121.2 4.8 %collective-permute-start.23 = (bf16[4864,256]{1,0:T(8,128)(2,1)S(1)}, bf16[4864,256]{1,0:T(8,128)(2,1)S(1)}, u32[]{:S(2)}, u32[]{:S(2)}) collective-permute-start(bf16[4864,256]{1,0:T(8,128)(2,1)S(1)} %get-tuple-element.113), channel_id=1, source_target_pairs={{0,1},{1,0},{2,3},{3,2},{4,5},{5,4},{6,7},{7,6},{8,9},{9,8},{10,11... | collective-permute-start | bytes 7471112 | tf_op jit(solution)/shard_map/ppermute | solution.py:818
  121.4 5.8 %collective-permute-start.24 = (bf16[1024,256]{1,0:T(8,128)(2,1)S(1)}, bf16[1024,256]{1,0:T(8,128)(2,1)S(1)}, u32[]{:S(2)}, u32[]{:S(2)}) collective-permute-start(bf16[1024,256]{1,0:T(8,128)(2,1)S(1)} %get-tuple-element.122), channel_id=1, source_target_pairs={{0,1},{1,0},{2,3},{3,2},{4,5},{5,4},{6,7},{7,6},{8,9},{9,8},{10,11... | collective-permute-start | bytes 1572872 | tf_op jit(solution)/shard_map/ppermute | solution.py:818
  127.2 29.5 %collective-permute-start.28 = (bf16[832,128]{1,0:T(8,128)(2,1)S(1)}, bf16[832,128]{1,0:T(8,128)(2,1)S(1)}, u32[]{:S(2)}, u32[]{:S(2)}) collective-permute-start(bf16[832,128]{1,0:T(8,128)(2,1)S(1)} %get-tuple-element.129), channel_id=1, source_target_pairs={{0,4},{1,5},{2,6},{3,7},{4,0},{5,1},{6,2},{7,3},{8,12},{9,13},{10,... | collective-permute-start | bytes 638984 | tf_op jit(solution)/shard_map/ppermute | solution.py:818
  131.7 25.0 %collective-permute-start.29 = (bf16[832,128]{1,0:T(8,128)(2,1)S(1)}, bf16[832,128]{1,0:T(8,128)(2,1)S(1)}, u32[]{:S(2)}, u32[]{:S(2)}) collective-permute-start(bf16[832,128]{1,0:T(8,128)(2,1)S(1)} %get-tuple-element.130), channel_id=1, source_target_pairs={{0,6},{1,7},{2,4},{3,5},{4,2},{5,3},{6,0},{7,1},{8,14},{9,15},{10,... | collective-permute-start | bytes 638984 | tf_op jit(solution)/shard_map/ppermute | solution.py:818
  132.7 24.0 %collective-permute-start.25 = (bf16[1600,128]{1,0:T(8,128)(2,1)S(1)}, bf16[1600,128]{1,0:T(8,128)(2,1)S(1)}, u32[]{:S(2)}, u32[]{:S(2)}) collective-permute-start(bf16[1600,128]{1,0:T(8,128)(2,1)S(1)} %get-tuple-element.125), channel_id=1, source_target_pairs={{0,8},{1,9},{2,10},{3,11},{4,12},{5,13},{6,14},{7,15},{8,0},{9,1},... | collective-permute-start | bytes 1228808 | tf_op jit(solution)/shard_map/ppermute | solution.py:818
  133.3 23.4 %collective-permute-start.26 = (bf16[1600,128]{1,0:T(8,128)(2,1)S(1)}, bf16[1600,128]{1,0:T(8,128)(2,1)S(1)}, u32[]{:S(2)}, u32[]{:S(2)}) collective-permute-start(bf16[1600,128]{1,0:T(8,128)(2,1)S(1)} %get-tuple-element.126), channel_id=1, source_target_pairs={{0,16},{1,17},{2,18},{3,19},{4,20},{5,21},{6,22},{7,23},{8,24},{9,... | collective-permute-start | bytes 1228808 | tf_op jit(solution)/shard_map/ppermute | solution.py:818
  134.0 22.7 %collective-permute-start.27 = (bf16[1600,128]{1,0:T(8,128)(2,1)S(1)}, bf16[1600,128]{1,0:T(8,128)(2,1)S(1)}, u32[]{:S(2)}, u32[]{:S(2)}) collective-permute-start(bf16[1600,128]{1,0:T(8,128)(2,1)S(1)} %get-tuple-element.127), channel_id=1, source_target_pairs={{0,24},{1,25},{2,26},{3,27},{4,28},{5,29},{6,30},{7,31},{8,16},{9,... | collective-permute-start | bytes 1228808 | tf_op jit(solution)/shard_map/ppermute | solution.py:818
  156.8 9.9 %collective-permute-start.37 = (bf16[832,128]{1,0:T(8,128)(2,1)S(1)}, bf16[832,128]{1,0:T(8,128)(2,1)S(1)}, u32[]{:S(2)}, u32[]{:S(2)}) collective-permute-start(bf16[832,128]{1,0:T(8,128)(2,1)S(1)} %get-tuple-element.161), channel_id=1, source_target_pairs={{0,2},{1,3},{2,0},{3,1},{4,6},{5,7},{6,4},{7,5},{8,10},{9,11},{10,... | collective-permute-start | bytes 638984 | tf_op jit(solution)/shard_map/ppermute | solution.py:818
  162.7 8.9 %collective-permute-start.34 = (bf16[832,128]{1,0:T(8,128)(2,1)S(1)}, bf16[832,128]{1,0:T(8,128)(2,1)S(1)}, u32[]{:S(2)}, u32[]{:S(2)}) collective-permute-start(bf16[832,128]{1,0:T(8,128)(2,1)S(1)} %get-tuple-element.153), channel_id=1, source_target_pairs={{0,2},{1,3},{2,0},{3,1},{4,6},{5,7},{6,4},{7,5},{8,10},{9,11},{10,... | collective-permute-start | bytes 638984 | tf_op jit(solution)/shard_map/ppermute | solution.py:818
  163.2 21.5 %collective-permute-start.31 = (bf16[1664,128]{1,0:T(8,128)(2,1)S(1)}, bf16[1664,128]{1,0:T(8,128)(2,1)S(1)}, u32[]{:S(2)}, u32[]{:S(2)}) collective-permute-start(bf16[1664,128]{1,0:T(8,128)(2,1)S(1)} %get-tuple-element.149), channel_id=1, source_target_pairs={{0,8},{1,9},{2,10},{3,11},{4,12},{5,13},{6,14},{7,15},{8,0},{9,1},... | collective-permute-start | bytes 1277960 | tf_op jit(solution)/shard_map/ppermute | solution.py:818
  163.9 20.8 %collective-permute-start.32 = (bf16[1664,128]{1,0:T(8,128)(2,1)S(1)}, bf16[1664,128]{1,0:T(8,128)(2,1)S(1)}, u32[]{:S(2)}, u32[]{:S(2)}) collective-permute-start(bf16[1664,128]{1,0:T(8,128)(2,1)S(1)} %get-tuple-element.150), channel_id=1, source_target_pairs={{0,16},{1,17},{2,18},{3,19},{4,20},{5,21},{6,22},{7,23},{8,24},{9,... | collective-permute-start | bytes 1277960 | tf_op jit(solution)/shard_map/ppermute | solution.py:818
  164.6 20.1 %collective-permute-start.33 = (bf16[1664,128]{1,0:T(8,128)(2,1)S(1)}, bf16[1664,128]{1,0:T(8,128)(2,1)S(1)}, u32[]{:S(2)}, u32[]{:S(2)}) collective-permute-start(bf16[1664,128]{1,0:T(8,128)(2,1)S(1)} %get-tuple-element.151), channel_id=1, source_target_pairs={{0,24},{1,25},{2,26},{3,27},{4,28},{5,29},{6,30},{7,31},{8,16},{9,... | collective-permute-start | bytes 1277960 | tf_op jit(solution)/shard_map/ppermute | solution.py:818
  166.7 18.0 %collective-permute-start.35 = (bf16[832,128]{1,0:T(8,128)(2,1)S(1)}, bf16[832,128]{1,0:T(8,128)(2,1)S(1)}, u32[]{:S(2)}, u32[]{:S(2)}) collective-permute-start(bf16[832,128]{1,0:T(8,128)(2,1)S(1)} %get-tuple-element.154), channel_id=1, source_target_pairs={{0,4},{1,5},{2,6},{3,7},{4,0},{5,1},{6,2},{7,3},{8,12},{9,13},{10,... | collective-permute-start | bytes 638984 | tf_op jit(solution)/shard_map/ppermute | solution.py:818
  171.6 13.1 %collective-permute-start.36 = (bf16[832,128]{1,0:T(8,128)(2,1)S(1)}, bf16[832,128]{1,0:T(8,128)(2,1)S(1)}, u32[]{:S(2)}, u32[]{:S(2)}) collective-permute-start(bf16[832,128]{1,0:T(8,128)(2,1)S(1)} %get-tuple-element.155), channel_id=1, source_target_pairs={{0,6},{1,7},{2,4},{3,5},{4,2},{5,3},{6,0},{7,1},{8,14},{9,15},{10,... | collective-permute-start | bytes 638984 | tf_op jit(solution)/shard_map/ppermute | solution.py:818
  186.0 16.7 %collective-permute-start.38 = (bf16[864,128]{1,0:T(8,128)(2,1)S(1)}, bf16[864,128]{1,0:T(8,128)(2,1)S(1)}, u32[]{:S(2)}, u32[]{:S(2)}) collective-permute-start(bf16[864,128]{1,0:T(8,128)(2,1)S(1)} %get-tuple-element.165), channel_id=1, source_target_pairs={{0,2},{1,3},{2,0},{3,1},{4,6},{5,7},{6,4},{7,5},{8,10},{9,11},{10,... | collective-permute-start | bytes 663560 | tf_op jit(solution)/shard_map/ppermute | solution.py:818
  189.7 18.6 %collective-permute-start.39 = (bf16[864,128]{1,0:T(8,128)(2,1)S(1)}, bf16[864,128]{1,0:T(8,128)(2,1)S(1)}, u32[]{:S(2)}, u32[]{:S(2)}) collective-permute-start(bf16[864,128]{1,0:T(8,128)(2,1)S(1)} %get-tuple-element.166), channel_id=1, source_target_pairs={{0,4},{1,5},{2,6},{3,7},{4,0},{5,1},{6,2},{7,3},{8,12},{9,13},{10,... | collective-permute-start | bytes 663560 | tf_op jit(solution)/shard_map/ppermute | solution.py:818
  191.0 17.3 %collective-permute-start.40 = (bf16[864,128]{1,0:T(8,128)(2,1)S(1)}, bf16[864,128]{1,0:T(8,128)(2,1)S(1)}, u32[]{:S(2)}, u32[]{:S(2)}) collective-permute-start(bf16[864,128]{1,0:T(8,128)(2,1)S(1)} %get-tuple-element.167), channel_id=1, source_target_pairs={{0,6},{1,7},{2,4},{3,5},{4,2},{5,3},{6,0},{7,1},{8,14},{9,15},{10,... | collective-permute-start | bytes 663560 | tf_op jit(solution)/shard_map/ppermute | solution.py:818
  192.3 4.7 %collective-permute-start.41 = (bf16[416,128]{1,0:T(8,128)(2,1)S(1)}, bf16[416,128]{1,0:T(8,128)(2,1)S(1)}, u32[]{:S(2)}, u32[]{:S(2)}) collective-permute-start(bf16[416,128]{1,0:T(8,128)(2,1)S(1)} %get-tuple-element.169), channel_id=1, source_target_pairs={{0,8},{1,9},{2,10},{3,11},{4,12},{5,13},{6,14},{7,15},{8,0},{9,1},... | collective-permute-start | bytes 319496 | tf_op jit(solution)/shard_map/ppermute | solution.py:818
  193.0 4.8 %collective-permute-start.42 = (bf16[416,128]{1,0:T(8,128)(2,1)S(1)}, bf16[416,128]{1,0:T(8,128)(2,1)S(1)}, u32[]{:S(2)}, u32[]{:S(2)}) collective-permute-start(bf16[416,128]{1,0:T(8,128)(2,1)S(1)} %get-tuple-element.170), channel_id=1, source_target_pairs={{0,16},{1,17},{2,18},{3,19},{4,20},{5,21},{6,22},{7,23},{8,24},{9,... | collective-permute-start | bytes 319496 | tf_op jit(solution)/shard_map/ppermute | solution.py:818
  197.0 5.6 %collective-permute-start.43 = (bf16[416,128]{1,0:T(8,128)(2,1)S(1)}, bf16[416,128]{1,0:T(8,128)(2,1)S(1)}, u32[]{:S(2)}, u32[]{:S(2)}) collective-permute-start(bf16[416,128]{1,0:T(8,128)(2,1)S(1)} %get-tuple-element.171), channel_id=1, source_target_pairs={{0,24},{1,25},{2,26},{3,27},{4,28},{5,29},{6,30},{7,31},{8,16},{9,... | collective-permute-start | bytes 319496 | tf_op jit(solution)/shard_map/ppermute | solution.py:818
  210.4 4.5 %collective-permute-start.50 = (f32[8,128]{1,0:T(8,128)S(1)}, f32[8,128]{1,0:T(8,128)S(1)}, u32[]{:S(2)}, u32[]{:S(2)}) collective-permute-start(f32[8,128]{1,0:T(8,128)S(1)} %add.26), channel_id=1, source_target_pairs={{0,24},{1,25},{2,26},{3,27},{4,28},{5,29},{6,30},{7,31},{8,16},{9,... | collective-permute-start | bytes 12296 | tf_op jit(solution)/shard_map/ppermute | solution.py:818
  210.9 5.2 %collective-permute-start.49 = (f32[8,128]{1,0:T(8,128)S(1)}, f32[8,128]{1,0:T(8,128)S(1)}, u32[]{:S(2)}, u32[]{:S(2)}) collective-permute-start(f32[8,128]{1,0:T(8,128)S(1)} %add.26), channel_id=1, source_target_pairs={{0,16},{1,17},{2,18},{3,19},{4,20},{5,21},{6,22},{7,23},{8,24},{9,... | collective-permute-start | bytes 12296 | tf_op jit(solution)/shard_map/ppermute | solution.py:818
  213.9 11.2 %collective-permute-start.44 = (f32[304,128]{1,0:T(8,128)S(1)}, f32[304,128]{1,0:T(8,128)S(1)}, u32[]{:S(2)}, u32[]{:S(2)}) collective-permute-start(f32[304,128]{1,0:T(8,128)S(1)} %get-tuple-element.173), channel_id=1, source_target_pairs={{0,16},{1,17},{2,18},{3,19},{4,20},{5,21},{6,22},{7,23},{8,24},{9,... | collective-permute-start | bytes 466952 | tf_op jit(solution)/shard_map/ppermute | solution.py:818
  214.4 10.7 %collective-permute-start.45 = (f32[304,128]{1,0:T(8,128)S(1)}, f32[304,128]{1,0:T(8,128)S(1)}, u32[]{:S(2)}, u32[]{:S(2)}) collective-permute-start(f32[304,128]{1,0:T(8,128)S(1)} %get-tuple-element.174), channel_id=1, source_target_pairs={{0,1},{1,0},{2,3},{3,2},{4,5},{5,4},{6,7},{7,6},{8,9},{9,8},{10,11... | collective-permute-start | bytes 466952 | tf_op jit(solution)/shard_map/ppermute | solution.py:818
  214.9 10.2 %collective-permute-start.46 = (f32[304,128]{1,0:T(8,128)S(1)}, f32[304,128]{1,0:T(8,128)S(1)}, u32[]{:S(2)}, u32[]{:S(2)}) collective-permute-start(f32[304,128]{1,0:T(8,128)S(1)} %get-tuple-element.175), channel_id=1, source_target_pairs={{0,17},{1,16},{2,19},{3,18},{4,21},{5,20},{6,23},{7,22},{8,25},{9,... | collective-permute-start | bytes 466952 | tf_op jit(solution)/shard_map/ppermute | solution.py:818
  216.1 5.5 %collective-permute-start.53 = (f32[8,128]{1,0:T(8,128)S(1)}, f32[8,128]{1,0:T(8,128)S(1)}, u32[]{:S(2)}, u32[]{:S(2)}) collective-permute-start(f32[8,128]{1,0:T(8,128)S(1)} %add_add_fusion.q0), channel_id=1, source_target_pairs={{0,6},{1,7},{2,4},{3,5},{4,2},{5,3},{6,0},{7,1},{8,14},{9,15},{10,... | collective-permute-start | bytes 12296 | tf_op jit(solution)/shard_map/ppermute | solution.py:818
  218.1 4.6 %collective-permute-start.52 = (f32[8,128]{1,0:T(8,128)S(1)}, f32[8,128]{1,0:T(8,128)S(1)}, u32[]{:S(2)}, u32[]{:S(2)}) collective-permute-start(f32[8,128]{1,0:T(8,128)S(1)} %add_add_fusion.q0), channel_id=1, source_target_pairs={{0,4},{1,5},{2,6},{3,7},{4,0},{5,1},{6,2},{7,3},{8,12},{9,13},{10,... | collective-permute-start | bytes 12296 | tf_op jit(solution)/shard_map/ppermute | solution.py:818
  (28 other events, 633.0 us)

commit v3 on v2

--- a/solution.py
+++ b/solution.py
@@ -220,22 +220,17 @@
 
     left_lanes = lax.broadcasted_iota(jnp.int32, (short_len, 2 * HEAD), 1) < HEAD
 
-    def slot_step(index, carry):
-        slot, lower = index // 2, index % 2
+    def slot_step(slot, carry):
         at = rows_of(slot, short_len)
-
-        @pl.when(lower == 0)
-        def _():
-            attention_bias(lay_ref[slot], short_len, dist_ref, mask_ref)
-
-        for pair in range(HEADS // 4):
-            lanes, lanes_k, lanes_v = (pair_lanes(part, lower, pair) for part in range(3))
+        attention_bias(lay_ref[slot], short_len, dist_ref, mask_ref)
+        for pair in range(HEADS // 2):
+            lanes, lanes_k, lanes_v = (pair_lanes(part, pair) for part in range(3))
             queries = qkv_ref[at, lanes] * jnp.asarray(0.125, BF16)
             keys, values = qkv_ref[at, lanes_k], qkv_ref[at, lanes_v]
             mixed = jnp.zeros((short_len, 2 * HEAD), F32)
             for side in range(2):
-                head = lower * (HEADS // 2) + pair * 2 + side
-                slope = head_slope(lower, pair * 2 + side)
+                head = pair * 2 + side
+                slope = 2.0 ** (-8.0 * (head + 1.0) / HEADS)
                 scores = nt(one_side(left_lanes, side, keys), queries)
                 scores = scores + jnp.minimum(dist_ref[...] * slope, mask_ref[...])
                 top = jnp.max(scores, 0, keepdims=True)
@@ -247,18 +242,14 @@
             mixed_ref[at, lanes] = mixed.astype(BF16)
         return carry
 
-    lax.fori_loop(0, 2 * slots, slot_step, 0)
+    lax.fori_loop(0, slots, slot_step, 0)
     resid_ref[...] = short_ref[...] + nn(mixed_ref[...], w_ref[ROW_O:ROW_F1, :])
     if pieces > 1:
         leave.wait()
 
 
-def head_slope(lower, head):
-    return jnp.where(lower == 0, *(2.0 ** (-8.0 * (head + more + 1.0) / HEADS) for more in (0, HEADS // 2)))
-
-
-def pair_lanes(part, lower, pair):
-    return pl.ds(pl.multiple_of(part * D + lower * (D // 2) + pair * 2 * HEAD, 2 * HEAD), 2 * HEAD)
+def pair_lanes(part, pair):
+    return slice(part * D + pair * 2 * HEAD, part * D + (pair + 1) * 2 * HEAD)
 
 
 def one_side(left_lanes, side, array):
@@ -429,23 +420,18 @@
 
     left_lanes = lax.broadcasted_iota(jnp.int32, (short_len, 2 * HEAD), 1) < HEAD
 
-    def slot_step(index, carry):
-        slot, lower = index // 2, index % 2
+    def slot_step(slot, carry):
         at = rows_of(slot, short_len)
-
-        @pl.when(lower == 0)
-        def _():
-            attention_bias(lay_ref[slot], short_len, dist_ref, mask_ref)
-
-        for pair in range(HEADS // 4):
-            lanes, lanes_k, lanes_v = (pair_lanes(part, lower, pair) for part in range(3))
+        attention_bias(lay_ref[slot], short_len, dist_ref, mask_ref)
+        for pair in range(HEADS // 2):
+            lanes, lanes_k, lanes_v = (pair_lanes(part, pair) for part in range(3))
             queries, keys, values = qkv_ref[at, lanes], qkv_ref[at, lanes_k], qkv_ref[at, lanes_v]
             dmix = dmix_ref[at, lanes]
             scaled = queries * jnp.asarray(0.125, BF16)
             dqueries, dkeys, dvalues = (jnp.zeros((short_len, 2 * HEAD), F32) for _ in range(3))
             for side in range(2):
-                head = lower * (HEADS // 2) + pair * 2 + side
-                slope = head_slope(lower, pair * 2 + side)
+                head = pair * 2 + side
+                slope = 2.0 ** (-8.0 * (head + 1.0) / HEADS)
                 keys_here = one_side(left_lanes, side, keys)
                 scores = nt(keys_here, scaled)
                 scores = scores + jnp.minimum(dist_ref[...] * slope, mask_ref[...])
@@ -461,7 +447,7 @@
             dqkv_ref[at, lanes_v] = dvalues.astype(BF16)
         return carry
 
-    lax.fori_loop(0, 2 * lse_ref.shape[0], slot_step, 0)
+    lax.fori_loop(0, lse_ref.shape[0], slot_step, 0)
     split_store(keep_ref, send_ref, core, pl.ds(ROW_O, D), tn(mixed_ref[...], dbranch_ref[...]))
 
     def dproj_step(part, carry):

time: 228 us -> 227 us (level)
  no operation moved by 1% of the time
where the time goes in v3:
time: 227 us; the launch traced here: 226 us
  waiting for transfers between devices  86.8 us (38%)
  Pallas kernels  74.9 us (33%)
  starting transfers between devices  59.9 us (26%)
    ppermute x54, waiting for transfers between devices, swap_with(): return lax.ppermute(array, AXES, pairs)  86.8 us
    ppermute x54, starting transfers between devices, swap_with(): return lax.ppermute(array, AXES, pairs)  59.9 us
    pallas_call x1, Pallas kernels, device_grads(): pl.pallas_call(partial(deep_kernel, count), out_shape=(shape((ROW_HALF -...  31.4 us
    pallas_call x1, Pallas kernels, device_grads(): pl.pallas_call(partial(back_kernel, short_len), out_shape=(shape((ROW_F1,...  19.9 us
    pallas_call x1, Pallas kernels, device_grads(): pl.pallas_call(partial(attend_kernel, short_len, slots, number), out_shap...  16 us
  transfers between devices with their start and end apart: 54, of which 23 were waited for; matrix products, arithmetic and copies ran while one was open for 0% of the time, Pallas kernels for 10%

profile of v3, /device:TPU:0, one launch (start us, length us, event | category | flops | bytes accessed | tf_op | source)
XLA Modules:
  0.0 226.5 jit_solution(5076734446025049954)
XLA Ops:
  1.4 1.1 convert_element_type.8
  2.6 4.1 %collective-permute-start = (bf16[241,512]{1,0:T(8,128)(2,1)S(1)}, bf16[241,512]{1,0:T(8,128)(2,1)S(1)}, u32[]{:S(2)}, u32[]{:S(2)}) collective-permute-start(bf16[241,512]{1,0:T(8,128)(2,1)S(1)} %pad_maximum_fusion.1), channel_id=1, source_target_pairs={{0,4},{1,5},{2,6},{3,7},{4,0},{5,1},{6,2},{7,3},{8,12},{9,13},{10,... | collective-permute-start | bytes 740360 | tf_op jit(solution)/shard_map/ppermute | solution.py:804
  6.7 2.5 %collective-permute-start.3 = (bf16[64,512]{1,0:T(8,128)(2,1)S(1)}, bf16[64,512]{1,0:T(8,128)(2,1)S(1)}, u32[]{:S(2)}, u32[]{:S(2)}) collective-permute-start(bf16[64,512]{1,0:T(8,128)(2,1)S(1)} %slice.19), channel_id=1, source_target_pairs={{0,24},{1,25},{2,26},{3,27},{4,28},{5,29},{6,30},{7,31},{8,16},{9,... | collective-permute-start | bytes 196616 | tf_op jit(solution)/shard_map/ppermute | solution.py:804
  10.3 1.8 collective-permute-done.3
  12.1 1.4 collective-permute-done.2
  14.0 4.3 %collective-permute-done = bf16[241,512]{1,0:T(8,128)(2,1)S(1)} collective-permute-done((bf16[241,512]{1,0:T(8,128)(2,1)S(1)}, bf16[241,512]{1,0:T(8,128)(2,1)S(1)}, u32[]{:S(2)}, u32[]{:S(2)}) %collective-permute-start) | collective-permute-done | bytes 246816 | tf_op jit(solution)/shard_map/ppermute | solution.py:804
  18.7 1.6 collective-permute-start.6
  20.3 1.5 collective-permute-start.5
  22.5 9.0 %collective-permute-done.6.refs_2_ = bf16[496,512]{1,0:T(8,128)(2,1)S(1)} collective-permute-done((bf16[496,512]{1,0:T(8,128)(2,1)S(1)}, bf16[496,512]{1,0:T(8,128)(2,1)S(1)}, u32[]{:S(2)}, u32[]{:S(2)}) %collective-permute-start.6) | collective-permute-done | bytes 507936 | tf_op jit(solution)/shard_map/ppermute | solution.py:804
  32.5 1.2 collective-permute-done.4.refs_4_
  35.0 3.1 %collective-permute-start.10 = (bf16[256,512]{1,0:T(8,128)(2,1)S(1)}, bf16[256,512]{1,0:T(8,128)(2,1)S(1)}, u32[]{:S(2)}, u32[]{:S(2)}) collective-permute-start(bf16[256,512]{1,0:T(8,128)(2,1)S(1)} %pad_maximum_fusion), channel_id=1, source_target_pairs={{0,4},{1,5},{2,6},{3,7},{4,0},{5,1},{6,2},{7,3},{8,12},{9,13},{10,... | collective-permute-start | bytes 786440 | tf_op jit(solution)/shard_map/ppermute | solution.py:804
  38.1 1.5 collective-permute-start.7
  39.6 8.8 %collective-permute-done.10 = bf16[256,512]{1,0:T(8,128)(2,1)S(1)} collective-permute-done((bf16[256,512]{1,0:T(8,128)(2,1)S(1)}, bf16[256,512]{1,0:T(8,128)(2,1)S(1)}, u32[]{:S(2)}, u32[]{:S(2)}) %collective-permute-start.10) | collective-permute-done | bytes 262176 | tf_op jit(solution)/shard_map/ppermute | solution.py:804
  48.6 1.6 collective-permute-start.12
  50.7 5.2 %collective-permute-done.7.refs_3_ = bf16[496,512]{1,0:T(8,128)(2,1)S(1)} collective-permute-done((bf16[496,512]{1,0:T(8,128)(2,1)S(1)}, bf16[496,512]{1,0:T(8,128)(2,1)S(1)}, u32[]{:S(2)}, u32[]{:S(2)}) %collective-permute-start.7) | collective-permute-done | bytes 507936 | tf_op jit(solution)/shard_map/ppermute | solution.py:804
  56.6 6.3 %collective-permute-done.12.refs_9_ = bf16[512,512]{1,0:T(8,128)(2,1)S(1)} collective-permute-done((bf16[512,512]{1,0:T(8,128)(2,1)S(1)}, bf16[512,512]{1,0:T(8,128)(2,1)S(1)}, u32[]{:S(2)}, u32[]{:S(2)}) %collective-permute-start.12) | collective-permute-done | bytes 524320 | tf_op jit(solution)/shard_map/ppermute | solution.py:804
  63.7 6.5 %collective-permute-done.11.refs_7_ = bf16[496,512]{1,0:T(8,128)(2,1)} collective-permute-done((bf16[496,512]{1,0:T(8,128)(2,1)}, bf16[496,512]{1,0:T(8,128)(2,1)}, u32[]{:S(2)}, u32[]{:S(2)}) %collective-permute-start.11) | collective-permute-done | bytes 507936 | tf_op jit(solution)/shard_map/ppermute | solution.py:804
  70.8 1.6 collective-permute-done.20.refs_17_
  73.2 16.0 %attend.1 = (bf16[9728,512]{1,0:T(8,128)(2,1)}, bf16[768,1536]{1,0:T(8,128)(2,1)S(1)}, f32[768,512]{1,0:T(8,128)S(1)}, bf16[768,512]{1,0:T(8,128)(2,1)S(1)}, bf1...) custom-call(s32[4]{0:T(128)S(1)} %pad_add_fusion.coords_ref, ...), custom_call_target="tpu_custom_call" | custom-call | flops 8999999488 | bytes 20000000 | tf_op jit(solution)/shard_map/attend/pallas_call | solution.py:669
  89.2 31.4 %deep.1 = (bf16[1024,256]{1,0:T(8,128)(2,1)S(1)}, bf16[1024,256]{1,0:T(8,128)(2,1)S(1)}, bf16[4864,256]{1,0:T(8,128)(2,1)S(1)}, bf16[4864,256]{1,0:T(8,128)(2,1)...) custom-call(s32[4]{0:T(128)S(1)} %pad_add_fusion.coords_ref, ...), custom_call_target="tpu_custom_call" | custom-call | tf_op jit(solution)/shard_map/deep/pallas_call | solution.py:687
  121.1 4.2 %collective-permute-done.23.recv_ref = bf16[4864,256]{1,0:T(8,128)(2,1)S(1)} collective-permute-done((bf16[4864,256]{1,0:T(8,128)(2,1)S(1)}, bf16[4864,256]{1,0:T(8,128)(2,1)S(1)}, u32[]{:S(2)}, u32[]{:S(2)}) %collective-permute-start.23) | collective-permute-done | bytes 2490400 | tf_op jit(solution)/shard_map/ppermute | solution.py:804
  125.3 1.2 core_sum.1
  126.6 4.5 %collective-permute-start.28 = (bf16[832,128]{1,0:T(8,128)(2,1)S(1)}, bf16[832,128]{1,0:T(8,128)(2,1)S(1)}, u32[]{:S(2)}, u32[]{:S(2)}) collective-permute-start(bf16[832,128]{1,0:T(8,128)(2,1)S(1)} %get-tuple-element.129), channel_id=1, source_target_pairs={{0,4},{1,5},{2,6},{3,7},{4,0},{5,1},{6,2},{7,3},{8,12},{9,13},{10,... | collective-permute-start | bytes 638984 | tf_op jit(solution)/shard_map/ppermute | solution.py:804
  133.3 2.2 collective-permute-start.27
  135.5 19.9 %back.1 = (bf16[3840,256]{1,0:T(8,128)(2,1)S(1)}, bf16[3872,256]{1,0:T(8,128)(2,1)S(1)}, f32[8,512]{1,0:T(8,128)S(1)}) custom-call(s32[4]{0:T(128)S(1)} %pad_add_fusion.coords_ref, s32[2]{0:T(128)S(1)} %bitcast.11, f32[8,512]{1,0:T(8,128)S(1)} %get-tuple-element.107.vec_ref, f32[8,512]{1,0:T(8,128)S(1)} %get-tuple-element.131.deep_small_ref, ...), custom_call_target="tpu_custom_call" | custom-call | flops 19000000512 | bytes 20000000 | tf_op jit(solution)/shard_map/back/pallas_call | solution.py:723
  156.1 3.4 %collective-permute-done.30.recv_front = bf16[3872,256]{1,0:T(8,128)(2,1)S(1)} collective-permute-done((bf16[3872,256]{1,0:T(8,128)(2,1)S(1)}, bf16[3872,256]{1,0:T(8,128)(2,1)S(1)}, u32[]{:S(2)}, u32[]{:S(2)}) %collective-permute-start.30) | collective-permute-done | bytes 1982496 | tf_op jit(solution)/shard_map/ppermute | solution.py:804
  159.5 1.9 core_sum_front.1
  163.3 2.2 collective-permute-start.33
  165.5 3.0 %collective-permute-start.35 = (bf16[832,128]{1,0:T(8,128)(2,1)S(1)}, bf16[832,128]{1,0:T(8,128)(2,1)S(1)}, u32[]{:S(2)}, u32[]{:S(2)}) collective-permute-start(bf16[832,128]{1,0:T(8,128)(2,1)S(1)} %get-tuple-element.154), channel_id=1, source_target_pairs={{0,4},{1,5},{2,6},{3,7},{4,0},{5,1},{6,2},{7,3},{8,12},{9,13},{10,... | collective-permute-start | bytes 638984 | tf_op jit(solution)/shard_map/ppermute | solution.py:804
  168.4 1.8 collective-permute-done.34.refs_5_
  170.3 2.5 %collective-permute-start.36 = (bf16[832,128]{1,0:T(8,128)(2,1)S(1)}, bf16[832,128]{1,0:T(8,128)(2,1)S(1)}, u32[]{:S(2)}, u32[]{:S(2)}) collective-permute-start(bf16[832,128]{1,0:T(8,128)(2,1)S(1)} %get-tuple-element.155), channel_id=1, source_target_pairs={{0,6},{1,7},{2,4},{3,5},{4,2},{5,3},{6,0},{7,1},{8,14},{9,15},{10,... | collective-permute-start | bytes 638984 | tf_op jit(solution)/shard_map/ppermute | solution.py:804
  172.7 10.7 %collective-permute-done.35.refs_6_ = bf16[832,128]{1,0:T(8,128)(2,1)S(1)} collective-permute-done((bf16[832,128]{1,0:T(8,128)(2,1)S(1)}, bf16[832,128]{1,0:T(8,128)(2,1)S(1)}, u32[]{:S(2)}, u32[]{:S(2)}) %collective-permute-start.35) | collective-permute-done | bytes 213024 | tf_op jit(solution)/shard_map/ppermute | solution.py:804
  183.5 1.2 first_sum.1
  184.7 3.8 %collective-permute-start.38 = (bf16[864,128]{1,0:T(8,128)(2,1)S(1)}, bf16[864,128]{1,0:T(8,128)(2,1)S(1)}, u32[]{:S(2)}, u32[]{:S(2)}) collective-permute-start(bf16[864,128]{1,0:T(8,128)(2,1)S(1)} %get-tuple-element.165), channel_id=1, source_target_pairs={{0,2},{1,3},{2,0},{3,1},{4,6},{5,7},{6,4},{7,5},{8,10},{9,11},{10,... | collective-permute-start | bytes 663560 | tf_op jit(solution)/shard_map/ppermute | solution.py:804
  188.5 1.2 collective-permute-start.39
  189.7 1.4 collective-permute-start.40
  192.4 3.4 %collective-permute-done.41.refs_5_ = bf16[416,128]{1,0:T(8,128)(2,1)S(1)} collective-permute-done((bf16[416,128]{1,0:T(8,128)(2,1)S(1)}, bf16[416,128]{1,0:T(8,128)(2,1)S(1)}, u32[]{:S(2)}, u32[]{:S(2)}) %collective-permute-start.41) | collective-permute-done | bytes 106528 | tf_op jit(solution)/shard_map/ppermute | solution.py:804
  196.5 4.8 %collective-permute-done.43.refs_7_ = bf16[416,128]{1,0:T(8,128)(2,1)S(1)} collective-permute-done((bf16[416,128]{1,0:T(8,128)(2,1)S(1)}, bf16[416,128]{1,0:T(8,128)(2,1)S(1)}, u32[]{:S(2)}, u32[]{:S(2)}) %collective-permute-start.43) | collective-permute-done | bytes 106528 | tf_op jit(solution)/shard_map/ppermute | solution.py:804
  201.4 5.7 %collective-permute-done.39.refs_2_ = bf16[864,128]{1,0:T(8,128)(2,1)S(1)} collective-permute-done((bf16[864,128]{1,0:T(8,128)(2,1)S(1)}, bf16[864,128]{1,0:T(8,128)(2,1)S(1)}, u32[]{:S(2)}, u32[]{:S(2)}) %collective-permute-start.39) | collective-permute-done | bytes 221216 | tf_op jit(solution)/shard_map/ppermute | solution.py:804
  208.0 1.2 collective-permute-done.47
  209.7 1.4 collective-permute-start.49
  211.1 1.6 collective-permute-start.48
  213.7 1.2 collective-permute-start.46
  214.9 2.0 collective-permute-start.53
  216.9 2.5 %collective-permute-start.52 = (f32[8,128]{1,0:T(8,128)S(1)}, f32[8,128]{1,0:T(8,128)S(1)}, u32[]{:S(2)}, u32[]{:S(2)}) collective-permute-start(f32[8,128]{1,0:T(8,128)S(1)} %add_add_fusion.q0), channel_id=1, source_target_pairs={{0,4},{1,5},{2,6},{3,7},{4,0},{5,1},{6,2},{7,3},{8,12},{9,13},{10,... | collective-permute-start | bytes 12296 | tf_op jit(solution)/shard_map/ppermute | solution.py:804
  220.3 1.1 collective-permute-start.51
  221.5 2.5 %collective-permute-done.51.q1 = f32[8,128]{1,0:T(8,128)S(1)} collective-permute-done((f32[8,128]{1,0:T(8,128)S(1)}, f32[8,128]{1,0:T(8,128)S(1)}, u32[]{:S(2)}, u32[]{:S(2)}) %collective-permute-start.51) | collective-permute-done | bytes 4128 | tf_op jit(solution)/shard_map/ppermute | solution.py:804
  224.0 2.5 %update.1 = (f32[1,1]{1,0:T(1,128)}, f32[1,1]{1,0:T(1,128)}, f32[304,512]{1,0:T(8,128)}, f32[304,512]{1,0:T(8,128)}, f32[304,512]{1,0:T(8,128)}, /*index=5*/f32[...) custom-call(s32[4]{0:T(128)S(1)} %pad_add_fusion.coords_ref, f32[304,128]{1,0:T(8,128)S(1)} %get-tuple-element.172.g0, ...), custom_call_target="tpu_custom_call" | custom-call | tf_op jit(solution)/shard_map/update/pallas_call | solution.py:883
  (133 shorter events, 20.0 us)
Async XLA Ops:
  2.6 15.7 %collective-permute-start = (bf16[241,512]{1,0:T(8,128)(2,1)S(1)}, bf16[241,512]{1,0:T(8,128)(2,1)S(1)}, u32[]{:S(2)}, u32[]{:S(2)}) collective-permute-start(bf16[241,512]{1,0:T(8,128)(2,1)S(1)} %pad_maximum_fusion.1), channel_id=1, source_target_pairs={{0,4},{1,5},{2,6},{3,7},{4,0},{5,1},{6,2},{7,3},{8,12},{9,13},{10,... | collective-permute-start | bytes 740360 | tf_op jit(solution)/shard_map/ppermute | solution.py:804
  6.7 5.3 %collective-permute-start.3 = (bf16[64,512]{1,0:T(8,128)(2,1)S(1)}, bf16[64,512]{1,0:T(8,128)(2,1)S(1)}, u32[]{:S(2)}, u32[]{:S(2)}) collective-permute-start(bf16[64,512]{1,0:T(8,128)(2,1)S(1)} %slice.19), channel_id=1, source_target_pairs={{0,24},{1,25},{2,26},{3,27},{4,28},{5,29},{6,30},{7,31},{8,16},{9,... | collective-permute-start | bytes 196616 | tf_op jit(solution)/shard_map/ppermute | solution.py:804
  9.2 4.3 %collective-permute-start.2 = (bf16[64,512]{1,0:T(8,128)(2,1)S(1)}, bf16[64,512]{1,0:T(8,128)(2,1)S(1)}, u32[]{:S(2)}, u32[]{:S(2)}) collective-permute-start(bf16[64,512]{1,0:T(8,128)(2,1)S(1)} %slice.19), channel_id=1, source_target_pairs={{0,16},{1,17},{2,18},{3,19},{4,20},{5,21},{6,22},{7,23},{8,24},{9,... | collective-permute-start | bytes 196616 | tf_op jit(solution)/shard_map/ppermute | solution.py:804
  18.7 12.8 %collective-permute-start.6 = (bf16[496,512]{1,0:T(8,128)(2,1)S(1)}, bf16[496,512]{1,0:T(8,128)(2,1)S(1)}, u32[]{:S(2)}, u32[]{:S(2)}) collective-permute-start(bf16[496,512]{1,0:T(8,128)(2,1)S(1)} %concatenate.13.refs_0_), channel_id=1, source_target_pairs={{0,16},{1,17},{2,18},{3,19},{4,20},{5,21},{6,22},{7,23},{8,24},{9,... | collective-permute-start | bytes 1523720 | tf_op jit(solution)/shard_map/ppermute | solution.py:804
  20.3 12.2 %collective-permute-start.5 = (bf16[496,512]{1,0:T(8,128)(2,1)S(1)}, bf16[496,512]{1,0:T(8,128)(2,1)S(1)}, u32[]{:S(2)}, u32[]{:S(2)}) collective-permute-start(bf16[496,512]{1,0:T(8,128)(2,1)S(1)} %concatenate.13.refs_0_), channel_id=1, source_target_pairs={{0,8},{1,9},{2,10},{3,11},{4,12},{5,13},{6,14},{7,15},{8,0},{9,1},... | collective-permute-start | bytes 1523720 | tf_op jit(solution)/shard_map/ppermute | solution.py:804
  21.8 11.9 %collective-permute-start.4 = (bf16[496,512]{1,0:T(8,128)(2,1)S(1)}, bf16[496,512]{1,0:T(8,128)(2,1)S(1)}, u32[]{:S(2)}, u32[]{:S(2)}) collective-permute-start(bf16[496,512]{1,0:T(8,128)(2,1)S(1)} %concatenate.13.refs_0_), channel_id=1, source_target_pairs={{0,2},{1,3},{2,0},{3,1},{4,6},{5,7},{6,4},{7,5},{8,10},{9,11},{10,... | collective-permute-start | bytes 1523720 | tf_op jit(solution)/shard_map/ppermute | solution.py:804
  33.7 14.8 %collective-permute-start.9 = (bf16[496,512]{1,0:T(8,128)(2,1)S(1)}, bf16[496,512]{1,0:T(8,128)(2,1)}, u32[]{:S(2)}, u32[]{:S(2)}) collective-permute-start(bf16[496,512]{1,0:T(8,128)(2,1)S(1)} %collective-permute-done.4.refs_4_), channel_id=1, source_target_pairs={{0,16},{1,17},{2,18},{3,19},{4,20},{5,21},{6,22},{7,23},{8,24},{9,... | collective-permute-start | bytes 1523720 | tf_op jit(solution)/shard_map/ppermute | solution.py:804
  34.2 14.3 %collective-permute-start.8 = (bf16[496,512]{1,0:T(8,128)(2,1)S(1)}, bf16[496,512]{1,0:T(8,128)(2,1)}, u32[]{:S(2)}, u32[]{:S(2)}) collective-permute-start(bf16[496,512]{1,0:T(8,128)(2,1)S(1)} %collective-permute-done.4.refs_4_), channel_id=1, source_target_pairs={{0,8},{1,9},{2,10},{3,11},{4,12},{5,13},{6,14},{7,15},{8,0},{9,1},... | collective-permute-start | bytes 1523720 | tf_op jit(solution)/shard_map/ppermute | solution.py:804
  35.0 13.5 %collective-permute-start.10 = (bf16[256,512]{1,0:T(8,128)(2,1)S(1)}, bf16[256,512]{1,0:T(8,128)(2,1)S(1)}, u32[]{:S(2)}, u32[]{:S(2)}) collective-permute-start(bf16[256,512]{1,0:T(8,128)(2,1)S(1)} %pad_maximum_fusion), channel_id=1, source_target_pairs={{0,4},{1,5},{2,6},{3,7},{4,0},{5,1},{6,2},{7,3},{8,12},{9,13},{10,... | collective-permute-start | bytes 786440 | tf_op jit(solution)/shard_map/ppermute | solution.py:804
  38.1 12.1 %collective-permute-start.13 = (bf16[496,512]{1,0:T(8,128)(2,1)S(1)}, bf16[496,512]{1,0:T(8,128)(2,1)S(1)}, u32[]{:S(2)}, u32[]{:S(2)}) collective-permute-start(bf16[496,512]{1,0:T(8,128)(2,1)S(1)} %concatenate.13.refs_0_), channel_id=1, source_target_pairs={{0,1},{1,0},{2,3},{3,2},{4,5},{5,4},{6,7},{7,6},{8,9},{9,8},{10,11... | collective-permute-start | bytes 1523720 | tf_op jit(solution)/shard_map/ppermute | solution.py:804
  38.1 17.7 %collective-permute-start.7 = (bf16[496,512]{1,0:T(8,128)(2,1)S(1)}, bf16[496,512]{1,0:T(8,128)(2,1)S(1)}, u32[]{:S(2)}, u32[]{:S(2)}) collective-permute-start(bf16[496,512]{1,0:T(8,128)(2,1)S(1)} %collective-permute-done.5.refs_1_), channel_id=1, source_target_pairs={{0,16},{1,17},{2,18},{3,19},{4,20},{5,21},{6,22},{7,23},{8,24},{9,... | collective-permute-start | bytes 1523720 | tf_op jit(solution)/shard_map/ppermute | solution.py:804
  48.5 7.4 %collective-permute-start.15 = (bf16[496,512]{1,0:T(8,128)(2,1)S(1)}, bf16[496,512]{1,0:T(8,128)(2,1)S(1)}, u32[]{:S(2)}, u32[]{:S(2)}) collective-permute-start(bf16[496,512]{1,0:T(8,128)(2,1)S(1)} %collective-permute-done.6.refs_2_), channel_id=1, source_target_pairs={{0,1},{1,0},{2,3},{3,2},{4,5},{5,4},{6,7},{7,6},{8,9},{9,8},{10,11... | collective-permute-start | bytes 1523720 | tf_op jit(solution)/shard_map/ppermute | solution.py:804
  48.6 14.4 %collective-permute-start.12 = (bf16[512,512]{1,0:T(8,128)(2,1)S(1)}, bf16[512,512]{1,0:T(8,128)(2,1)S(1)}, u32[]{:S(2)}, u32[]{:S(2)}) collective-permute-start(bf16[512,512]{1,0:T(8,128)(2,1)S(1)} %constant_dynamic-update-slice_fusion.refs_8_), channel_id=1, source_target_pairs={{0,2},{1,3},{2,0},{3,1},{4,6},{5,7},{6,4},{7,5},{8,10},{9,11},{10,... | collective-permute-start | bytes 1572872 | tf_op jit(solution)/shard_map/ppermute | solution.py:804
  50.2 6.3 %collective-permute-start.14 = (bf16[496,512]{1,0:T(8,128)(2,1)S(1)}, bf16[496,512]{1,0:T(8,128)(2,1)S(1)}, u32[]{:S(2)}, u32[]{:S(2)}) collective-permute-start(bf16[496,512]{1,0:T(8,128)(2,1)S(1)} %collective-permute-done.5.refs_1_), channel_id=1, source_target_pairs={{0,1},{1,0},{2,3},{3,2},{4,5},{5,4},{6,7},{7,6},{8,9},{9,8},{10,11... | collective-permute-start | bytes 1523720 | tf_op jit(solution)/shard_map/ppermute | solution.py:804
  50.2 12.8 %collective-permute-start.17 = (bf16[496,512]{1,0:T(8,128)(2,1)S(1)}, bf16[496,512]{1,0:T(8,128)(2,1)S(1)}, u32[]{:S(2)}, u32[]{:S(2)}) collective-permute-start(bf16[496,512]{1,0:T(8,128)(2,1)S(1)} %collective-permute-done.4.refs_4_), channel_id=1, source_target_pairs={{0,1},{1,0},{2,3},{3,2},{4,5},{5,4},{6,7},{7,6},{8,9},{9,8},{10,11... | collective-permute-start | bytes 1523720 | tf_op jit(solution)/shard_map/ppermute | solution.py:804
  55.8 7.7 %collective-permute-start.16 = (bf16[496,512]{1,0:T(8,128)(2,1)S(1)}, bf16[496,512]{1,0:T(8,128)(2,1)S(1)}, u32[]{:S(2)}, u32[]{:S(2)}) collective-permute-start(bf16[496,512]{1,0:T(8,128)(2,1)S(1)} %collective-permute-done.7.refs_3_), channel_id=1, source_target_pairs={{0,1},{1,0},{2,3},{3,2},{4,5},{5,4},{6,7},{7,6},{8,9},{9,8},{10,11... | collective-permute-start | bytes 1523720 | tf_op jit(solution)/shard_map/ppermute | solution.py:804
  55.9 14.3 %collective-permute-start.11 = (bf16[496,512]{1,0:T(8,128)(2,1)}, bf16[496,512]{1,0:T(8,128)(2,1)}, u32[]{:S(2)}, u32[]{:S(2)}) collective-permute-start(bf16[496,512]{1,0:T(8,128)(2,1)} %collective-permute-done.9.refs_6_), channel_id=1, source_target_pairs={{0,8},{1,9},{2,10},{3,11},{4,12},{5,13},{6,14},{7,15},{8,0},{9,1},... | collective-permute-start | bytes 1523720 | tf_op jit(solution)/shard_map/ppermute | solution.py:804
  56.5 14.3 %collective-permute-start.21 = (bf16[512,512]{1,0:T(8,128)(2,1)S(1)}, bf16[512,512]{1,0:T(8,128)(2,1)S(1)}, u32[]{:S(2)}, u32[]{:S(2)}) collective-permute-start(bf16[512,512]{1,0:T(8,128)(2,1)S(1)} %constant_dynamic-update-slice_fusion.refs_8_), channel_id=1, source_target_pairs={{0,1},{1,0},{2,3},{3,2},{4,5},{5,4},{6,7},{7,6},{8,9},{9,8},{10,11... | collective-permute-start | bytes 1572872 | tf_op jit(solution)/shard_map/ppermute | solution.py:804
  63.0 9.4 %collective-permute-start.22 = (bf16[512,512]{1,0:T(8,128)(2,1)S(1)}, bf16[512,512]{1,0:T(8,128)(2,1)S(1)}, u32[]{:S(2)}, u32[]{:S(2)}) collective-permute-start(bf16[512,512]{1,0:T(8,128)(2,1)S(1)} %collective-permute-done.12.refs_9_), channel_id=1, source_target_pairs={{0,1},{1,0},{2,3},{3,2},{4,5},{5,4},{6,7},{7,6},{8,9},{9,8},{10,11... | collective-permute-start | bytes 1572872 | tf_op jit(solution)/shard_map/ppermute | solution.py:804
  63.0 7.8 %collective-permute-start.18 = (bf16[496,512]{1,0:T(8,128)(2,1)}, bf16[496,512]{1,0:T(8,128)(2,1)}, u32[]{:S(2)}, u32[]{:S(2)}) collective-permute-start(bf16[496,512]{1,0:T(8,128)(2,1)} %collective-permute-done.8.refs_5_), channel_id=1, source_target_pairs={{0,1},{1,0},{2,3},{3,2},{4,5},{5,4},{6,7},{7,6},{8,9},{9,8},{10,11... | collective-permute-start | bytes 1523720 | tf_op jit(solution)/shard_map/ppermute | solution.py:804
  63.6 7.2 %collective-permute-start.19 = (bf16[496,512]{1,0:T(8,128)(2,1)}, bf16[496,512]{1,0:T(8,128)(2,1)}, u32[]{:S(2)}, u32[]{:S(2)}) collective-permute-start(bf16[496,512]{1,0:T(8,128)(2,1)} %collective-permute-done.9.refs_6_), channel_id=1, source_target_pairs={{0,1},{1,0},{2,3},{3,2},{4,5},{5,4},{6,7},{7,6},{8,9},{9,8},{10,11... | collective-permute-start | bytes 1523720 | tf_op jit(solution)/shard_map/ppermute | solution.py:804
  120.5 4.8 %collective-permute-start.23 = (bf16[4864,256]{1,0:T(8,128)(2,1)S(1)}, bf16[4864,256]{1,0:T(8,128)(2,1)S(1)}, u32[]{:S(2)}, u32[]{:S(2)}) collective-permute-start(bf16[4864,256]{1,0:T(8,128)(2,1)S(1)} %get-tuple-element.113), channel_id=1, source_target_pairs={{0,1},{1,0},{2,3},{3,2},{4,5},{5,4},{6,7},{7,6},{8,9},{9,8},{10,11... | collective-permute-start | bytes 7471112 | tf_op jit(solution)/shard_map/ppermute | solution.py:804
  120.7 5.8 %collective-permute-start.24 = (bf16[1024,256]{1,0:T(8,128)(2,1)S(1)}, bf16[1024,256]{1,0:T(8,128)(2,1)S(1)}, u32[]{:S(2)}, u32[]{:S(2)}) collective-permute-start(bf16[1024,256]{1,0:T(8,128)(2,1)S(1)} %get-tuple-element.122), channel_id=1, source_target_pairs={{0,1},{1,0},{2,3},{3,2},{4,5},{5,4},{6,7},{7,6},{8,9},{9,8},{10,11... | collective-permute-start | bytes 1572872 | tf_op jit(solution)/shard_map/ppermute | solution.py:804
  126.6 28.9 %collective-permute-start.28 = (bf16[832,128]{1,0:T(8,128)(2,1)S(1)}, bf16[832,128]{1,0:T(8,128)(2,1)S(1)}, u32[]{:S(2)}, u32[]{:S(2)}) collective-permute-start(bf16[832,128]{1,0:T(8,128)(2,1)S(1)} %get-tuple-element.129), channel_id=1, source_target_pairs={{0,4},{1,5},{2,6},{3,7},{4,0},{5,1},{6,2},{7,3},{8,12},{9,13},{10,... | collective-permute-start | bytes 638984 | tf_op jit(solution)/shard_map/ppermute | solution.py:804
  131.0 24.4 %collective-permute-start.29 = (bf16[832,128]{1,0:T(8,128)(2,1)S(1)}, bf16[832,128]{1,0:T(8,128)(2,1)S(1)}, u32[]{:S(2)}, u32[]{:S(2)}) collective-permute-start(bf16[832,128]{1,0:T(8,128)(2,1)S(1)} %get-tuple-element.130), channel_id=1, source_target_pairs={{0,6},{1,7},{2,4},{3,5},{4,2},{5,3},{6,0},{7,1},{8,14},{9,15},{10,... | collective-permute-start | bytes 638984 | tf_op jit(solution)/shard_map/ppermute | solution.py:804
  132.0 23.4 %collective-permute-start.25 = (bf16[1600,128]{1,0:T(8,128)(2,1)S(1)}, bf16[1600,128]{1,0:T(8,128)(2,1)S(1)}, u32[]{:S(2)}, u32[]{:S(2)}) collective-permute-start(bf16[1600,128]{1,0:T(8,128)(2,1)S(1)} %get-tuple-element.125), channel_id=1, source_target_pairs={{0,8},{1,9},{2,10},{3,11},{4,12},{5,13},{6,14},{7,15},{8,0},{9,1},... | collective-permute-start | bytes 1228808 | tf_op jit(solution)/shard_map/ppermute | solution.py:804
  132.7 22.8 %collective-permute-start.26 = (bf16[1600,128]{1,0:T(8,128)(2,1)S(1)}, bf16[1600,128]{1,0:T(8,128)(2,1)S(1)}, u32[]{:S(2)}, u32[]{:S(2)}) collective-permute-start(bf16[1600,128]{1,0:T(8,128)(2,1)S(1)} %get-tuple-element.126), channel_id=1, source_target_pairs={{0,16},{1,17},{2,18},{3,19},{4,20},{5,21},{6,22},{7,23},{8,24},{9,... | collective-permute-start | bytes 1228808 | tf_op jit(solution)/shard_map/ppermute | solution.py:804
  133.3 22.1 %collective-permute-start.27 = (bf16[1600,128]{1,0:T(8,128)(2,1)S(1)}, bf16[1600,128]{1,0:T(8,128)(2,1)S(1)}, u32[]{:S(2)}, u32[]{:S(2)}) collective-permute-start(bf16[1600,128]{1,0:T(8,128)(2,1)S(1)} %get-tuple-element.127), channel_id=1, source_target_pairs={{0,24},{1,25},{2,26},{3,27},{4,28},{5,29},{6,30},{7,31},{8,16},{9,... | collective-permute-start | bytes 1228808 | tf_op jit(solution)/shard_map/ppermute | solution.py:804
  155.5 9.9 %collective-permute-start.37 = (bf16[832,128]{1,0:T(8,128)(2,1)S(1)}, bf16[832,128]{1,0:T(8,128)(2,1)S(1)}, u32[]{:S(2)}, u32[]{:S(2)}) collective-permute-start(bf16[832,128]{1,0:T(8,128)(2,1)S(1)} %get-tuple-element.161), channel_id=1, source_target_pairs={{0,2},{1,3},{2,0},{3,1},{4,6},{5,7},{6,4},{7,5},{8,10},{9,11},{10,... | collective-permute-start | bytes 638984 | tf_op jit(solution)/shard_map/ppermute | solution.py:804
  161.4 8.8 %collective-permute-start.34 = (bf16[832,128]{1,0:T(8,128)(2,1)S(1)}, bf16[832,128]{1,0:T(8,128)(2,1)S(1)}, u32[]{:S(2)}, u32[]{:S(2)}) collective-permute-start(bf16[832,128]{1,0:T(8,128)(2,1)S(1)} %get-tuple-element.153), channel_id=1, source_target_pairs={{0,2},{1,3},{2,0},{3,1},{4,6},{5,7},{6,4},{7,5},{8,10},{9,11},{10,... | collective-permute-start | bytes 638984 | tf_op jit(solution)/shard_map/ppermute | solution.py:804
  162.0 21.4 %collective-permute-start.31 = (bf16[1664,128]{1,0:T(8,128)(2,1)S(1)}, bf16[1664,128]{1,0:T(8,128)(2,1)S(1)}, u32[]{:S(2)}, u32[]{:S(2)}) collective-permute-start(bf16[1664,128]{1,0:T(8,128)(2,1)S(1)} %get-tuple-element.149), channel_id=1, source_target_pairs={{0,8},{1,9},{2,10},{3,11},{4,12},{5,13},{6,14},{7,15},{8,0},{9,1},... | collective-permute-start | bytes 1277960 | tf_op jit(solution)/shard_map/ppermute | solution.py:804
  162.6 20.8 %collective-permute-start.32 = (bf16[1664,128]{1,0:T(8,128)(2,1)S(1)}, bf16[1664,128]{1,0:T(8,128)(2,1)S(1)}, u32[]{:S(2)}, u32[]{:S(2)}) collective-permute-start(bf16[1664,128]{1,0:T(8,128)(2,1)S(1)} %get-tuple-element.150), channel_id=1, source_target_pairs={{0,16},{1,17},{2,18},{3,19},{4,20},{5,21},{6,22},{7,23},{8,24},{9,... | collective-permute-start | bytes 1277960 | tf_op jit(solution)/shard_map/ppermute | solution.py:804
  163.3 20.1 %collective-permute-start.33 = (bf16[1664,128]{1,0:T(8,128)(2,1)S(1)}, bf16[1664,128]{1,0:T(8,128)(2,1)S(1)}, u32[]{:S(2)}, u32[]{:S(2)}) collective-permute-start(bf16[1664,128]{1,0:T(8,128)(2,1)S(1)} %get-tuple-element.151), channel_id=1, source_target_pairs={{0,24},{1,25},{2,26},{3,27},{4,28},{5,29},{6,30},{7,31},{8,16},{9,... | collective-permute-start | bytes 1277960 | tf_op jit(solution)/shard_map/ppermute | solution.py:804
  165.5 17.9 %collective-permute-start.35 = (bf16[832,128]{1,0:T(8,128)(2,1)S(1)}, bf16[832,128]{1,0:T(8,128)(2,1)S(1)}, u32[]{:S(2)}, u32[]{:S(2)}) collective-permute-start(bf16[832,128]{1,0:T(8,128)(2,1)S(1)} %get-tuple-element.154), channel_id=1, source_target_pairs={{0,4},{1,5},{2,6},{3,7},{4,0},{5,1},{6,2},{7,3},{8,12},{9,13},{10,... | collective-permute-start | bytes 638984 | tf_op jit(solution)/shard_map/ppermute | solution.py:804
  170.3 13.2 %collective-permute-start.36 = (bf16[832,128]{1,0:T(8,128)(2,1)S(1)}, bf16[832,128]{1,0:T(8,128)(2,1)S(1)}, u32[]{:S(2)}, u32[]{:S(2)}) collective-permute-start(bf16[832,128]{1,0:T(8,128)(2,1)S(1)} %get-tuple-element.155), channel_id=1, source_target_pairs={{0,6},{1,7},{2,4},{3,5},{4,2},{5,3},{6,0},{7,1},{8,14},{9,15},{10,... | collective-permute-start | bytes 638984 | tf_op jit(solution)/shard_map/ppermute | solution.py:804
  184.7 16.7 %collective-permute-start.38 = (bf16[864,128]{1,0:T(8,128)(2,1)S(1)}, bf16[864,128]{1,0:T(8,128)(2,1)S(1)}, u32[]{:S(2)}, u32[]{:S(2)}) collective-permute-start(bf16[864,128]{1,0:T(8,128)(2,1)S(1)} %get-tuple-element.165), channel_id=1, source_target_pairs={{0,2},{1,3},{2,0},{3,1},{4,6},{5,7},{6,4},{7,5},{8,10},{9,11},{10,... | collective-permute-start | bytes 663560 | tf_op jit(solution)/shard_map/ppermute | solution.py:804
  188.5 18.6 %collective-permute-start.39 = (bf16[864,128]{1,0:T(8,128)(2,1)S(1)}, bf16[864,128]{1,0:T(8,128)(2,1)S(1)}, u32[]{:S(2)}, u32[]{:S(2)}) collective-permute-start(bf16[864,128]{1,0:T(8,128)(2,1)S(1)} %get-tuple-element.166), channel_id=1, source_target_pairs={{0,4},{1,5},{2,6},{3,7},{4,0},{5,1},{6,2},{7,3},{8,12},{9,13},{10,... | collective-permute-start | bytes 663560 | tf_op jit(solution)/shard_map/ppermute | solution.py:804
  189.7 17.4 %collective-permute-start.40 = (bf16[864,128]{1,0:T(8,128)(2,1)S(1)}, bf16[864,128]{1,0:T(8,128)(2,1)S(1)}, u32[]{:S(2)}, u32[]{:S(2)}) collective-permute-start(bf16[864,128]{1,0:T(8,128)(2,1)S(1)} %get-tuple-element.167), channel_id=1, source_target_pairs={{0,6},{1,7},{2,4},{3,5},{4,2},{5,3},{6,0},{7,1},{8,14},{9,15},{10,... | collective-permute-start | bytes 663560 | tf_op jit(solution)/shard_map/ppermute | solution.py:804
  191.1 4.7 %collective-permute-start.41 = (bf16[416,128]{1,0:T(8,128)(2,1)S(1)}, bf16[416,128]{1,0:T(8,128)(2,1)S(1)}, u32[]{:S(2)}, u32[]{:S(2)}) collective-permute-start(bf16[416,128]{1,0:T(8,128)(2,1)S(1)} %get-tuple-element.169), channel_id=1, source_target_pairs={{0,8},{1,9},{2,10},{3,11},{4,12},{5,13},{6,14},{7,15},{8,0},{9,1},... | collective-permute-start | bytes 319496 | tf_op jit(solution)/shard_map/ppermute | solution.py:804
  191.7 4.8 %collective-permute-start.42 = (bf16[416,128]{1,0:T(8,128)(2,1)S(1)}, bf16[416,128]{1,0:T(8,128)(2,1)S(1)}, u32[]{:S(2)}, u32[]{:S(2)}) collective-permute-start(bf16[416,128]{1,0:T(8,128)(2,1)S(1)} %get-tuple-element.170), channel_id=1, source_target_pairs={{0,16},{1,17},{2,18},{3,19},{4,20},{5,21},{6,22},{7,23},{8,24},{9,... | collective-permute-start | bytes 319496 | tf_op jit(solution)/shard_map/ppermute | solution.py:804
  195.8 5.6 %collective-permute-start.43 = (bf16[416,128]{1,0:T(8,128)(2,1)S(1)}, bf16[416,128]{1,0:T(8,128)(2,1)S(1)}, u32[]{:S(2)}, u32[]{:S(2)}) collective-permute-start(bf16[416,128]{1,0:T(8,128)(2,1)S(1)} %get-tuple-element.171), channel_id=1, source_target_pairs={{0,24},{1,25},{2,26},{3,27},{4,28},{5,29},{6,30},{7,31},{8,16},{9,... | collective-permute-start | bytes 319496 | tf_op jit(solution)/shard_map/ppermute | solution.py:804
  209.2 4.5 %collective-permute-start.50 = (f32[8,128]{1,0:T(8,128)S(1)}, f32[8,128]{1,0:T(8,128)S(1)}, u32[]{:S(2)}, u32[]{:S(2)}) collective-permute-start(f32[8,128]{1,0:T(8,128)S(1)} %add.26), channel_id=1, source_target_pairs={{0,24},{1,25},{2,26},{3,27},{4,28},{5,29},{6,30},{7,31},{8,16},{9,... | collective-permute-start | bytes 12296 | tf_op jit(solution)/shard_map/ppermute | solution.py:804
  209.7 5.2 %collective-permute-start.49 = (f32[8,128]{1,0:T(8,128)S(1)}, f32[8,128]{1,0:T(8,128)S(1)}, u32[]{:S(2)}, u32[]{:S(2)}) collective-permute-start(f32[8,128]{1,0:T(8,128)S(1)} %add.26), channel_id=1, source_target_pairs={{0,16},{1,17},{2,18},{3,19},{4,20},{5,21},{6,22},{7,23},{8,24},{9,... | collective-permute-start | bytes 12296 | tf_op jit(solution)/shard_map/ppermute | solution.py:804
  212.7 11.2 %collective-permute-start.44 = (f32[304,128]{1,0:T(8,128)S(1)}, f32[304,128]{1,0:T(8,128)S(1)}, u32[]{:S(2)}, u32[]{:S(2)}) collective-permute-start(f32[304,128]{1,0:T(8,128)S(1)} %get-tuple-element.173), channel_id=1, source_target_pairs={{0,16},{1,17},{2,18},{3,19},{4,20},{5,21},{6,22},{7,23},{8,24},{9,... | collective-permute-start | bytes 466952 | tf_op jit(solution)/shard_map/ppermute | solution.py:804
  213.2 10.7 %collective-permute-start.45 = (f32[304,128]{1,0:T(8,128)S(1)}, f32[304,128]{1,0:T(8,128)S(1)}, u32[]{:S(2)}, u32[]{:S(2)}) collective-permute-start(f32[304,128]{1,0:T(8,128)S(1)} %get-tuple-element.174), channel_id=1, source_target_pairs={{0,1},{1,0},{2,3},{3,2},{4,5},{5,4},{6,7},{7,6},{8,9},{9,8},{10,11... | collective-permute-start | bytes 466952 | tf_op jit(solution)/shard_map/ppermute | solution.py:804
  213.7 10.3 %collective-permute-start.46 = (f32[304,128]{1,0:T(8,128)S(1)}, f32[304,128]{1,0:T(8,128)S(1)}, u32[]{:S(2)}, u32[]{:S(2)}) collective-permute-start(f32[304,128]{1,0:T(8,128)S(1)} %get-tuple-element.175), channel_id=1, source_target_pairs={{0,17},{1,16},{2,19},{3,18},{4,21},{5,20},{6,23},{7,22},{8,25},{9,... | collective-permute-start | bytes 466952 | tf_op jit(solution)/shard_map/ppermute | solution.py:804
  214.9 5.5 %collective-permute-start.53 = (f32[8,128]{1,0:T(8,128)S(1)}, f32[8,128]{1,0:T(8,128)S(1)}, u32[]{:S(2)}, u32[]{:S(2)}) collective-permute-start(f32[8,128]{1,0:T(8,128)S(1)} %add_add_fusion.q0), channel_id=1, source_target_pairs={{0,6},{1,7},{2,4},{3,5},{4,2},{5,3},{6,0},{7,1},{8,14},{9,15},{10,... | collective-permute-start | bytes 12296 | tf_op jit(solution)/shard_map/ppermute | solution.py:804
  216.9 4.6 %collective-permute-start.52 = (f32[8,128]{1,0:T(8,128)S(1)}, f32[8,128]{1,0:T(8,128)S(1)}, u32[]{:S(2)}, u32[]{:S(2)}) collective-permute-start(f32[8,128]{1,0:T(8,128)S(1)} %add_add_fusion.q0), channel_id=1, source_target_pairs={{0,4},{1,5},{2,6},{3,7},{4,0},{5,1},{6,2},{7,3},{8,12},{9,13},{10,... | collective-permute-start | bytes 12296 | tf_op jit(solution)/shard_map/ppermute | solution.py:804
  (28 other events, 633.4 us)

commit v4 on v3

--- a/solution.py
+++ b/solution.py
@@ -212,7 +212,7 @@
         qkv_ref[at, :] = nt(normed_ref[at, :], w_ref[ROW_QKV:ROW_O, :]).astype(BF16)
         return carry
 
-    lax.fori_loop(0, 2, short_step, 0)
+    lax.fori_loop(0, 2, short_step, 0, unroll=True)
     if pieces > 1:
         fetch.wait(False)
         leave = pltpu.make_async_copy(w_ref, w_out, part_sems.at[len(copies)])
@@ -402,7 +402,7 @@
         sums_ref[3, :, :] += fold_rows(dnormed)
         return carry
 
-    lax.fori_loop(0, 2, dnorm_step, 0)
+    lax.fori_loop(0, 2, dnorm_step, 0, unroll=True)
     for k in range(8):
         small_ref[k : k + 1, :] = jnp.sum(sums_ref[k], 0, keepdims=True)
 

time: 227 us -> 227 us (level)
  no operation moved by 1% of the time
where the time goes in v4:
time: 227 us; the launch traced here: 226 us
  waiting for transfers between devices  86.7 us (38%)
  Pallas kernels  74.7 us (33%)
  starting transfers between devices  59.9 us (26%)
    ppermute x54, waiting for transfers between devices, swap_with(): return lax.ppermute(array, AXES, pairs)  86.7 us
    ppermute x54, starting transfers between devices, swap_with(): return lax.ppermute(array, AXES, pairs)  59.9 us
    pallas_call x1, Pallas kernels, device_grads(): pl.pallas_call(partial(deep_kernel, count), out_shape=(shape((ROW_HALF -...  31 us
    pallas_call x1, Pallas kernels, device_grads(): pl.pallas_call(partial(back_kernel, short_len), out_shape=(shape((ROW_F1,...  19.7 us
    pallas_call x1, Pallas kernels, device_grads(): pl.pallas_call(partial(attend_kernel, short_len, slots, number), out_shap...  15.8 us
  transfers between devices with their start and end apart: 54, of which 23 were waited for; matrix products, arithmetic and copies ran while one was open for 0% of the time, Pallas kernels for 10%

profile of v4, /device:TPU:0, one launch (start us, length us, event | category | flops | bytes accessed | tf_op | source)
XLA Modules:
  0.0 226.3 jit_solution(10692102807980860909)
XLA Ops:
  1.4 1.1 convert_element_type.8
  2.6 4.1 %collective-permute-start = (bf16[241,512]{1,0:T(8,128)(2,1)S(1)}, bf16[241,512]{1,0:T(8,128)(2,1)S(1)}, u32[]{:S(2)}, u32[]{:S(2)}) collective-permute-start(bf16[241,512]{1,0:T(8,128)(2,1)S(1)} %pad_maximum_fusion.1), channel_id=1, source_target_pairs={{0,4},{1,5},{2,6},{3,7},{4,0},{5,1},{6,2},{7,3},{8,12},{9,13},{10,... | collective-permute-start | bytes 740360 | tf_op jit(solution)/shard_map/ppermute | solution.py:804
  6.7 2.5 %collective-permute-start.3 = (bf16[64,512]{1,0:T(8,128)(2,1)S(1)}, bf16[64,512]{1,0:T(8,128)(2,1)S(1)}, u32[]{:S(2)}, u32[]{:S(2)}) collective-permute-start(bf16[64,512]{1,0:T(8,128)(2,1)S(1)} %slice.19), channel_id=1, source_target_pairs={{0,24},{1,25},{2,26},{3,27},{4,28},{5,29},{6,30},{7,31},{8,16},{9,... | collective-permute-start | bytes 196616 | tf_op jit(solution)/shard_map/ppermute | solution.py:804
  10.3 1.8 collective-permute-done.3
  12.1 1.4 collective-permute-done.2
  14.0 4.3 %collective-permute-done = bf16[241,512]{1,0:T(8,128)(2,1)S(1)} collective-permute-done((bf16[241,512]{1,0:T(8,128)(2,1)S(1)}, bf16[241,512]{1,0:T(8,128)(2,1)S(1)}, u32[]{:S(2)}, u32[]{:S(2)}) %collective-permute-start) | collective-permute-done | bytes 246816 | tf_op jit(solution)/shard_map/ppermute | solution.py:804
  18.7 1.6 collective-permute-start.6
  20.3 1.5 collective-permute-start.5
  22.5 9.0 %collective-permute-done.6.refs_2_ = bf16[496,512]{1,0:T(8,128)(2,1)S(1)} collective-permute-done((bf16[496,512]{1,0:T(8,128)(2,1)S(1)}, bf16[496,512]{1,0:T(8,128)(2,1)S(1)}, u32[]{:S(2)}, u32[]{:S(2)}) %collective-permute-start.6) | collective-permute-done | bytes 507936 | tf_op jit(solution)/shard_map/ppermute | solution.py:804
  32.5 1.2 collective-permute-done.4.refs_4_
  35.0 3.1 %collective-permute-start.10 = (bf16[256,512]{1,0:T(8,128)(2,1)S(1)}, bf16[256,512]{1,0:T(8,128)(2,1)S(1)}, u32[]{:S(2)}, u32[]{:S(2)}) collective-permute-start(bf16[256,512]{1,0:T(8,128)(2,1)S(1)} %pad_maximum_fusion), channel_id=1, source_target_pairs={{0,4},{1,5},{2,6},{3,7},{4,0},{5,1},{6,2},{7,3},{8,12},{9,13},{10,... | collective-permute-start | bytes 786440 | tf_op jit(solution)/shard_map/ppermute | solution.py:804
  38.1 1.5 collective-permute-start.7
  39.6 8.8 %collective-permute-done.10 = bf16[256,512]{1,0:T(8,128)(2,1)S(1)} collective-permute-done((bf16[256,512]{1,0:T(8,128)(2,1)S(1)}, bf16[256,512]{1,0:T(8,128)(2,1)S(1)}, u32[]{:S(2)}, u32[]{:S(2)}) %collective-permute-start.10) | collective-permute-done | bytes 262176 | tf_op jit(solution)/shard_map/ppermute | solution.py:804
  48.6 1.6 collective-permute-start.12
  50.7 5.2 %collective-permute-done.7.refs_3_ = bf16[496,512]{1,0:T(8,128)(2,1)S(1)} collective-permute-done((bf16[496,512]{1,0:T(8,128)(2,1)S(1)}, bf16[496,512]{1,0:T(8,128)(2,1)S(1)}, u32[]{:S(2)}, u32[]{:S(2)}) %collective-permute-start.7) | collective-permute-done | bytes 507936 | tf_op jit(solution)/shard_map/ppermute | solution.py:804
  56.6 6.3 %collective-permute-done.12.refs_9_ = bf16[512,512]{1,0:T(8,128)(2,1)S(1)} collective-permute-done((bf16[512,512]{1,0:T(8,128)(2,1)S(1)}, bf16[512,512]{1,0:T(8,128)(2,1)S(1)}, u32[]{:S(2)}, u32[]{:S(2)}) %collective-permute-start.12) | collective-permute-done | bytes 524320 | tf_op jit(solution)/shard_map/ppermute | solution.py:804
  63.7 6.5 %collective-permute-done.11.refs_7_ = bf16[496,512]{1,0:T(8,128)(2,1)} collective-permute-done((bf16[496,512]{1,0:T(8,128)(2,1)}, bf16[496,512]{1,0:T(8,128)(2,1)}, u32[]{:S(2)}, u32[]{:S(2)}) %collective-permute-start.11) | collective-permute-done | bytes 507936 | tf_op jit(solution)/shard_map/ppermute | solution.py:804
  70.8 1.6 collective-permute-done.20.refs_17_
  73.2 15.8 %attend.1 = (bf16[9728,512]{1,0:T(8,128)(2,1)}, bf16[768,1536]{1,0:T(8,128)(2,1)S(1)}, f32[768,512]{1,0:T(8,128)S(1)}, bf16[768,512]{1,0:T(8,128)(2,1)S(1)}, bf1...) custom-call(s32[4]{0:T(128)S(1)} %pad_add_fusion.coords_ref, ...), custom_call_target="tpu_custom_call" | custom-call | flops 8999999488 | bytes 20000000 | tf_op jit(solution)/shard_map/attend/pallas_call | solution.py:669
  89.0 31.0 %deep.1 = (bf16[1024,256]{1,0:T(8,128)(2,1)S(1)}, bf16[1024,256]{1,0:T(8,128)(2,1)S(1)}, bf16[4864,256]{1,0:T(8,128)(2,1)S(1)}, bf16[4864,256]{1,0:T(8,128)(2,1)...) custom-call(s32[4]{0:T(128)S(1)} %pad_add_fusion.coords_ref, ...), custom_call_target="tpu_custom_call" | custom-call | tf_op jit(solution)/shard_map/deep/pallas_call | solution.py:687
  120.7 4.2 %collective-permute-done.23.recv_ref = bf16[4864,256]{1,0:T(8,128)(2,1)S(1)} collective-permute-done((bf16[4864,256]{1,0:T(8,128)(2,1)S(1)}, bf16[4864,256]{1,0:T(8,128)(2,1)S(1)}, u32[]{:S(2)}, u32[]{:S(2)}) %collective-permute-start.23) | collective-permute-done | bytes 2490400 | tf_op jit(solution)/shard_map/ppermute | solution.py:804
  124.9 1.4 core_sum.1
  126.3 4.5 %collective-permute-start.28 = (bf16[832,128]{1,0:T(8,128)(2,1)S(1)}, bf16[832,128]{1,0:T(8,128)(2,1)S(1)}, u32[]{:S(2)}, u32[]{:S(2)}) collective-permute-start(bf16[832,128]{1,0:T(8,128)(2,1)S(1)} %get-tuple-element.129), channel_id=1, source_target_pairs={{0,4},{1,5},{2,6},{3,7},{4,0},{5,1},{6,2},{7,3},{8,12},{9,13},{10,... | collective-permute-start | bytes 638984 | tf_op jit(solution)/shard_map/ppermute | solution.py:804
  133.1 2.2 collective-permute-start.27
  135.2 19.7 %back.1 = (bf16[3840,256]{1,0:T(8,128)(2,1)S(1)}, bf16[3872,256]{1,0:T(8,128)(2,1)S(1)}, f32[8,512]{1,0:T(8,128)S(1)}) custom-call(s32[4]{0:T(128)S(1)} %pad_add_fusion.coords_ref, s32[2]{0:T(128)S(1)} %bitcast.11, f32[8,512]{1,0:T(8,128)S(1)} %get-tuple-element.107.vec_ref, f32[8,512]{1,0:T(8,128)S(1)} %get-tuple-element.131.deep_small_ref, ...), custom_call_target="tpu_custom_call" | custom-call | flops 19000000512 | bytes 20000000 | tf_op jit(solution)/shard_map/back/pallas_call | solution.py:723
  155.6 3.4 %collective-permute-done.30.recv_front = bf16[3872,256]{1,0:T(8,128)(2,1)S(1)} collective-permute-done((bf16[3872,256]{1,0:T(8,128)(2,1)S(1)}, bf16[3872,256]{1,0:T(8,128)(2,1)S(1)}, u32[]{:S(2)}, u32[]{:S(2)}) %collective-permute-start.30) | collective-permute-done | bytes 1982496 | tf_op jit(solution)/shard_map/ppermute | solution.py:804
  159.1 2.2 core_sum_front.1
  163.1 2.2 collective-permute-start.33
  165.3 3.0 %collective-permute-start.35 = (bf16[832,128]{1,0:T(8,128)(2,1)S(1)}, bf16[832,128]{1,0:T(8,128)(2,1)S(1)}, u32[]{:S(2)}, u32[]{:S(2)}) collective-permute-start(bf16[832,128]{1,0:T(8,128)(2,1)S(1)} %get-tuple-element.154), channel_id=1, source_target_pairs={{0,4},{1,5},{2,6},{3,7},{4,0},{5,1},{6,2},{7,3},{8,12},{9,13},{10,... | collective-permute-start | bytes 638984 | tf_op jit(solution)/shard_map/ppermute | solution.py:804
  168.2 1.8 collective-permute-done.34.refs_5_
  170.0 2.5 %collective-permute-start.36 = (bf16[832,128]{1,0:T(8,128)(2,1)S(1)}, bf16[832,128]{1,0:T(8,128)(2,1)S(1)}, u32[]{:S(2)}, u32[]{:S(2)}) collective-permute-start(bf16[832,128]{1,0:T(8,128)(2,1)S(1)} %get-tuple-element.155), channel_id=1, source_target_pairs={{0,6},{1,7},{2,4},{3,5},{4,2},{5,3},{6,0},{7,1},{8,14},{9,15},{10,... | collective-permute-start | bytes 638984 | tf_op jit(solution)/shard_map/ppermute | solution.py:804
  172.5 10.7 %collective-permute-done.35.refs_6_ = bf16[832,128]{1,0:T(8,128)(2,1)S(1)} collective-permute-done((bf16[832,128]{1,0:T(8,128)(2,1)S(1)}, bf16[832,128]{1,0:T(8,128)(2,1)S(1)}, u32[]{:S(2)}, u32[]{:S(2)}) %collective-permute-start.35) | collective-permute-done | bytes 213024 | tf_op jit(solution)/shard_map/ppermute | solution.py:804
  183.3 1.2 first_sum.1
  184.5 3.8 %collective-permute-start.38 = (bf16[864,128]{1,0:T(8,128)(2,1)S(1)}, bf16[864,128]{1,0:T(8,128)(2,1)S(1)}, u32[]{:S(2)}, u32[]{:S(2)}) collective-permute-start(bf16[864,128]{1,0:T(8,128)(2,1)S(1)} %get-tuple-element.165), channel_id=1, source_target_pairs={{0,2},{1,3},{2,0},{3,1},{4,6},{5,7},{6,4},{7,5},{8,10},{9,11},{10,... | collective-permute-start | bytes 663560 | tf_op jit(solution)/shard_map/ppermute | solution.py:804
  188.3 1.2 collective-permute-start.39
  189.5 1.4 collective-permute-start.40
  192.2 3.4 %collective-permute-done.41.refs_5_ = bf16[416,128]{1,0:T(8,128)(2,1)S(1)} collective-permute-done((bf16[416,128]{1,0:T(8,128)(2,1)S(1)}, bf16[416,128]{1,0:T(8,128)(2,1)S(1)}, u32[]{:S(2)}, u32[]{:S(2)}) %collective-permute-start.41) | collective-permute-done | bytes 106528 | tf_op jit(solution)/shard_map/ppermute | solution.py:804
  196.3 4.8 %collective-permute-done.43.refs_7_ = bf16[416,128]{1,0:T(8,128)(2,1)S(1)} collective-permute-done((bf16[416,128]{1,0:T(8,128)(2,1)S(1)}, bf16[416,128]{1,0:T(8,128)(2,1)S(1)}, u32[]{:S(2)}, u32[]{:S(2)}) %collective-permute-start.43) | collective-permute-done | bytes 106528 | tf_op jit(solution)/shard_map/ppermute | solution.py:804
  201.2 5.7 %collective-permute-done.39.refs_2_ = bf16[864,128]{1,0:T(8,128)(2,1)S(1)} collective-permute-done((bf16[864,128]{1,0:T(8,128)(2,1)S(1)}, bf16[864,128]{1,0:T(8,128)(2,1)S(1)}, u32[]{:S(2)}, u32[]{:S(2)}) %collective-permute-start.39) | collective-permute-done | bytes 221216 | tf_op jit(solution)/shard_map/ppermute | solution.py:804
  207.8 1.2 collective-permute-done.47
  209.5 1.4 collective-permute-start.49
  210.9 1.6 collective-permute-start.48
  213.5 1.1 collective-permute-start.46
  214.6 2.0 collective-permute-start.53
  216.7 2.5 %collective-permute-start.52 = (f32[8,128]{1,0:T(8,128)S(1)}, f32[8,128]{1,0:T(8,128)S(1)}, u32[]{:S(2)}, u32[]{:S(2)}) collective-permute-start(f32[8,128]{1,0:T(8,128)S(1)} %add_add_fusion.q0), channel_id=1, source_target_pairs={{0,4},{1,5},{2,6},{3,7},{4,0},{5,1},{6,2},{7,3},{8,12},{9,13},{10,... | collective-permute-start | bytes 12296 | tf_op jit(solution)/shard_map/ppermute | solution.py:804
  220.1 1.2 collective-permute-start.51
  221.3 2.4 %collective-permute-done.51.q1 = f32[8,128]{1,0:T(8,128)S(1)} collective-permute-done((f32[8,128]{1,0:T(8,128)S(1)}, f32[8,128]{1,0:T(8,128)S(1)}, u32[]{:S(2)}, u32[]{:S(2)}) %collective-permute-start.51) | collective-permute-done | bytes 4128 | tf_op jit(solution)/shard_map/ppermute | solution.py:804
  223.8 2.5 %update.1 = (f32[1,1]{1,0:T(1,128)}, f32[1,1]{1,0:T(1,128)}, f32[304,512]{1,0:T(8,128)}, f32[304,512]{1,0:T(8,128)}, f32[304,512]{1,0:T(8,128)}, /*index=5*/f32[...) custom-call(s32[4]{0:T(128)S(1)} %pad_add_fusion.coords_ref, f32[304,128]{1,0:T(8,128)S(1)} %get-tuple-element.172.g0, ...), custom_call_target="tpu_custom_call" | custom-call | tf_op jit(solution)/shard_map/update/pallas_call | solution.py:883
  (133 shorter events, 20.0 us)
Async XLA Ops:
  2.6 15.7 %collective-permute-start = (bf16[241,512]{1,0:T(8,128)(2,1)S(1)}, bf16[241,512]{1,0:T(8,128)(2,1)S(1)}, u32[]{:S(2)}, u32[]{:S(2)}) collective-permute-start(bf16[241,512]{1,0:T(8,128)(2,1)S(1)} %pad_maximum_fusion.1), channel_id=1, source_target_pairs={{0,4},{1,5},{2,6},{3,7},{4,0},{5,1},{6,2},{7,3},{8,12},{9,13},{10,... | collective-permute-start | bytes 740360 | tf_op jit(solution)/shard_map/ppermute | solution.py:804
  6.7 5.3 %collective-permute-start.3 = (bf16[64,512]{1,0:T(8,128)(2,1)S(1)}, bf16[64,512]{1,0:T(8,128)(2,1)S(1)}, u32[]{:S(2)}, u32[]{:S(2)}) collective-permute-start(bf16[64,512]{1,0:T(8,128)(2,1)S(1)} %slice.19), channel_id=1, source_target_pairs={{0,24},{1,25},{2,26},{3,27},{4,28},{5,29},{6,30},{7,31},{8,16},{9,... | collective-permute-start | bytes 196616 | tf_op jit(solution)/shard_map/ppermute | solution.py:804
  9.2 4.3 %collective-permute-start.2 = (bf16[64,512]{1,0:T(8,128)(2,1)S(1)}, bf16[64,512]{1,0:T(8,128)(2,1)S(1)}, u32[]{:S(2)}, u32[]{:S(2)}) collective-permute-start(bf16[64,512]{1,0:T(8,128)(2,1)S(1)} %slice.19), channel_id=1, source_target_pairs={{0,16},{1,17},{2,18},{3,19},{4,20},{5,21},{6,22},{7,23},{8,24},{9,... | collective-permute-start | bytes 196616 | tf_op jit(solution)/shard_map/ppermute | solution.py:804
  18.7 12.8 %collective-permute-start.6 = (bf16[496,512]{1,0:T(8,128)(2,1)S(1)}, bf16[496,512]{1,0:T(8,128)(2,1)S(1)}, u32[]{:S(2)}, u32[]{:S(2)}) collective-permute-start(bf16[496,512]{1,0:T(8,128)(2,1)S(1)} %concatenate.13.refs_0_), channel_id=1, source_target_pairs={{0,16},{1,17},{2,18},{3,19},{4,20},{5,21},{6,22},{7,23},{8,24},{9,... | collective-permute-start | bytes 1523720 | tf_op jit(solution)/shard_map/ppermute | solution.py:804
  20.3 12.2 %collective-permute-start.5 = (bf16[496,512]{1,0:T(8,128)(2,1)S(1)}, bf16[496,512]{1,0:T(8,128)(2,1)S(1)}, u32[]{:S(2)}, u32[]{:S(2)}) collective-permute-start(bf16[496,512]{1,0:T(8,128)(2,1)S(1)} %concatenate.13.refs_0_), channel_id=1, source_target_pairs={{0,8},{1,9},{2,10},{3,11},{4,12},{5,13},{6,14},{7,15},{8,0},{9,1},... | collective-permute-start | bytes 1523720 | tf_op jit(solution)/shard_map/ppermute | solution.py:804
  21.8 11.9 %collective-permute-start.4 = (bf16[496,512]{1,0:T(8,128)(2,1)S(1)}, bf16[496,512]{1,0:T(8,128)(2,1)S(1)}, u32[]{:S(2)}, u32[]{:S(2)}) collective-permute-start(bf16[496,512]{1,0:T(8,128)(2,1)S(1)} %concatenate.13.refs_0_), channel_id=1, source_target_pairs={{0,2},{1,3},{2,0},{3,1},{4,6},{5,7},{6,4},{7,5},{8,10},{9,11},{10,... | collective-permute-start | bytes 1523720 | tf_op jit(solution)/shard_map/ppermute | solution.py:804
  33.7 14.8 %collective-permute-start.9 = (bf16[496,512]{1,0:T(8,128)(2,1)S(1)}, bf16[496,512]{1,0:T(8,128)(2,1)}, u32[]{:S(2)}, u32[]{:S(2)}) collective-permute-start(bf16[496,512]{1,0:T(8,128)(2,1)S(1)} %collective-permute-done.4.refs_4_), channel_id=1, source_target_pairs={{0,16},{1,17},{2,18},{3,19},{4,20},{5,21},{6,22},{7,23},{8,24},{9,... | collective-permute-start | bytes 1523720 | tf_op jit(solution)/shard_map/ppermute | solution.py:804
  34.2 14.3 %collective-permute-start.8 = (bf16[496,512]{1,0:T(8,128)(2,1)S(1)}, bf16[496,512]{1,0:T(8,128)(2,1)}, u32[]{:S(2)}, u32[]{:S(2)}) collective-permute-start(bf16[496,512]{1,0:T(8,128)(2,1)S(1)} %collective-permute-done.4.refs_4_), channel_id=1, source_target_pairs={{0,8},{1,9},{2,10},{3,11},{4,12},{5,13},{6,14},{7,15},{8,0},{9,1},... | collective-permute-start | bytes 1523720 | tf_op jit(solution)/shard_map/ppermute | solution.py:804
  35.0 13.5 %collective-permute-start.10 = (bf16[256,512]{1,0:T(8,128)(2,1)S(1)}, bf16[256,512]{1,0:T(8,128)(2,1)S(1)}, u32[]{:S(2)}, u32[]{:S(2)}) collective-permute-start(bf16[256,512]{1,0:T(8,128)(2,1)S(1)} %pad_maximum_fusion), channel_id=1, source_target_pairs={{0,4},{1,5},{2,6},{3,7},{4,0},{5,1},{6,2},{7,3},{8,12},{9,13},{10,... | collective-permute-start | bytes 786440 | tf_op jit(solution)/shard_map/ppermute | solution.py:804
  38.1 12.1 %collective-permute-start.13 = (bf16[496,512]{1,0:T(8,128)(2,1)S(1)}, bf16[496,512]{1,0:T(8,128)(2,1)S(1)}, u32[]{:S(2)}, u32[]{:S(2)}) collective-permute-start(bf16[496,512]{1,0:T(8,128)(2,1)S(1)} %concatenate.13.refs_0_), channel_id=1, source_target_pairs={{0,1},{1,0},{2,3},{3,2},{4,5},{5,4},{6,7},{7,6},{8,9},{9,8},{10,11... | collective-permute-start | bytes 1523720 | tf_op jit(solution)/shard_map/ppermute | solution.py:804
  38.1 17.7 %collective-permute-start.7 = (bf16[496,512]{1,0:T(8,128)(2,1)S(1)}, bf16[496,512]{1,0:T(8,128)(2,1)S(1)}, u32[]{:S(2)}, u32[]{:S(2)}) collective-permute-start(bf16[496,512]{1,0:T(8,128)(2,1)S(1)} %collective-permute-done.5.refs_1_), channel_id=1, source_target_pairs={{0,16},{1,17},{2,18},{3,19},{4,20},{5,21},{6,22},{7,23},{8,24},{9,... | collective-permute-start | bytes 1523720 | tf_op jit(solution)/shard_map/ppermute | solution.py:804
  48.5 7.4 %collective-permute-start.15 = (bf16[496,512]{1,0:T(8,128)(2,1)S(1)}, bf16[496,512]{1,0:T(8,128)(2,1)S(1)}, u32[]{:S(2)}, u32[]{:S(2)}) collective-permute-start(bf16[496,512]{1,0:T(8,128)(2,1)S(1)} %collective-permute-done.6.refs_2_), channel_id=1, source_target_pairs={{0,1},{1,0},{2,3},{3,2},{4,5},{5,4},{6,7},{7,6},{8,9},{9,8},{10,11... | collective-permute-start | bytes 1523720 | tf_op jit(solution)/shard_map/ppermute | solution.py:804
  48.6 14.4 %collective-permute-start.12 = (bf16[512,512]{1,0:T(8,128)(2,1)S(1)}, bf16[512,512]{1,0:T(8,128)(2,1)S(1)}, u32[]{:S(2)}, u32[]{:S(2)}) collective-permute-start(bf16[512,512]{1,0:T(8,128)(2,1)S(1)} %constant_dynamic-update-slice_fusion.refs_8_), channel_id=1, source_target_pairs={{0,2},{1,3},{2,0},{3,1},{4,6},{5,7},{6,4},{7,5},{8,10},{9,11},{10,... | collective-permute-start | bytes 1572872 | tf_op jit(solution)/shard_map/ppermute | solution.py:804
  50.2 6.3 %collective-permute-start.14 = (bf16[496,512]{1,0:T(8,128)(2,1)S(1)}, bf16[496,512]{1,0:T(8,128)(2,1)S(1)}, u32[]{:S(2)}, u32[]{:S(2)}) collective-permute-start(bf16[496,512]{1,0:T(8,128)(2,1)S(1)} %collective-permute-done.5.refs_1_), channel_id=1, source_target_pairs={{0,1},{1,0},{2,3},{3,2},{4,5},{5,4},{6,7},{7,6},{8,9},{9,8},{10,11... | collective-permute-start | bytes 1523720 | tf_op jit(solution)/shard_map/ppermute | solution.py:804
  50.2 12.8 %collective-permute-start.17 = (bf16[496,512]{1,0:T(8,128)(2,1)S(1)}, bf16[496,512]{1,0:T(8,128)(2,1)S(1)}, u32[]{:S(2)}, u32[]{:S(2)}) collective-permute-start(bf16[496,512]{1,0:T(8,128)(2,1)S(1)} %collective-permute-done.4.refs_4_), channel_id=1, source_target_pairs={{0,1},{1,0},{2,3},{3,2},{4,5},{5,4},{6,7},{7,6},{8,9},{9,8},{10,11... | collective-permute-start | bytes 1523720 | tf_op jit(solution)/shard_map/ppermute | solution.py:804
  55.8 7.7 %collective-permute-start.16 = (bf16[496,512]{1,0:T(8,128)(2,1)S(1)}, bf16[496,512]{1,0:T(8,128)(2,1)S(1)}, u32[]{:S(2)}, u32[]{:S(2)}) collective-permute-start(bf16[496,512]{1,0:T(8,128)(2,1)S(1)} %collective-permute-done.7.refs_3_), channel_id=1, source_target_pairs={{0,1},{1,0},{2,3},{3,2},{4,5},{5,4},{6,7},{7,6},{8,9},{9,8},{10,11... | collective-permute-start | bytes 1523720 | tf_op jit(solution)/shard_map/ppermute | solution.py:804
  55.9 14.3 %collective-permute-start.11 = (bf16[496,512]{1,0:T(8,128)(2,1)}, bf16[496,512]{1,0:T(8,128)(2,1)}, u32[]{:S(2)}, u32[]{:S(2)}) collective-permute-start(bf16[496,512]{1,0:T(8,128)(2,1)} %collective-permute-done.9.refs_6_), channel_id=1, source_target_pairs={{0,8},{1,9},{2,10},{3,11},{4,12},{5,13},{6,14},{7,15},{8,0},{9,1},... | collective-permute-start | bytes 1523720 | tf_op jit(solution)/shard_map/ppermute | solution.py:804
  56.5 14.3 %collective-permute-start.21 = (bf16[512,512]{1,0:T(8,128)(2,1)S(1)}, bf16[512,512]{1,0:T(8,128)(2,1)S(1)}, u32[]{:S(2)}, u32[]{:S(2)}) collective-permute-start(bf16[512,512]{1,0:T(8,128)(2,1)S(1)} %constant_dynamic-update-slice_fusion.refs_8_), channel_id=1, source_target_pairs={{0,1},{1,0},{2,3},{3,2},{4,5},{5,4},{6,7},{7,6},{8,9},{9,8},{10,11... | collective-permute-start | bytes 1572872 | tf_op jit(solution)/shard_map/ppermute | solution.py:804
  63.0 9.4 %collective-permute-start.22 = (bf16[512,512]{1,0:T(8,128)(2,1)S(1)}, bf16[512,512]{1,0:T(8,128)(2,1)S(1)}, u32[]{:S(2)}, u32[]{:S(2)}) collective-permute-start(bf16[512,512]{1,0:T(8,128)(2,1)S(1)} %collective-permute-done.12.refs_9_), channel_id=1, source_target_pairs={{0,1},{1,0},{2,3},{3,2},{4,5},{5,4},{6,7},{7,6},{8,9},{9,8},{10,11... | collective-permute-start | bytes 1572872 | tf_op jit(solution)/shard_map/ppermute | solution.py:804
  63.0 7.8 %collective-permute-start.18 = (bf16[496,512]{1,0:T(8,128)(2,1)}, bf16[496,512]{1,0:T(8,128)(2,1)}, u32[]{:S(2)}, u32[]{:S(2)}) collective-permute-start(bf16[496,512]{1,0:T(8,128)(2,1)} %collective-permute-done.8.refs_5_), channel_id=1, source_target_pairs={{0,1},{1,0},{2,3},{3,2},{4,5},{5,4},{6,7},{7,6},{8,9},{9,8},{10,11... | collective-permute-start | bytes 1523720 | tf_op jit(solution)/shard_map/ppermute | solution.py:804
  63.6 7.2 %collective-permute-start.19 = (bf16[496,512]{1,0:T(8,128)(2,1)}, bf16[496,512]{1,0:T(8,128)(2,1)}, u32[]{:S(2)}, u32[]{:S(2)}) collective-permute-start(bf16[496,512]{1,0:T(8,128)(2,1)} %collective-permute-done.9.refs_6_), channel_id=1, source_target_pairs={{0,1},{1,0},{2,3},{3,2},{4,5},{5,4},{6,7},{7,6},{8,9},{9,8},{10,11... | collective-permute-start | bytes 1523720 | tf_op jit(solution)/shard_map/ppermute | solution.py:804
  120.1 4.8 %collective-permute-start.23 = (bf16[4864,256]{1,0:T(8,128)(2,1)S(1)}, bf16[4864,256]{1,0:T(8,128)(2,1)S(1)}, u32[]{:S(2)}, u32[]{:S(2)}) collective-permute-start(bf16[4864,256]{1,0:T(8,128)(2,1)S(1)} %get-tuple-element.113), channel_id=1, source_target_pairs={{0,1},{1,0},{2,3},{3,2},{4,5},{5,4},{6,7},{7,6},{8,9},{9,8},{10,11... | collective-permute-start | bytes 7471112 | tf_op jit(solution)/shard_map/ppermute | solution.py:804
  120.3 6.0 %collective-permute-start.24 = (bf16[1024,256]{1,0:T(8,128)(2,1)S(1)}, bf16[1024,256]{1,0:T(8,128)(2,1)S(1)}, u32[]{:S(2)}, u32[]{:S(2)}) collective-permute-start(bf16[1024,256]{1,0:T(8,128)(2,1)S(1)} %get-tuple-element.122), channel_id=1, source_target_pairs={{0,1},{1,0},{2,3},{3,2},{4,5},{5,4},{6,7},{7,6},{8,9},{9,8},{10,11... | collective-permute-start | bytes 1572872 | tf_op jit(solution)/shard_map/ppermute | solution.py:804
  126.3 28.6 %collective-permute-start.28 = (bf16[832,128]{1,0:T(8,128)(2,1)S(1)}, bf16[832,128]{1,0:T(8,128)(2,1)S(1)}, u32[]{:S(2)}, u32[]{:S(2)}) collective-permute-start(bf16[832,128]{1,0:T(8,128)(2,1)S(1)} %get-tuple-element.129), channel_id=1, source_target_pairs={{0,4},{1,5},{2,6},{3,7},{4,0},{5,1},{6,2},{7,3},{8,12},{9,13},{10,... | collective-permute-start | bytes 638984 | tf_op jit(solution)/shard_map/ppermute | solution.py:804
  130.8 24.1 %collective-permute-start.29 = (bf16[832,128]{1,0:T(8,128)(2,1)S(1)}, bf16[832,128]{1,0:T(8,128)(2,1)S(1)}, u32[]{:S(2)}, u32[]{:S(2)}) collective-permute-start(bf16[832,128]{1,0:T(8,128)(2,1)S(1)} %get-tuple-element.130), channel_id=1, source_target_pairs={{0,6},{1,7},{2,4},{3,5},{4,2},{5,3},{6,0},{7,1},{8,14},{9,15},{10,... | collective-permute-start | bytes 638984 | tf_op jit(solution)/shard_map/ppermute | solution.py:804
  131.7 23.2 %collective-permute-start.25 = (bf16[1600,128]{1,0:T(8,128)(2,1)S(1)}, bf16[1600,128]{1,0:T(8,128)(2,1)S(1)}, u32[]{:S(2)}, u32[]{:S(2)}) collective-permute-start(bf16[1600,128]{1,0:T(8,128)(2,1)S(1)} %get-tuple-element.125), channel_id=1, source_target_pairs={{0,8},{1,9},{2,10},{3,11},{4,12},{5,13},{6,14},{7,15},{8,0},{9,1},... | collective-permute-start | bytes 1228808 | tf_op jit(solution)/shard_map/ppermute | solution.py:804
  132.4 22.6 %collective-permute-start.26 = (bf16[1600,128]{1,0:T(8,128)(2,1)S(1)}, bf16[1600,128]{1,0:T(8,128)(2,1)S(1)}, u32[]{:S(2)}, u32[]{:S(2)}) collective-permute-start(bf16[1600,128]{1,0:T(8,128)(2,1)S(1)} %get-tuple-element.126), channel_id=1, source_target_pairs={{0,16},{1,17},{2,18},{3,19},{4,20},{5,21},{6,22},{7,23},{8,24},{9,... | collective-permute-start | bytes 1228808 | tf_op jit(solution)/shard_map/ppermute | solution.py:804
  133.1 21.9 %collective-permute-start.27 = (bf16[1600,128]{1,0:T(8,128)(2,1)S(1)}, bf16[1600,128]{1,0:T(8,128)(2,1)S(1)}, u32[]{:S(2)}, u32[]{:S(2)}) collective-permute-start(bf16[1600,128]{1,0:T(8,128)(2,1)S(1)} %get-tuple-element.127), channel_id=1, source_target_pairs={{0,24},{1,25},{2,26},{3,27},{4,28},{5,29},{6,30},{7,31},{8,16},{9,... | collective-permute-start | bytes 1228808 | tf_op jit(solution)/shard_map/ppermute | solution.py:804
  155.1 10.2 %collective-permute-start.37 = (bf16[832,128]{1,0:T(8,128)(2,1)S(1)}, bf16[832,128]{1,0:T(8,128)(2,1)S(1)}, u32[]{:S(2)}, u32[]{:S(2)}) collective-permute-start(bf16[832,128]{1,0:T(8,128)(2,1)S(1)} %get-tuple-element.161), channel_id=1, source_target_pairs={{0,2},{1,3},{2,0},{3,1},{4,6},{5,7},{6,4},{7,5},{8,10},{9,11},{10,... | collective-permute-start | bytes 638984 | tf_op jit(solution)/shard_map/ppermute | solution.py:804
  161.2 8.8 %collective-permute-start.34 = (bf16[832,128]{1,0:T(8,128)(2,1)S(1)}, bf16[832,128]{1,0:T(8,128)(2,1)S(1)}, u32[]{:S(2)}, u32[]{:S(2)}) collective-permute-start(bf16[832,128]{1,0:T(8,128)(2,1)S(1)} %get-tuple-element.153), channel_id=1, source_target_pairs={{0,2},{1,3},{2,0},{3,1},{4,6},{5,7},{6,4},{7,5},{8,10},{9,11},{10,... | collective-permute-start | bytes 638984 | tf_op jit(solution)/shard_map/ppermute | solution.py:804
  161.8 21.5 %collective-permute-start.31 = (bf16[1664,128]{1,0:T(8,128)(2,1)S(1)}, bf16[1664,128]{1,0:T(8,128)(2,1)S(1)}, u32[]{:S(2)}, u32[]{:S(2)}) collective-permute-start(bf16[1664,128]{1,0:T(8,128)(2,1)S(1)} %get-tuple-element.149), channel_id=1, source_target_pairs={{0,8},{1,9},{2,10},{3,11},{4,12},{5,13},{6,14},{7,15},{8,0},{9,1},... | collective-permute-start | bytes 1277960 | tf_op jit(solution)/shard_map/ppermute | solution.py:804
  162.4 20.8 %collective-permute-start.32 = (bf16[1664,128]{1,0:T(8,128)(2,1)S(1)}, bf16[1664,128]{1,0:T(8,128)(2,1)S(1)}, u32[]{:S(2)}, u32[]{:S(2)}) collective-permute-start(bf16[1664,128]{1,0:T(8,128)(2,1)S(1)} %get-tuple-element.150), channel_id=1, source_target_pairs={{0,16},{1,17},{2,18},{3,19},{4,20},{5,21},{6,22},{7,23},{8,24},{9,... | collective-permute-start | bytes 1277960 | tf_op jit(solution)/shard_map/ppermute | solution.py:804
  163.1 20.1 %collective-permute-start.33 = (bf16[1664,128]{1,0:T(8,128)(2,1)S(1)}, bf16[1664,128]{1,0:T(8,128)(2,1)S(1)}, u32[]{:S(2)}, u32[]{:S(2)}) collective-permute-start(bf16[1664,128]{1,0:T(8,128)(2,1)S(1)} %get-tuple-element.151), channel_id=1, source_target_pairs={{0,24},{1,25},{2,26},{3,27},{4,28},{5,29},{6,30},{7,31},{8,16},{9,... | collective-permute-start | bytes 1277960 | tf_op jit(solution)/shard_map/ppermute | solution.py:804
  165.3 18.0 %collective-permute-start.35 = (bf16[832,128]{1,0:T(8,128)(2,1)S(1)}, bf16[832,128]{1,0:T(8,128)(2,1)S(1)}, u32[]{:S(2)}, u32[]{:S(2)}) collective-permute-start(bf16[832,128]{1,0:T(8,128)(2,1)S(1)} %get-tuple-element.154), channel_id=1, source_target_pairs={{0,4},{1,5},{2,6},{3,7},{4,0},{5,1},{6,2},{7,3},{8,12},{9,13},{10,... | collective-permute-start | bytes 638984 | tf_op jit(solution)/shard_map/ppermute | solution.py:804
  170.0 13.2 %collective-permute-start.36 = (bf16[832,128]{1,0:T(8,128)(2,1)S(1)}, bf16[832,128]{1,0:T(8,128)(2,1)S(1)}, u32[]{:S(2)}, u32[]{:S(2)}) collective-permute-start(bf16[832,128]{1,0:T(8,128)(2,1)S(1)} %get-tuple-element.155), channel_id=1, source_target_pairs={{0,6},{1,7},{2,4},{3,5},{4,2},{5,3},{6,0},{7,1},{8,14},{9,15},{10,... | collective-permute-start | bytes 638984 | tf_op jit(solution)/shard_map/ppermute | solution.py:804
  184.5 16.7 %collective-permute-start.38 = (bf16[864,128]{1,0:T(8,128)(2,1)S(1)}, bf16[864,128]{1,0:T(8,128)(2,1)S(1)}, u32[]{:S(2)}, u32[]{:S(2)}) collective-permute-start(bf16[864,128]{1,0:T(8,128)(2,1)S(1)} %get-tuple-element.165), channel_id=1, source_target_pairs={{0,2},{1,3},{2,0},{3,1},{4,6},{5,7},{6,4},{7,5},{8,10},{9,11},{10,... | collective-permute-start | bytes 663560 | tf_op jit(solution)/shard_map/ppermute | solution.py:804
  188.3 18.6 %collective-permute-start.39 = (bf16[864,128]{1,0:T(8,128)(2,1)S(1)}, bf16[864,128]{1,0:T(8,128)(2,1)S(1)}, u32[]{:S(2)}, u32[]{:S(2)}) collective-permute-start(bf16[864,128]{1,0:T(8,128)(2,1)S(1)} %get-tuple-element.166), channel_id=1, source_target_pairs={{0,4},{1,5},{2,6},{3,7},{4,0},{5,1},{6,2},{7,3},{8,12},{9,13},{10,... | collective-permute-start | bytes 663560 | tf_op jit(solution)/shard_map/ppermute | solution.py:804
  189.5 17.4 %collective-permute-start.40 = (bf16[864,128]{1,0:T(8,128)(2,1)S(1)}, bf16[864,128]{1,0:T(8,128)(2,1)S(1)}, u32[]{:S(2)}, u32[]{:S(2)}) collective-permute-start(bf16[864,128]{1,0:T(8,128)(2,1)S(1)} %get-tuple-element.167), channel_id=1, source_target_pairs={{0,6},{1,7},{2,4},{3,5},{4,2},{5,3},{6,0},{7,1},{8,14},{9,15},{10,... | collective-permute-start | bytes 663560 | tf_op jit(solution)/shard_map/ppermute | solution.py:804
  190.9 4.7 %collective-permute-start.41 = (bf16[416,128]{1,0:T(8,128)(2,1)S(1)}, bf16[416,128]{1,0:T(8,128)(2,1)S(1)}, u32[]{:S(2)}, u32[]{:S(2)}) collective-permute-start(bf16[416,128]{1,0:T(8,128)(2,1)S(1)} %get-tuple-element.169), channel_id=1, source_target_pairs={{0,8},{1,9},{2,10},{3,11},{4,12},{5,13},{6,14},{7,15},{8,0},{9,1},... | collective-permute-start | bytes 319496 | tf_op jit(solution)/shard_map/ppermute | solution.py:804
  191.5 4.8 %collective-permute-start.42 = (bf16[416,128]{1,0:T(8,128)(2,1)S(1)}, bf16[416,128]{1,0:T(8,128)(2,1)S(1)}, u32[]{:S(2)}, u32[]{:S(2)}) collective-permute-start(bf16[416,128]{1,0:T(8,128)(2,1)S(1)} %get-tuple-element.170), channel_id=1, source_target_pairs={{0,16},{1,17},{2,18},{3,19},{4,20},{5,21},{6,22},{7,23},{8,24},{9,... | collective-permute-start | bytes 319496 | tf_op jit(solution)/shard_map/ppermute | solution.py:804
  195.6 5.6 %collective-permute-start.43 = (bf16[416,128]{1,0:T(8,128)(2,1)S(1)}, bf16[416,128]{1,0:T(8,128)(2,1)S(1)}, u32[]{:S(2)}, u32[]{:S(2)}) collective-permute-start(bf16[416,128]{1,0:T(8,128)(2,1)S(1)} %get-tuple-element.171), channel_id=1, source_target_pairs={{0,24},{1,25},{2,26},{3,27},{4,28},{5,29},{6,30},{7,31},{8,16},{9,... | collective-permute-start | bytes 319496 | tf_op jit(solution)/shard_map/ppermute | solution.py:804
  209.0 4.5 %collective-permute-start.50 = (f32[8,128]{1,0:T(8,128)S(1)}, f32[8,128]{1,0:T(8,128)S(1)}, u32[]{:S(2)}, u32[]{:S(2)}) collective-permute-start(f32[8,128]{1,0:T(8,128)S(1)} %add.26), channel_id=1, source_target_pairs={{0,24},{1,25},{2,26},{3,27},{4,28},{5,29},{6,30},{7,31},{8,16},{9,... | collective-permute-start | bytes 12296 | tf_op jit(solution)/shard_map/ppermute | solution.py:804
  209.5 5.2 %collective-permute-start.49 = (f32[8,128]{1,0:T(8,128)S(1)}, f32[8,128]{1,0:T(8,128)S(1)}, u32[]{:S(2)}, u32[]{:S(2)}) collective-permute-start(f32[8,128]{1,0:T(8,128)S(1)} %add.26), channel_id=1, source_target_pairs={{0,16},{1,17},{2,18},{3,19},{4,20},{5,21},{6,22},{7,23},{8,24},{9,... | collective-permute-start | bytes 12296 | tf_op jit(solution)/shard_map/ppermute | solution.py:804
  212.5 11.2 %collective-permute-start.44 = (f32[304,128]{1,0:T(8,128)S(1)}, f32[304,128]{1,0:T(8,128)S(1)}, u32[]{:S(2)}, u32[]{:S(2)}) collective-permute-start(f32[304,128]{1,0:T(8,128)S(1)} %get-tuple-element.173), channel_id=1, source_target_pairs={{0,16},{1,17},{2,18},{3,19},{4,20},{5,21},{6,22},{7,23},{8,24},{9,... | collective-permute-start | bytes 466952 | tf_op jit(solution)/shard_map/ppermute | solution.py:804
  213.0 10.7 %collective-permute-start.45 = (f32[304,128]{1,0:T(8,128)S(1)}, f32[304,128]{1,0:T(8,128)S(1)}, u32[]{:S(2)}, u32[]{:S(2)}) collective-permute-start(f32[304,128]{1,0:T(8,128)S(1)} %get-tuple-element.174), channel_id=1, source_target_pairs={{0,1},{1,0},{2,3},{3,2},{4,5},{5,4},{6,7},{7,6},{8,9},{9,8},{10,11... | collective-permute-start | bytes 466952 | tf_op jit(solution)/shard_map/ppermute | solution.py:804
  213.5 10.2 %collective-permute-start.46 = (f32[304,128]{1,0:T(8,128)S(1)}, f32[304,128]{1,0:T(8,128)S(1)}, u32[]{:S(2)}, u32[]{:S(2)}) collective-permute-start(f32[304,128]{1,0:T(8,128)S(1)} %get-tuple-element.175), channel_id=1, source_target_pairs={{0,17},{1,16},{2,19},{3,18},{4,21},{5,20},{6,23},{7,22},{8,25},{9,... | collective-permute-start | bytes 466952 | tf_op jit(solution)/shard_map/ppermute | solution.py:804
  214.6 5.5 %collective-permute-start.53 = (f32[8,128]{1,0:T(8,128)S(1)}, f32[8,128]{1,0:T(8,128)S(1)}, u32[]{:S(2)}, u32[]{:S(2)}) collective-permute-start(f32[8,128]{1,0:T(8,128)S(1)} %add_add_fusion.q0), channel_id=1, source_target_pairs={{0,6},{1,7},{2,4},{3,5},{4,2},{5,3},{6,0},{7,1},{8,14},{9,15},{10,... | collective-permute-start | bytes 12296 | tf_op jit(solution)/shard_map/ppermute | solution.py:804
  216.7 4.6 %collective-permute-start.52 = (f32[8,128]{1,0:T(8,128)S(1)}, f32[8,128]{1,0:T(8,128)S(1)}, u32[]{:S(2)}, u32[]{:S(2)}) collective-permute-start(f32[8,128]{1,0:T(8,128)S(1)} %add_add_fusion.q0), channel_id=1, source_target_pairs={{0,4},{1,5},{2,6},{3,7},{4,0},{5,1},{6,2},{7,3},{8,12},{9,13},{10,... | collective-permute-start | bytes 12296 | tf_op jit(solution)/shard_map/ppermute | solution.py:804
  (28 other events, 633.3 us)
